TPU v7x, 32 devices: a whole 2x2x4 slice. The times are simulated.
32 devices in a mesh: lat: 16 (over z, y, x), dp: 2 (over core).
Axes of the slice: x: 2, y: 2, z: 4, core: 2. Of those that a mesh axis runs over, the one named last changes fastest.
Arguments:
- inputs: bfloat16 [1024, 4096], P('dp', 'lat'), may hold values from -6 to 6
- dec_bias: bfloat16 [4096], P('lat'), may hold values from -3 to 3
- enc_weight: bfloat16 [4096, 4096], P(None, 'lat'), may hold values from -0.09375 to 0.09375
- enc_bias: float32 [4096], P('lat'), may hold values from -3 to 3
- dec_weight: bfloat16 [4096, 4096], P('lat'), may hold values from -0.09375 to 0.09375
- other_recon: float32 [1024, 4096], P('dp', 'lat'), may hold values from -6 to 6
- active_blocks: int32 [1024, 32], P('dp', 'lat'), may hold values 0 or 1
Outputs:
- error_full: float32 [1024, 4096], P('dp', 'lat')
- mse_loss: float32 [], replicated
- grad_dec: float32 [4096, 4096], P(('lat', 'dp'))
- grad_enc: float32 [4096, 4096], P(None, ('lat', 'dp'))
All inputs are finite; a program needn't handle non-finite values. No bound on the sum of `active_blocks` on one device may be relied on, other than what follows from the above.
Results may differ from a plain program's by a relative error of at most 0.0033.
Values may be sent and summed in bfloat16 or wider, within the bound.
No kernel may reach another device: no remote copies, remote signals or barrier semaphores. Data moves between devices by JAX's collectives and lax.ppermute only.
A program may use at most 128 MiB of HBM per device.

v0:
```python
import jax
import jax.numpy as jnp
from jax import lax
from jax.sharding import PartitionSpec as P


def local(inputs, dec_bias, enc_weight, enc_bias, dec_weight, other_recon, active_blocks):
    row_count = inputs.shape[0]
    col_count = inputs.shape[1]
    block_size = enc_weight.shape[1] // active_blocks.shape[1]
    full_inputs, full_bias = (
        lax.all_gather(inputs, "lat", axis=1, tiled=True),
        lax.all_gather(dec_bias.reshape(1, -1), "lat", axis=1, tiled=True),
    )
    inputs_float = full_inputs.astype(jnp.float32)
    centered = (inputs_float - full_bias.astype(jnp.float32)).astype(jnp.bfloat16)
    pre_act = jnp.dot(centered, enc_weight, preferred_element_type=jnp.float32) + enc_bias[None, :]
    block_gate = (
        active_blocks.astype(jnp.float32)[:, :, None] * jnp.ones((1, 1, block_size), jnp.float32)
    ).reshape(row_count, -1)
    positive = jnp.maximum(pre_act, 0.0)
    activations = (positive * positive * block_gate).astype(jnp.bfloat16)
    outside = other_recon + dec_bias.astype(jnp.float32)[None, :]
    summed = lax.psum_scatter(
        lax.dot_general(
            dec_weight, activations, (((0,), (1,)), ((), ())), preferred_element_type=jnp.float32
        ),
        "lat",
        scatter_dimension=0,
        tiled=True,
    )
    error_local = summed.T + outside - inputs.astype(jnp.float32)
    error_bf = lax.all_gather(error_local.astype(jnp.bfloat16), "lat", axis=1, tiled=True)
    squares = lax.psum(jnp.sum(error_local * error_local), ("lat", "dp"))
    mse_loss = squares / (row_count * lax.axis_size("dp") * col_count * lax.axis_size("lat"))
    grad_dec = lax.psum_scatter(
        lax.dot_general(
            activations, error_bf, (((0,), (0,)), ((), ())), preferred_element_type=jnp.float32
        ),
        "dp",
        scatter_dimension=0,
        tiled=True,
    )
    dact = lax.dot_general(
        error_bf, dec_weight, (((1,), (1,)), ((), ())), preferred_element_type=jnp.float32
    )
    dpre = (dact * 2.0 * positive * block_gate).astype(jnp.bfloat16)
    enc_term = lax.dot_general(
        centered, dpre, (((0,), (0,)), ((), ())), preferred_element_type=jnp.float32
    )
    grad_enc = lax.psum_scatter(enc_term, "dp", scatter_dimension=1, tiled=True)
    return (error_local, mse_loss, grad_dec, grad_enc)


def solution(mesh):
    placed = (
        P("dp", "lat"),
        P("lat"),
        P(None, "lat"),
        P("lat"),
        P("lat", None),
        P("dp", "lat"),
        P("dp", "lat"),
    )
    return jax.shard_map(
        local,
        mesh=mesh,
        in_specs=placed,
        out_specs=(P("dp", "lat"), P(), P(("lat", "dp"), None), P(None, ("lat", "dp"))),
        check_vma=False,
    )
```

profile of v0, /device:TPU:0, one launch (start us, length us, event | category | flops | bytes accessed | tf_op | source)
XLA Modules:
  0.0 442.8 jit_solution(15962213694085128784)
XLA Ops:
  7.2 0.0 copy-start
  7.2 0.0 all-gather.5.cloned.1.call-start
  7.2 0.7 all-gather.5.cloned.1.call-update
  7.9 0.0 reduce-scatter.4.cloned.1.call-start
  8.0 0.7 convert_element_type.27
  8.7 0.1 copy.12
  8.8 0.7 reshape.23
  9.5 42.4 %all-gather.1 = bf16[16,1,256]{2,1,0:T(2,128)(2,1)S(1)} all-gather(bf16[1,1,256]{2,1,0:T(2,128)(2,1)S(1)} %reshape.23), channel_id=2, replica_groups=mesh['lat'=16,'dp'=2] {'lat'}, dimensions={0}, use_global_device_ids=true | all-gather | bytes 8704 | tf_op jit(solution)/shard_map/all_gather | solution.py:13
  51.9 48.7 %all-gather.5.cloned.1.call-done = bf16[512,4096]{1,0:T(8,128)(2,1)} async-done(((bf16[512,256]{1,0:T(8,128)(2,1)}), bf16[512,4096]{1,0:T(8,128)(2,1)}) %all-gather.5.cloned.1.call-update) | async-done | bytes 4194320 | tf_op jit(solution)/shard_map/all_gather | solution.py:12
  100.6 0.6 mul.27
  101.2 0.0 copy-start.3
  101.2 5.1 %fusion.8 = (bf16[512,256]{1,0:T(8,128)(2,1)S(1)}, f32[512,256]{1,0:T(8,128)}) fusion(f32[64,8,2,128]{3,2,1,0:T(2,128)S(1)} %bitcast.24, f32[256]{0:T(256)} %param.10, bf16[4096,256]{1,0:T(8,128)(2,1)} %param.9, bf16[512,4096]{1,0:T(8,128)(2,1)} %all-gather.5.cloned.1.call-done, f32[4096]{0:T(1024)S(1)} %bitcast.26), kind=kOutput, calls=%fused_computation.12 | convolution fusion | flops 1080688640 | bytes 7619584 | tf_op jit(solution)/shard_map/dot_general | solution.py:17
  106.3 0.0 copy-done.3
  106.3 0.0 copy-done
  106.3 4.5 %convolution_bitcast_fusion = f32[4096,512]{0,1:T(8,128)} fusion(bf16[512,256]{1,0:T(8,128)(2,1)S(1)} %get-tuple-element.6, bf16[256,4096]{1,0:T(8,128)(2,1)S(1)} %copy-done), kind=kOutput, calls=%fused_computation.1 | convolution fusion | flops 1073741824 | bytes 10747904 | tf_op jit(solution)/shard_map/dot_general | solution.py:25
  110.8 0.0 copy-start.4
  110.8 0.0 copy-start.2
  110.8 0.0 reduce-scatter.4.cloned.1.call-update
  110.8 0.0 all-gather.7.cloned.1.call-start
  110.9 0.6 copy-done.4
  111.5 175.6 %reduce-scatter.4.cloned.1.call-done = f32[256,512]{0,1:T(8,128)} async-done(((f32[4096,512]{0,1:T(8,128)}), f32[256,512]{0,1:T(8,128)}) %reduce-scatter.4.cloned.1.call-update) | async-done | bytes 524304 | tf_op jit(solution)/shard_map/reduce_scatter | solution.py:24
  287.0 0.0 copy-done.2
  287.1 2.0 fusion.13
  289.0 0.0 copy-start.1
  289.0 0.0 all-gather.7.cloned.1.call-update
  289.1 0.0 reduce-scatter.8.cloned.1.call-start
  289.1 90.2 %all-gather.7.cloned.1.call-done = bf16[512,4096]{1,0:T(8,128)(2,1)} async-done(((bf16[512,256]{1,0:T(8,128)(2,1)}), bf16[512,4096]{1,0:T(8,128)(2,1)}) %all-gather.7.cloned.1.call-update) | async-done | bytes 4194320 | tf_op jit(solution)/shard_map/all_gather | solution.py:33
  379.3 10.2 %fusion = f32[4096,256]{1,0:T(8,128)} fusion(bf16[512,4096]{1,0:T(8,128)(2,1)} %all-gather.5.cloned.1.call-done, f32[4096]{0:T(1024)S(1)} %bitcast.27, f32[512,256]{1,0:T(8,128)} %get-tuple-element.7, bf16[512,4096]{1,0:T(8,128)(2,1)} %all-gather.7.cloned.1.call-done, bf16[256,4096]{1,0:T(8,128)(2,1)S(1)} %copy-done, f32[64,8,2,128]{3,2,1,0:T(2,128)} %bitcast.25), kind=kOutput, calls=%fused_computation.2 | convolution fusion | flops 2154299392 | bytes 15745024 | tf_op jit(solution)/shard_map/dot_general | solution.py:48
  389.5 0.0 reduce-scatter.8.cloned.1.call-update
  389.6 0.0 reduce-scatter.6.cloned.1.call-start
  389.6 5.4 %fusion.15 = f32[256,4096]{1,0:T(8,128)} fusion(bf16[512,256]{1,0:T(8,128)(2,1)S(1)} %get-tuple-element.6, bf16[512,4096]{1,0:T(8,128)(2,1)} %all-gather.7.cloned.1.call-done), kind=kOutput, calls=%fused_computation.20 | convolution fusion | flops 1073741824 | bytes 8650752 | tf_op jit(solution)/shard_map/dot_general | solution.py:37
  395.1 0.0 reduce-scatter.6.cloned.1.call-update
  395.1 0.0 copy-done.1
  395.1 0.7 multiply_reduce_fusion
  395.8 38.6 %psum.7 = f32[]{:T(128)} all-reduce(f32[]{:T(128)} %multiply_reduce_fusion), channel_id=1, replica_groups=mesh['lat'=16,'dp'=2] {'lat','dp'}, use_global_device_ids=true, to_apply=%region_2.0 | all-reduce | flops 1 | bytes 8 | tf_op jit(solution)/shard_map/psum | solution.py:34
  435.1 0.0 reduce-scatter.8.cloned.1.call-done
  435.2 0.0 reduce-scatter.6.cloned.1.call-done
  (2 shorter events, 0.0 us)
Async XLA Ops:
  7.2 99.1 %copy-start = (bf16[256,4096]{1,0:T(8,128)(2,1)S(1)}, bf16[256,4096]{1,0:T(8,128)(2,1)}, u32[]{:S(2)}) copy-start(bf16[256,4096]{1,0:T(8,128)(2,1)} %param.11) | copy-start | bytes 6291460
  7.2 93.4 %all-gather.5.cloned.1.call-start = ((), (), s32[]{:S(2)}) async-start(), calls=%async_computation.3 | async-start | bytes 4456448 | tf_op jit(solution)/shard_map/all_gather | solution.py:12
  7.9 279.1 %reduce-scatter.4.cloned.1.call-start = ((), (), s32[]{:S(2)}) async-start(), calls=%async_computation.4 | async-start | bytes 8912896 | tf_op jit(solution)/shard_map/reduce_scatter | solution.py:24
  101.2 5.1 %copy-start.3 = (f32[512,2,128]{2,1,0:T(2,128)}, f32[512,2,128]{2,1,0:T(2,128)S(1)}, u32[]{:S(2)}) copy-start(f32[512,2,128]{2,1,0:T(2,128)S(1)} %mul.27) | copy-start | bytes 1572868
  110.8 0.7 copy-start.4
  110.8 176.3 %copy-start.2 = (bf16[512,256]{1,0:T(8,128)(2,1)S(1)}, bf16[512,256]{1,0:T(8,128)(2,1)}, u32[]{:S(2)}) copy-start(bf16[512,256]{1,0:T(8,128)(2,1)} %param.7) | copy-start | bytes 786436
  110.8 268.5 %all-gather.7.cloned.1.call-start = ((), (), s32[]{:S(2)}) async-start(), calls=%async_computation.5 | async-start | bytes 4456448 | tf_op jit(solution)/shard_map/all_gather | solution.py:33
  289.0 106.0 %copy-start.1 = (f32[512,256]{1,0:T(8,128)}, f32[512,256]{1,0:T(8,128)S(1)}, u32[]{:S(2)}) copy-start(f32[512,256]{1,0:T(8,128)S(1)} %get-tuple-element.5) | copy-start | bytes 1572868
  289.1 146.1 %reduce-scatter.8.cloned.1.call-start = ((), (), s32[]{:S(2)}) async-start(), calls=%async_computation.7 | async-start | bytes 6291456 | tf_op jit(solution)/shard_map/reduce_scatter | solution.py:51
  389.6 45.6 %reduce-scatter.6.cloned.1.call-start = ((), (), s32[]{:S(2)}) async-start(), calls=%async_computation.6 | async-start | bytes 6291456 | tf_op jit(solution)/shard_map/reduce_scatter | solution.py:36
Sparse Core Ops, SparseCore 0:
  10.7 89.8 all-gather.4
  110.9 176.0 reduce-scatter.3
  289.8 89.5 all-gather.6
  389.7 10.2 reduce-scatter.7
  402.8 13.3 reduce-scatter.5
where the time goes:
time: 444 us; the launch traced here: 443 us
  waiting for transfers between devices  315 us (71%)
  blocking collectives  81.1 us (18%)
  matrix products  25.2 us (6%)
  between operations  15.6 us (4%)
    reduce_scatter x1, waiting for transfers between devices, local(): lax.psum_scatter(lax.dot_general(dec_weight, activations, (((0,), (1,)),...  176 us
    all_gather x1, waiting for transfers between devices, local(): lax.all_gather(error_local.astype(jnp.bfloat16), 'lat', axis=1, tiled=True)  90.2 us
    all_gather x1, waiting for transfers between devices, local(): lax.all_gather(inputs, 'lat', axis=1, tiled=True)  48.7 us
    all_gather x1, blocking collectives, local(): lax.all_gather(dec_bias.reshape(1, -1), 'lat', axis=1, tiled=True)  42.4 us
    psum x1, blocking collectives, local(): squares = lax.psum(jnp.sum(error_local * error_local), ('lat', 'dp'))  38.6 us
    dot_general x1, matrix products, local(): lax.dot_general(centered, dpre, (((0,), (0,)), ((), ())), preferred_eleme...  10.2 us
  transfers between devices with their start and end apart: 5, of which 3 were waited for; matrix products, arithmetic and copies ran while one was open for 2% of the time, Pallas kernels for 0%

commit v1 on v0

v1 whole, which is shorter than its diff:
```python
import jax
import jax.numpy as jnp
from jax import lax
from jax.sharding import PartitionSpec as P


def _slot_table(planes):
    table = []
    for z in range(planes):
        near = [(d, s) for d in range(1, planes) for s in (1, -1) if 0 <= z + s * d < planes]
        table.append(near)
    return table


class Grid:
    def __init__(self, lat, dp):
        self.lat, self.dp, self.planes = lat, dp, lat // 4
        self.table = _slot_table(self.planes)
        self.me = lax.axis_index("lat")
        self.rank = lax.axis_index("dp")
        self.z = self.me // 4
        self.square = self.me % 4
        self.first = jnp.where(self.rank % 2 == 0, 1, 2)

    def send(self, x, pairs_of):
        pairs = []
        for i in range(self.lat):
            for d in range(self.dp):
                to = pairs_of(i, d)
                if to is not None:
                    pairs.append((i * self.dp + d, to * self.dp + d))
        return lax.ppermute(x, ("lat", "dp"), pairs)

    def swap_first(self, x):
        return self.send(x, lambda i, d: i ^ (1 if d % 2 == 0 else 2))

    def swap_second(self, x):
        return self.send(x, lambda i, d: i ^ (2 if d % 2 == 0 else 1))

    def shift(self, x, sign, sources):
        return self.send(x, lambda i, d: i + 4 * sign if i // 4 in sources else None)

    def pick(self, choices):
        kinds = []
        for c in choices:
            if c is not None and not any(c is k for k in kinds):
                kinds.append(c)
        out = kinds[0]
        for k in kinds[1:]:
            mine = [c is k for c in choices]
            out = jnp.where(jnp.array(mine)[self.z], k, out)
        return out

    def index(self, slot, member):
        if slot == 0:
            plane = self.z
        else:
            plane = jnp.array([z + s * d for z, (d, s) in enumerate(row[slot - 1] for row in self.table)])[self.z]
        change = (0, self.first, 3 - self.first, 3)[member]
        return 4 * plane + (self.square ^ change)

    def gather(self, own):
        planes = self.planes
        slots = [own]
        arrived = {}
        up, down = own, own
        for d in range(1, planes):
            up = self.shift(up, 1, range(d - 1, planes - 1))
            down = self.shift(down, -1, range(1, planes - d + 1))
            arrived[(d, -1)], arrived[(d, 1)] = up, down
        for k in range(planes - 1):
            slots.append(self.pick([arrived[self.table[z][k]] for z in range(planes)]))
        out = []
        for block in slots:
            a = self.swap_first(block)
            b = self.swap_second(block)
            c = self.swap_second(a)
            out.append((block, a, b, c))
        return out

    def scatter_sum(self, part):
        planes = self.planes
        column = [None] * planes
        for k in reversed(range(planes)):
            there = self.swap_second(
                jnp.stack([part(k, 2).astype(jnp.bfloat16), part(k, 3).astype(jnp.bfloat16)])
            )
            mine = part(k, 0) + there[0].astype(jnp.float32)
            other = part(k, 1) + there[1].astype(jnp.float32)
            column[k] = mine + self.swap_first(other.astype(jnp.bfloat16)).astype(jnp.float32)
        total = column[0]
        for sign in (1, -1):
            moving = None
            for d in reversed(range(1, planes)):
                sources = [z for z in range(planes) if 0 <= z + sign * d < planes]
                send = self.pick(
                    [column[1 + self.table[z].index((d, sign))] if z in sources else None for z in range(planes)]
                )
                if moving is not None:
                    send = send + moving
                moving = self.shift(send, sign, sources)
            total = total + moving
        return total

    def total(self, x):
        step = 1
        while step < self.dp:
            pairs = [(d, d ^ step) for d in range(self.dp)]
            x = x + lax.ppermute(x, "dp", pairs)
            step *= 2
        step = 1
        while step < self.lat:
            pairs = [(i, i ^ step) for i in range(self.lat)]
            x = x + lax.ppermute(x, "lat", pairs)
            step *= 2
        return x


def local(lat, dp, inputs, dec_bias, enc_weight, enc_bias, dec_weight, other_recon, active_blocks):
    grid = Grid(lat, dp)
    rows, width = inputs.shape
    lats = enc_weight.shape[1]
    block_size = lats // active_blocks.shape[1]
    f32, bf16 = jnp.float32, jnp.bfloat16
    bias = dec_bias.astype(f32)[None, :]
    x = inputs.astype(f32)
    centered_own = (x - bias).astype(bf16)
    centered = grid.gather(centered_own)
    planes = grid.planes

    pre_act = enc_bias[None, :]
    for k in range(planes):
        for m in range(4):
            w = lax.dynamic_slice(enc_weight, (grid.index(k, m) * width, 0), (width, lats))
            pre_act = pre_act + jnp.dot(centered[k][m], w, preferred_element_type=f32)
    gate = jnp.repeat(active_blocks.astype(f32), block_size, axis=1)
    positive = jnp.maximum(pre_act, 0.0)
    activations = (positive * positive * gate).astype(bf16)
    slope = positive * 2.0 * gate

    def dec_columns(k, m):
        return lax.dynamic_slice(dec_weight, (0, grid.index(k, m) * width), (lats, width))

    def part(k, m):
        return jnp.dot(activations, dec_columns(k, m), preferred_element_type=f32)

    recon = grid.scatter_sum(part)
    error_local = recon + (other_recon + bias) - x
    error = grid.gather(error_local.astype(bf16))
    squares = grid.total(jnp.broadcast_to(jnp.sum(error_local * error_local), (8, 128)))
    mse_loss = squares[0, 0] / (rows * dp * width * lat)

    dact = jnp.zeros((rows, lats), f32)
    grad_dec = jnp.zeros((lats, width * lat), f32)
    for k in range(planes):
        for m in range(4):
            e = error[k][m]
            g = lax.dot_general(activations, e, (((0,), (0,)), ((), ())), preferred_element_type=f32)
            grad_dec = lax.dynamic_update_slice(grad_dec, g, (0, grid.index(k, m) * width))
            dact = dact + lax.dot_general(
                e, dec_columns(k, m), (((1,), (1,)), ((), ())), preferred_element_type=f32
            )
    dpre = (dact * slope).astype(bf16)
    grad_enc = jnp.zeros((width * lat, lats), f32)
    for k in range(planes):
        for m in range(4):
            g = lax.dot_general(centered[k][m], dpre, (((0,), (0,)), ((), ())), preferred_element_type=f32)
            grad_enc = lax.dynamic_update_slice(grad_enc, g, (grid.index(k, m) * width, 0))
    grad_dec = lax.psum_scatter(grad_dec, "dp", scatter_dimension=0, tiled=True)
    grad_enc = lax.psum_scatter(grad_enc, "dp", scatter_dimension=1, tiled=True)
    return (error_local, mse_loss, grad_dec, grad_enc)


def solution(mesh):
    placed = (
        P("dp", "lat"),
        P("lat"),
        P(None, "lat"),
        P("lat"),
        P("lat", None),
        P("dp", "lat"),
        P("dp", "lat"),
    )
    lat, dp = mesh.shape["lat"], mesh.shape["dp"]

    def body(*args):
        return local(lat, dp, *args)

    return jax.shard_map(
        body,
        mesh=mesh,
        in_specs=placed,
        out_specs=(P("dp", "lat"), P(), P(("lat", "dp"), None), P(None, ("lat", "dp"))),
        check_vma=False,
    )
```

time: 444 us -> 283 us (0.64)
  waiting for transfers between devices: 315 us -> 109 us
  blocking collectives: 81.1 us -> 0 us
  starting transfers between devices: 0.2 us -> 76 us
  matrix products: 25.2 us -> 47.2 us
  local copies, waits for them, and re-layouts: 2.01 us -> 16.7 us
  other arithmetic: 3.44 us -> 14.2 us
    reduce_scatter x3 -> x2, waiting for transfers between devices: 176 us -> 0.04 us  [the longest x1 0.02 us: local(): grad_enc = lax.psum_scatter(grad_enc, 'dp', scatter_dimension=1, tiled=True)]
    all_gather x2 -> x0, waiting for transfers between devices: 139 us -> none  [the longest x1 90.2 us: local(): lax.all_gather(error_local.astype(jnp.bfloat16), 'lat', axis=1, tiled=True)]
    ppermute x0 -> x55, waiting for transfers between devices: none -> 109 us  [the longest x50 93.7 us: send(): return lax.ppermute(x, ('lat', 'dp'), pairs)]
    ppermute x0 -> x55, starting transfers between devices: none -> 75.9 us  [the longest x50 74.2 us: send(): return lax.ppermute(x, ('lat', 'dp'), pairs)]
    all_gather x1 -> x0, blocking collectives: 42.4 us -> none  [local(): lax.all_gather(dec_bias.reshape(1, -1), 'lat', axis=1, tiled=True)]
    psum x1 -> x0, blocking collectives: 38.6 us -> none  [local(): squares = lax.psum(jnp.sum(error_local * error_local), ('lat', 'dp'))]
    dot_general x4 -> x80, matrix products: 25.2 us -> 47.2 us  [the longest x16 16.6 us: local(): lax.dot_general(centered[k][m], dpre, (((0,), (0,)), ((), ())), preferred...]
    dynamic_slice x0 -> x7, local copies, waits for them, and re-layouts: none -> 8.69 us  [the longest x4 4.96 us: pick(): out = jnp.where(jnp.array(mine)[self.z], k, out)]
  transfers between devices with their start and end apart: 5 -> 57, of which waited for: 3 -> 29; matrix products, arithmetic and copies ran while one was open for 2% -> 19% of each run, Pallas kernels for 0% -> 0%
where the time goes in v1:
time: 283 us; the launch traced here: 282 us
  waiting for transfers between devices  109 us (39%)
  starting transfers between devices  76 us (27%)
  matrix products  47.2 us (17%)
  between operations  19 us (7%)
  local copies, waits for them, and re-layouts  16.7 us (6%)
  other arithmetic  14.2 us (5%)
    ppermute x50, waiting for transfers between devices, send(): return lax.ppermute(x, ('lat', 'dp'), pairs)  93.7 us
    ppermute x50, starting transfers between devices, send(): return lax.ppermute(x, ('lat', 'dp'), pairs)  74.2 us
    dot_general x16, matrix products, local(): lax.dot_general(centered[k][m], dpre, (((0,), (0,)), ((), ())), preferred...  16.6 us
    dot_general x16, matrix products, local(): lax.dot_general(activations, e, (((0,), (0,)), ((), ())), preferred_eleme...  16.1 us
    ppermute x4, waiting for transfers between devices, total(): x = x + lax.ppermute(x, 'lat', pairs)  13.7 us
    dot_general x16, matrix products, local(): pre_act = pre_act + jnp.dot(centered[k][m], w, preferred_element_type=f32)  6.52 us
    select_n x2, other arithmetic, pick(): out = jnp.where(jnp.array(mine)[self.z], k, out)  6.17 us
  transfers between devices with their start and end apart: 57, of which 29 were waited for; matrix products, arithmetic and copies ran while one was open for 19% of the time, Pallas kernels for 0%

profile of v1, /device:TPU:0, one launch (start us, length us, event | category | flops | bytes accessed | tf_op | source)
XLA Modules:
  0.0 281.9 jit_solution(7777177026898209239)
XLA Ops:
  9.0 5.6 %collective-permute-start.3 = (bf16[512,256]{1,0:T(8,128)(2,1)S(1)}, bf16[512,256]{1,0:T(8,128)(2,1)}, u32[]{:S(2)}, u32[]{:S(2)}) collective-permute-start(bf16[512,256]{1,0:T(8,128)(2,1)S(1)} %fusion.28), channel_id=1, source_target_pairs={{0,8},{1,9},{2,10},{3,11},{4,12},{5,13},{6,14},{7,15},{8,16},{9,17... | collective-permute-start | bytes 786440 | tf_op jit(solution)/shard_map/ppermute | solution.py:32
  16.0 1.6 collective-permute-start
  20.9 3.6 %collective-permute-done.4 = bf16[512,256]{1,0:T(8,128)(2,1)} collective-permute-done((bf16[512,256]{1,0:T(8,128)(2,1)S(1)}, bf16[512,256]{1,0:T(8,128)(2,1)}, u32[]{:S(2)}, u32[]{:S(2)}) %collective-permute-start.4) | collective-permute-done | bytes 262176 | tf_op jit(solution)/shard_map/ppermute | solution.py:32
  38.6 1.6 collective-permute-start.2
  44.7 6.3 %collective-permute-done.14 = bf16[512,256]{1,0:T(8,128)(2,1)S(1)} collective-permute-done((bf16[512,256]{1,0:T(8,128)(2,1)}, bf16[512,256]{1,0:T(8,128)(2,1)S(1)}, u32[]{:S(2)}, u32[]{:S(2)}) %collective-permute-start.14) | collective-permute-done | bytes 262176 | tf_op jit(solution)/shard_map/ppermute | solution.py:32
  51.1 3.7 %select_select_fusion.3 = (bf16[512,256]{1,0:T(8,128)(2,1)S(1)}, bf16[512,256]{1,0:T(8,128)(2,1)S(1)}, bf16[512,256]{1,0:T(8,128)(2,1)S(1)}) fusion(bf16[512,256]{1,0:T(8,128)(2,1)} %collective-permute-done.8, bf16[512,256]{1,0:T(8,128)(2,1)} %collective-permute-done.3, bf16[512,256]{1,0:T(8,128)(2,1)} %collective-permute-done.9, pred[]{:T(512)} %bitcast.2, ...), kind=kLoop, calls=%fused_computation.126 | loop fusion | flops 786432 | bytes 2359300 | tf_op jit(solution)/shard_map/jit(_where)/select_n | solution.py:51
  54.7 1.6 collective-permute-start.6
  59.3 4.7 %collective-permute-done.6 = bf16[512,256]{1,0:T(8,128)(2,1)S(1)} collective-permute-done((bf16[512,256]{1,0:T(8,128)(2,1)S(1)}, bf16[512,256]{1,0:T(8,128)(2,1)S(1)}, u32[]{:S(2)}, u32[]{:S(2)}) %collective-permute-start.6) | collective-permute-done | bytes 262176 | tf_op jit(solution)/shard_map/ppermute | solution.py:32
  69.3 2.4 collective-permute-start.12
  71.7 3.2 %collective-permute-done.15 = bf16[512,256]{1,0:T(8,128)(2,1)S(1)} collective-permute-done((bf16[512,256]{1,0:T(8,128)(2,1)S(1)}, bf16[512,256]{1,0:T(8,128)(2,1)S(1)}, u32[]{:S(2)}, u32[]{:S(2)}) %collective-permute-start.15) | collective-permute-done | bytes 262176 | tf_op jit(solution)/shard_map/ppermute | solution.py:32
  74.9 2.4 collective-permute-start.17
  79.3 2.4 collective-permute-done.17
  83.3 2.1 collective-permute-start.22
  86.5 6.0 %collective-permute-done.22 = bf16[2,512,256]{2,1,0:T(8,128)(2,1)S(1)} collective-permute-done((bf16[2,512,256]{2,1,0:T(8,128)(2,1)S(1)}, bf16[2,512,256]{2,1,0:T(8,128)(2,1)S(1)}, u32[]{:S(2)}, u32[]{:S(2)}) %collective-permute-start.22) | collective-permute-done | bytes 524320 | tf_op jit(solution)/shard_map/ppermute | solution.py:32
  94.5 4.8 %collective-permute-done.23 = bf16[512,256]{1,0:T(8,128)(2,1)S(1)} collective-permute-done((bf16[512,256]{1,0:T(8,128)(2,1)S(1)}, bf16[512,256]{1,0:T(8,128)(2,1)S(1)}, u32[]{:S(2)}, u32[]{:S(2)}) %collective-permute-start.23) | collective-permute-done | bytes 262176 | tf_op jit(solution)/shard_map/ppermute | solution.py:32
  99.3 1.6 collective-permute-start.26
  103.2 1.8 collective-permute-start.20
  105.2 5.0 %collective-permute-done.25 = bf16[512,256]{1,0:T(8,128)(2,1)S(1)} collective-permute-done((bf16[512,256]{1,0:T(8,128)(2,1)S(1)}, bf16[512,256]{1,0:T(8,128)(2,1)S(1)}, u32[]{:S(2)}, u32[]{:S(2)}) %collective-permute-start.25) | collective-permute-done | bytes 262176 | tf_op jit(solution)/shard_map/ppermute | solution.py:32
  110.2 2.8 collective-permute-done.26
  114.3 4.4 %collective-permute-start.27 = (f32[512,256]{1,0:T(8,128)S(1)}, f32[512,256]{1,0:T(8,128)S(1)}, u32[]{:S(2)}, u32[]{:S(2)}) collective-permute-start(f32[512,256]{1,0:T(8,128)S(1)} %get-tuple-element.6), channel_id=1, source_target_pairs={{0,8},{1,9},{2,10},{3,11},{4,12},{5,13},{6,14},{7,15},{8,16},{9,17... | collective-permute-start | bytes 1572872 | tf_op jit(solution)/shard_map/ppermute | solution.py:32
  120.2 1.7 collective-permute-start.18
  122.1 6.8 %collective-permute-done.21 = bf16[512,256]{1,0:T(8,128)(2,1)S(1)} collective-permute-done((bf16[512,256]{1,0:T(8,128)(2,1)S(1)}, bf16[512,256]{1,0:T(8,128)(2,1)S(1)}, u32[]{:S(2)}, u32[]{:S(2)}) %collective-permute-start.21) | collective-permute-done | bytes 262176 | tf_op jit(solution)/shard_map/ppermute | solution.py:32
  130.7 8.2 %collective-permute-start.28 = (f32[512,256]{1,0:T(8,128)S(1)}, f32[512,256]{1,0:T(8,128)S(1)}, u32[]{:S(2)}, u32[]{:S(2)}) collective-permute-start(f32[512,256]{1,0:T(8,128)S(1)} %get-tuple-element.8), channel_id=1, source_target_pairs={{0,8},{1,9},{2,10},{3,11},{4,12},{5,13},{6,14},{7,15},{8,16},{9,17... | collective-permute-start | bytes 1572872 | tf_op jit(solution)/shard_map/ppermute | solution.py:32
  140.7 6.1 %collective-permute-done.19 = bf16[512,256]{1,0:T(8,128)(2,1)S(1)} collective-permute-done((bf16[512,256]{1,0:T(8,128)(2,1)S(1)}, bf16[512,256]{1,0:T(8,128)(2,1)S(1)}, u32[]{:S(2)}, u32[]{:S(2)}) %collective-permute-start.19) | collective-permute-done | bytes 262176 | tf_op jit(solution)/shard_map/ppermute | solution.py:32
  146.9 1.8 collective-permute-done.28
  148.7 4.1 %collective-permute-done.31 = f32[512,256]{1,0:T(8,128)S(1)} collective-permute-done((f32[512,256]{1,0:T(8,128)S(1)}, f32[512,256]{1,0:T(8,128)S(1)}, u32[]{:S(2)}, u32[]{:S(2)}) %collective-permute-start.31) | collective-permute-done | bytes 524320 | tf_op jit(solution)/shard_map/ppermute | solution.py:32
  153.9 2.2 collective-permute-start.40
  157.4 2.5 collective-permute-done.40
  160.6 3.7 %collective-permute-done.41 = bf16[512,256]{1,0:T(8,128)(2,1)S(1)} collective-permute-done((bf16[512,256]{1,0:T(8,128)(2,1)S(1)}, bf16[512,256]{1,0:T(8,128)(2,1)S(1)}, u32[]{:S(2)}, u32[]{:S(2)}) %collective-permute-start.41) | collective-permute-done | bytes 262176 | tf_op jit(solution)/shard_map/ppermute | solution.py:32
  167.8 5.2 %collective-permute-done.46 = bf16[512,256]{1,0:T(8,128)(2,1)S(1)} collective-permute-done((bf16[512,256]{1,0:T(8,128)(2,1)S(1)}, bf16[512,256]{1,0:T(8,128)(2,1)S(1)}, u32[]{:S(2)}, u32[]{:S(2)}) %collective-permute-start.46) | collective-permute-done | bytes 262176 | tf_op jit(solution)/shard_map/ppermute | solution.py:32
  174.7 1.5 collective-permute-start.39
  176.6 4.7 %collective-permute-done.51 = bf16[512,256]{1,0:T(8,128)(2,1)S(1)} collective-permute-done((bf16[512,256]{1,0:T(8,128)(2,1)S(1)}, bf16[512,256]{1,0:T(8,128)(2,1)S(1)}, u32[]{:S(2)}, u32[]{:S(2)}) %collective-permute-start.51) | collective-permute-done | bytes 262176 | tf_op jit(solution)/shard_map/ppermute | solution.py:32
  181.3 2.5 select_select_fusion
  186.2 2.0 collective-permute-start.47
  188.5 3.9 %collective-permute-done.43 = bf16[512,256]{1,0:T(8,128)(2,1)S(1)} collective-permute-done((bf16[512,256]{1,0:T(8,128)(2,1)S(1)}, bf16[512,256]{1,0:T(8,128)(2,1)S(1)}, u32[]{:S(2)}, u32[]{:S(2)}) %collective-permute-start.43) | collective-permute-done | bytes 262176 | tf_op jit(solution)/shard_map/ppermute | solution.py:32
  193.1 1.6 collective-permute-start.53
  195.0 6.6 %collective-permute-done.52 = bf16[512,256]{1,0:T(8,128)(2,1)S(1)} collective-permute-done((bf16[512,256]{1,0:T(8,128)(2,1)S(1)}, bf16[512,256]{1,0:T(8,128)(2,1)S(1)}, u32[]{:S(2)}, u32[]{:S(2)}) %collective-permute-start.52) | collective-permute-done | bytes 262176 | tf_op jit(solution)/shard_map/ppermute | solution.py:32
  201.6 1.5 collective-permute-start.44
  204.0 1.5 collective-permute-start.49
  208.3 5.3 %collective-permute-done.49 = bf16[512,256]{1,0:T(8,128)(2,1)S(1)} collective-permute-done((bf16[512,256]{1,0:T(8,128)(2,1)S(1)}, bf16[512,256]{1,0:T(8,128)(2,1)S(1)}, u32[]{:S(2)}, u32[]{:S(2)}) %collective-permute-start.49) | collective-permute-done | bytes 262176 | tf_op jit(solution)/shard_map/ppermute | solution.py:32
  214.5 2.3 broadcast_in_dim.17
  218.8 1.9 convolution_dynamic-update-slice_fusion.13
  233.5 2.5 broadcast_in_dim.16
  256.6 3.6 %collective-permute-done.33 = f32[8,128]{1,0:T(8,128)S(1)} collective-permute-done((f32[8,128]{1,0:T(8,128)S(1)}, f32[8,128]{1,0:T(8,128)S(1)}, u32[]{:S(2)}, u32[]{:S(2)}) %collective-permute-start.33) | collective-permute-done | bytes 4128 | tf_op jit(solution)/shard_map/ppermute | solution.py:114
  260.9 1.6 collective-permute-start.34
  262.5 2.0 collective-permute-done.34
  264.5 3.6 %collective-permute-done.35 = f32[8,128]{1,0:T(8,128)S(1)} collective-permute-done((f32[8,128]{1,0:T(8,128)S(1)}, f32[8,128]{1,0:T(8,128)S(1)}, u32[]{:S(2)}, u32[]{:S(2)}) %collective-permute-start.35) | collective-permute-done | bytes 4128 | tf_op jit(solution)/shard_map/ppermute | solution.py:114
  268.2 4.5 %collective-permute-done.36 = f32[8,128]{1,0:T(8,128)S(1)} collective-permute-done((f32[8,128]{1,0:T(8,128)S(1)}, f32[8,128]{1,0:T(8,128)S(1)}, u32[]{:S(2)}, u32[]{:S(2)}) %collective-permute-start.36) | collective-permute-done | bytes 4128 | tf_op jit(solution)/shard_map/ppermute | solution.py:114
  (246 shorter events, 99.7 us)
Async XLA Ops:
  7.2 266.7 %reduce-scatter.5.cloned.1.call-start = ((), (), s32[]{:S(2)}) async-start(), calls=%async_computation.3 | async-start | bytes 6291456 | tf_op jit(solution)/shard_map/reduce_scatter | solution.py:170
  9.0 10.5 %collective-permute-start.3 = (bf16[512,256]{1,0:T(8,128)(2,1)S(1)}, bf16[512,256]{1,0:T(8,128)(2,1)}, u32[]{:S(2)}, u32[]{:S(2)}) collective-permute-start(bf16[512,256]{1,0:T(8,128)(2,1)S(1)} %fusion.28), channel_id=1, source_target_pairs={{0,8},{1,9},{2,10},{3,11},{4,12},{5,13},{6,14},{7,15},{8,16},{9,17... | collective-permute-start | bytes 786440 | tf_op jit(solution)/shard_map/ppermute | solution.py:32
  14.7 9.8 %collective-permute-start.4 = (bf16[512,256]{1,0:T(8,128)(2,1)S(1)}, bf16[512,256]{1,0:T(8,128)(2,1)}, u32[]{:S(2)}, u32[]{:S(2)}) collective-permute-start(bf16[512,256]{1,0:T(8,128)(2,1)S(1)} %fusion.28), channel_id=1, source_target_pairs={{8,0},{9,1},{10,2},{11,3},{12,4},{13,5},{14,6},{15,7},{16,8},{17,9... | collective-permute-start | bytes 786440 | tf_op jit(solution)/shard_map/ppermute | solution.py:32
  16.0 22.6 %collective-permute-start = (bf16[512,256]{1,0:T(8,128)(2,1)S(1)}, bf16[512,256]{1,0:T(8,128)(2,1)S(1)}, u32[]{:S(2)}, u32[]{:S(2)}) collective-permute-start(bf16[512,256]{1,0:T(8,128)(2,1)S(1)} %fusion.28), channel_id=1, source_target_pairs={{0,2},{1,5},{2,0},{3,7},{4,6},{5,1},{6,4},{7,3},{8,10},{9,13},{10,... | collective-permute-start | bytes 786440 | tf_op jit(solution)/shard_map/ppermute | solution.py:32
  17.5 22.7 %collective-permute-start.1 = (bf16[512,256]{1,0:T(8,128)(2,1)S(1)}, bf16[512,256]{1,0:T(8,128)(2,1)}, u32[]{:S(2)}, u32[]{:S(2)}) collective-permute-start(bf16[512,256]{1,0:T(8,128)(2,1)S(1)} %fusion.28), channel_id=1, source_target_pairs={{0,4},{1,3},{2,6},{3,1},{4,0},{5,7},{6,2},{7,5},{8,12},{9,11},{10,... | collective-permute-start | bytes 786440 | tf_op jit(solution)/shard_map/ppermute | solution.py:32
  19.5 21.9 %collective-permute-start.8 = (bf16[512,256]{1,0:T(8,128)(2,1)}, bf16[512,256]{1,0:T(8,128)(2,1)}, u32[]{:S(2)}, u32[]{:S(2)}) collective-permute-start(bf16[512,256]{1,0:T(8,128)(2,1)} %collective-permute-done.3), channel_id=1, source_target_pairs={{8,16},{9,17},{10,18},{11,19},{12,20},{13,21},{14,22},{15,23},{16,... | collective-permute-start | bytes 786440 | tf_op jit(solution)/shard_map/ppermute | solution.py:32
  24.4 17.8 %collective-permute-start.9 = (bf16[512,256]{1,0:T(8,128)(2,1)}, bf16[512,256]{1,0:T(8,128)(2,1)}, u32[]{:S(2)}, u32[]{:S(2)}) collective-permute-start(bf16[512,256]{1,0:T(8,128)(2,1)} %collective-permute-done.4), channel_id=1, source_target_pairs={{8,0},{9,1},{10,2},{11,3},{12,4},{13,5},{14,6},{15,7},{16,8},{17,9... | collective-permute-start | bytes 786440 | tf_op jit(solution)/shard_map/ppermute | solution.py:32
  38.6 28.0 %collective-permute-start.2 = (bf16[512,256]{1,0:T(8,128)(2,1)S(1)}, bf16[512,256]{1,0:T(8,128)(2,1)S(1)}, u32[]{:S(2)}, u32[]{:S(2)}) collective-permute-start(bf16[512,256]{1,0:T(8,128)(2,1)S(1)} %collective-permute-done), channel_id=1, source_target_pairs={{0,4},{1,3},{2,6},{3,1},{4,0},{5,7},{6,2},{7,5},{8,12},{9,11},{10,... | collective-permute-start | bytes 786440 | tf_op jit(solution)/shard_map/ppermute | solution.py:32
  42.2 8.8 %collective-permute-start.14 = (bf16[512,256]{1,0:T(8,128)(2,1)}, bf16[512,256]{1,0:T(8,128)(2,1)S(1)}, u32[]{:S(2)}, u32[]{:S(2)}) collective-permute-start(bf16[512,256]{1,0:T(8,128)(2,1)} %collective-permute-done.9), channel_id=1, source_target_pairs={{8,0},{9,1},{10,2},{11,3},{12,4},{13,5},{14,6},{15,7}} | collective-permute-start | bytes 786440 | tf_op jit(solution)/shard_map/ppermute | solution.py:32
  54.7 9.3 %collective-permute-start.6 = (bf16[512,256]{1,0:T(8,128)(2,1)S(1)}, bf16[512,256]{1,0:T(8,128)(2,1)S(1)}, u32[]{:S(2)}, u32[]{:S(2)}) collective-permute-start(bf16[512,256]{1,0:T(8,128)(2,1)S(1)} %get-tuple-element.15), channel_id=1, source_target_pairs={{0,4},{1,3},{2,6},{3,1},{4,0},{5,7},{6,2},{7,5},{8,12},{9,11},{10,... | collective-permute-start | bytes 786440 | tf_op jit(solution)/shard_map/ppermute | solution.py:32
  56.3 9.1 %collective-permute-start.5 = (bf16[512,256]{1,0:T(8,128)(2,1)S(1)}, bf16[512,256]{1,0:T(8,128)(2,1)S(1)}, u32[]{:S(2)}, u32[]{:S(2)}) collective-permute-start(bf16[512,256]{1,0:T(8,128)(2,1)S(1)} %get-tuple-element.15), channel_id=1, source_target_pairs={{0,2},{1,5},{2,0},{3,7},{4,6},{5,1},{6,4},{7,3},{8,10},{9,13},{10,... | collective-permute-start | bytes 786440 | tf_op jit(solution)/shard_map/ppermute | solution.py:32
  56.9 21.2 %collective-permute-start.11 = (bf16[512,256]{1,0:T(8,128)(2,1)S(1)}, bf16[512,256]{1,0:T(8,128)(2,1)S(1)}, u32[]{:S(2)}, u32[]{:S(2)}) collective-permute-start(bf16[512,256]{1,0:T(8,128)(2,1)S(1)} %get-tuple-element.12), channel_id=1, source_target_pairs={{0,4},{1,3},{2,6},{3,1},{4,0},{5,7},{6,2},{7,5},{8,12},{9,11},{10,... | collective-permute-start | bytes 786440 | tf_op jit(solution)/shard_map/ppermute | solution.py:32
  58.0 11.3 %collective-permute-start.10 = (bf16[512,256]{1,0:T(8,128)(2,1)S(1)}, bf16[512,256]{1,0:T(8,128)(2,1)S(1)}, u32[]{:S(2)}, u32[]{:S(2)}) collective-permute-start(bf16[512,256]{1,0:T(8,128)(2,1)S(1)} %get-tuple-element.12), channel_id=1, source_target_pairs={{0,2},{1,5},{2,0},{3,7},{4,6},{5,1},{6,4},{7,3},{8,10},{9,13},{10,... | collective-permute-start | bytes 786440 | tf_op jit(solution)/shard_map/ppermute | solution.py:32
  64.1 10.9 %collective-permute-start.15 = (bf16[512,256]{1,0:T(8,128)(2,1)S(1)}, bf16[512,256]{1,0:T(8,128)(2,1)S(1)}, u32[]{:S(2)}, u32[]{:S(2)}) collective-permute-start(bf16[512,256]{1,0:T(8,128)(2,1)S(1)} %get-tuple-element.13), channel_id=1, source_target_pairs={{0,2},{1,5},{2,0},{3,7},{4,6},{5,1},{6,4},{7,3},{8,10},{9,13},{10,... | collective-permute-start | bytes 786440 | tf_op jit(solution)/shard_map/ppermute | solution.py:32
  65.4 12.8 %collective-permute-start.16 = (bf16[512,256]{1,0:T(8,128)(2,1)S(1)}, bf16[512,256]{1,0:T(8,128)(2,1)S(1)}, u32[]{:S(2)}, u32[]{:S(2)}) collective-permute-start(bf16[512,256]{1,0:T(8,128)(2,1)S(1)} %get-tuple-element.13), channel_id=1, source_target_pairs={{0,4},{1,3},{2,6},{3,1},{4,0},{5,7},{6,2},{7,5},{8,12},{9,11},{10,... | collective-permute-start | bytes 786440 | tf_op jit(solution)/shard_map/ppermute | solution.py:32
  66.6 11.9 %collective-permute-start.7 = (bf16[512,256]{1,0:T(8,128)(2,1)S(1)}, bf16[512,256]{1,0:T(8,128)(2,1)S(1)}, u32[]{:S(2)}, u32[]{:S(2)}) collective-permute-start(bf16[512,256]{1,0:T(8,128)(2,1)S(1)} %collective-permute-done.5), channel_id=1, source_target_pairs={{0,4},{1,3},{2,6},{3,1},{4,0},{5,7},{6,2},{7,5},{8,12},{9,11},{10,... | collective-permute-start | bytes 786440 | tf_op jit(solution)/shard_map/ppermute | solution.py:32
  69.3 9.5 %collective-permute-start.12 = (bf16[512,256]{1,0:T(8,128)(2,1)S(1)}, bf16[512,256]{1,0:T(8,128)(2,1)S(1)}, u32[]{:S(2)}, u32[]{:S(2)}) collective-permute-start(bf16[512,256]{1,0:T(8,128)(2,1)S(1)} %collective-permute-done.10), channel_id=1, source_target_pairs={{0,4},{1,3},{2,6},{3,1},{4,0},{5,7},{6,2},{7,5},{8,12},{9,11},{10,... | collective-permute-start | bytes 786440 | tf_op jit(solution)/shard_map/ppermute | solution.py:32
  74.9 6.7 %collective-permute-start.17 = (bf16[512,256]{1,0:T(8,128)(2,1)S(1)}, bf16[512,256]{1,0:T(8,128)(2,1)S(1)}, u32[]{:S(2)}, u32[]{:S(2)}) collective-permute-start(bf16[512,256]{1,0:T(8,128)(2,1)S(1)} %collective-permute-done.15), channel_id=1, source_target_pairs={{0,4},{1,3},{2,6},{3,1},{4,0},{5,7},{6,2},{7,5},{8,12},{9,11},{10,... | collective-permute-start | bytes 786440 | tf_op jit(solution)/shard_map/ppermute | solution.py:32
  83.3 9.2 %collective-permute-start.22 = (bf16[2,512,256]{2,1,0:T(8,128)(2,1)S(1)}, bf16[2,512,256]{2,1,0:T(8,128)(2,1)S(1)}, u32[]{:S(2)}, u32[]{:S(2)}) collective-permute-start(bf16[2,512,256]{2,1,0:T(8,128)(2,1)S(1)} %pad_maximum_fusion.2), channel_id=1, source_target_pairs={{0,4},{1,3},{2,6},{3,1},{4,0},{5,7},{6,2},{7,5},{8,12},{9,11},{10,... | collective-permute-start | bytes 1572872 | tf_op jit(solution)/shard_map/ppermute | solution.py:32
  85.7 15.9 %collective-permute-start.24 = (bf16[2,512,256]{2,1,0:T(8,128)(2,1)S(1)}, bf16[2,512,256]{2,1,0:T(8,128)(2,1)S(1)}, u32[]{:S(2)}, u32[]{:S(2)}) collective-permute-start(bf16[2,512,256]{2,1,0:T(8,128)(2,1)S(1)} %pad_maximum_fusion.3), channel_id=1, source_target_pairs={{0,4},{1,3},{2,6},{3,1},{4,0},{5,7},{6,2},{7,5},{8,12},{9,11},{10,... | collective-permute-start | bytes 1572872 | tf_op jit(solution)/shard_map/ppermute | solution.py:32
  92.8 6.4 %collective-permute-start.23 = (bf16[512,256]{1,0:T(8,128)(2,1)S(1)}, bf16[512,256]{1,0:T(8,128)(2,1)S(1)}, u32[]{:S(2)}, u32[]{:S(2)}) collective-permute-start(bf16[512,256]{1,0:T(8,128)(2,1)S(1)} %fusion.32), channel_id=1, source_target_pairs={{0,2},{1,5},{2,0},{3,7},{4,6},{5,1},{6,4},{7,3},{8,10},{9,13},{10,... | collective-permute-start | bytes 786440 | tf_op jit(solution)/shard_map/ppermute | solution.py:32
  99.3 13.6 %collective-permute-start.26 = (f32[512,256]{1,0:T(8,128)S(1)}, f32[512,256]{1,0:T(8,128)S(1)}, u32[]{:S(2)}, u32[]{:S(2)}) collective-permute-start(f32[512,256]{1,0:T(8,128)S(1)} %fusion.33), channel_id=1, source_target_pairs={{0,8},{1,9},{2,10},{3,11},{4,12},{5,13},{6,14},{7,15}} | collective-permute-start | bytes 1572872 | tf_op jit(solution)/shard_map/ppermute | solution.py:32
  101.0 12.0 %collective-permute-start.29 = (f32[512,256]{1,0:T(8,128)S(1)}, f32[512,256]{1,0:T(8,128)S(1)}, u32[]{:S(2)}, u32[]{:S(2)}) collective-permute-start(f32[512,256]{1,0:T(8,128)S(1)} %fusion.33), channel_id=1, source_target_pairs={{24,16},{25,17},{26,18},{27,19},{28,20},{29,21},{30,22},{31,23}} | collective-permute-start | bytes 1572872 | tf_op jit(solution)/shard_map/ppermute | solution.py:32
  101.9 8.2 %collective-permute-start.25 = (bf16[512,256]{1,0:T(8,128)(2,1)S(1)}, bf16[512,256]{1,0:T(8,128)(2,1)S(1)}, u32[]{:S(2)}, u32[]{:S(2)}) collective-permute-start(bf16[512,256]{1,0:T(8,128)(2,1)S(1)} %fusion.30), channel_id=1, source_target_pairs={{0,2},{1,5},{2,0},{3,7},{4,6},{5,1},{6,4},{7,3},{8,10},{9,13},{10,... | collective-permute-start | bytes 786440 | tf_op jit(solution)/shard_map/ppermute | solution.py:32
  103.2 16.2 %collective-permute-start.20 = (bf16[2,512,256]{2,1,0:T(8,128)(2,1)S(1)}, bf16[2,512,256]{2,1,0:T(8,128)(2,1)S(1)}, u32[]{:S(2)}, u32[]{:S(2)}) collective-permute-start(bf16[2,512,256]{2,1,0:T(8,128)(2,1)S(1)} %pad_maximum_fusion.1), channel_id=1, source_target_pairs={{0,4},{1,3},{2,6},{3,1},{4,0},{5,7},{6,2},{7,5},{8,12},{9,11},{10,... | collective-permute-start | bytes 1572872 | tf_op jit(solution)/shard_map/ppermute | solution.py:32
  114.3 15.5 %collective-permute-start.27 = (f32[512,256]{1,0:T(8,128)S(1)}, f32[512,256]{1,0:T(8,128)S(1)}, u32[]{:S(2)}, u32[]{:S(2)}) collective-permute-start(f32[512,256]{1,0:T(8,128)S(1)} %get-tuple-element.6), channel_id=1, source_target_pairs={{0,8},{1,9},{2,10},{3,11},{4,12},{5,13},{6,14},{7,15},{8,16},{9,17... | collective-permute-start | bytes 1572872 | tf_op jit(solution)/shard_map/ppermute | solution.py:32
  118.7 11.1 %collective-permute-start.30 = (f32[512,256]{1,0:T(8,128)S(1)}, f32[512,256]{1,0:T(8,128)S(1)}, u32[]{:S(2)}, u32[]{:S(2)}) collective-permute-start(f32[512,256]{1,0:T(8,128)S(1)} %get-tuple-element.7), channel_id=1, source_target_pairs={{16,8},{17,9},{18,10},{19,11},{20,12},{21,13},{22,14},{23,15},{24,... | collective-permute-start | bytes 1572872 | tf_op jit(solution)/shard_map/ppermute | solution.py:32
  119.7 9.2 %collective-permute-start.21 = (bf16[512,256]{1,0:T(8,128)(2,1)S(1)}, bf16[512,256]{1,0:T(8,128)(2,1)S(1)}, u32[]{:S(2)}, u32[]{:S(2)}) collective-permute-start(bf16[512,256]{1,0:T(8,128)(2,1)S(1)} %fusion.34), channel_id=1, source_target_pairs={{0,2},{1,5},{2,0},{3,7},{4,6},{5,1},{6,4},{7,3},{8,10},{9,13},{10,... | collective-permute-start | bytes 786440 | tf_op jit(solution)/shard_map/ppermute | solution.py:32
  120.2 20.0 %collective-permute-start.18 = (bf16[2,512,256]{2,1,0:T(8,128)(2,1)S(1)}, bf16[2,512,256]{2,1,0:T(8,128)(2,1)S(1)}, u32[]{:S(2)}, u32[]{:S(2)}) collective-permute-start(bf16[2,512,256]{2,1,0:T(8,128)(2,1)S(1)} %pad_maximum_fusion), channel_id=1, source_target_pairs={{0,4},{1,3},{2,6},{3,1},{4,0},{5,7},{6,2},{7,5},{8,12},{9,11},{10,... | collective-permute-start | bytes 1572872 | tf_op jit(solution)/shard_map/ppermute | solution.py:32
  130.7 18.0 %collective-permute-start.28 = (f32[512,256]{1,0:T(8,128)S(1)}, f32[512,256]{1,0:T(8,128)S(1)}, u32[]{:S(2)}, u32[]{:S(2)}) collective-permute-start(f32[512,256]{1,0:T(8,128)S(1)} %get-tuple-element.8), channel_id=1, source_target_pairs={{0,8},{1,9},{2,10},{3,11},{4,12},{5,13},{6,14},{7,15},{8,16},{9,17... | collective-permute-start | bytes 1572872 | tf_op jit(solution)/shard_map/ppermute | solution.py:32
  138.9 14.0 %collective-permute-start.31 = (f32[512,256]{1,0:T(8,128)S(1)}, f32[512,256]{1,0:T(8,128)S(1)}, u32[]{:S(2)}, u32[]{:S(2)}) collective-permute-start(f32[512,256]{1,0:T(8,128)S(1)} %get-tuple-element.9), channel_id=1, source_target_pairs={{8,0},{9,1},{10,2},{11,3},{12,4},{13,5},{14,6},{15,7},{16,8},{17,9... | collective-permute-start | bytes 1572872 | tf_op jit(solution)/shard_map/ppermute | solution.py:32
  156.0 8.3 %collective-permute-start.41 = (bf16[512,256]{1,0:T(8,128)(2,1)S(1)}, bf16[512,256]{1,0:T(8,128)(2,1)S(1)}, u32[]{:S(2)}, u32[]{:S(2)}) collective-permute-start(bf16[512,256]{1,0:T(8,128)(2,1)S(1)} %get-tuple-element.4), channel_id=1, source_target_pairs={{8,0},{9,1},{10,2},{11,3},{12,4},{13,5},{14,6},{15,7},{16,8},{17,9... | collective-permute-start | bytes 786440 | tf_op jit(solution)/shard_map/ppermute | solution.py:32
  157.3 9.5 %collective-permute-start.37 = (bf16[512,256]{1,0:T(8,128)(2,1)S(1)}, bf16[512,256]{1,0:T(8,128)(2,1)S(1)}, u32[]{:S(2)}, u32[]{:S(2)}) collective-permute-start(bf16[512,256]{1,0:T(8,128)(2,1)S(1)} %get-tuple-element.4), channel_id=1, source_target_pairs={{0,2},{1,5},{2,0},{3,7},{4,6},{5,1},{6,4},{7,3},{8,10},{9,13},{10,... | collective-permute-start | bytes 786440 | tf_op jit(solution)/shard_map/ppermute | solution.py:32
  159.9 7.2 %collective-permute-start.45 = (bf16[512,256]{1,0:T(8,128)(2,1)S(1)}, bf16[512,256]{1,0:T(8,128)(2,1)S(1)}, u32[]{:S(2)}, u32[]{:S(2)}) collective-permute-start(bf16[512,256]{1,0:T(8,128)(2,1)S(1)} %collective-permute-done.40), channel_id=1, source_target_pairs={{8,16},{9,17},{10,18},{11,19},{12,20},{13,21},{14,22},{15,23},{16,... | collective-permute-start | bytes 786440 | tf_op jit(solution)/shard_map/ppermute | solution.py:32
  164.3 8.7 %collective-permute-start.46 = (bf16[512,256]{1,0:T(8,128)(2,1)S(1)}, bf16[512,256]{1,0:T(8,128)(2,1)S(1)}, u32[]{:S(2)}, u32[]{:S(2)}) collective-permute-start(bf16[512,256]{1,0:T(8,128)(2,1)S(1)} %collective-permute-done.41), channel_id=1, source_target_pairs={{8,0},{9,1},{10,2},{11,3},{12,4},{13,5},{14,6},{15,7},{16,8},{17,9... | collective-permute-start | bytes 786440 | tf_op jit(solution)/shard_map/ppermute | solution.py:32
  165.6 10.7 %collective-permute-start.38 = (bf16[512,256]{1,0:T(8,128)(2,1)S(1)}, bf16[512,256]{1,0:T(8,128)(2,1)S(1)}, u32[]{:S(2)}, u32[]{:S(2)}) collective-permute-start(bf16[512,256]{1,0:T(8,128)(2,1)S(1)} %get-tuple-element.4), channel_id=1, source_target_pairs={{0,4},{1,3},{2,6},{3,1},{4,0},{5,7},{6,2},{7,5},{8,12},{9,11},{10,... | collective-permute-start | bytes 786440 | tf_op jit(solution)/shard_map/ppermute | solution.py:32
  167.1 9.4 %collective-permute-start.50 = (bf16[512,256]{1,0:T(8,128)(2,1)S(1)}, bf16[512,256]{1,0:T(8,128)(2,1)S(1)}, u32[]{:S(2)}, u32[]{:S(2)}) collective-permute-start(bf16[512,256]{1,0:T(8,128)(2,1)S(1)} %collective-permute-done.45), channel_id=1, source_target_pairs={{16,24},{17,25},{18,26},{19,27},{20,28},{21,29},{22,30},{23,31}} | collective-permute-start | bytes 786440 | tf_op jit(solution)/shard_map/ppermute | solution.py:32
  173.0 8.3 %collective-permute-start.51 = (bf16[512,256]{1,0:T(8,128)(2,1)S(1)}, bf16[512,256]{1,0:T(8,128)(2,1)S(1)}, u32[]{:S(2)}, u32[]{:S(2)}) collective-permute-start(bf16[512,256]{1,0:T(8,128)(2,1)S(1)} %collective-permute-done.46), channel_id=1, source_target_pairs={{8,0},{9,1},{10,2},{11,3},{12,4},{13,5},{14,6},{15,7}} | collective-permute-start | bytes 786440 | tf_op jit(solution)/shard_map/ppermute | solution.py:32
  174.7 28.7 %collective-permute-start.39 = (bf16[512,256]{1,0:T(8,128)(2,1)S(1)}, bf16[512,256]{1,0:T(8,128)(2,1)S(1)}, u32[]{:S(2)}, u32[]{:S(2)}) collective-permute-start(bf16[512,256]{1,0:T(8,128)(2,1)S(1)} %collective-permute-done.37), channel_id=1, source_target_pairs={{0,4},{1,3},{2,6},{3,1},{4,0},{5,7},{6,2},{7,5},{8,12},{9,11},{10,... | collective-permute-start | bytes 786440 | tf_op jit(solution)/shard_map/ppermute | solution.py:32
  183.8 8.6 %collective-permute-start.43 = (bf16[512,256]{1,0:T(8,128)(2,1)S(1)}, bf16[512,256]{1,0:T(8,128)(2,1)S(1)}, u32[]{:S(2)}, u32[]{:S(2)}) collective-permute-start(bf16[512,256]{1,0:T(8,128)(2,1)S(1)} %get-tuple-element.14), channel_id=1, source_target_pairs={{0,4},{1,3},{2,6},{3,1},{4,0},{5,7},{6,2},{7,5},{8,12},{9,11},{10,... | collective-permute-start | bytes 786440 | tf_op jit(solution)/shard_map/ppermute | solution.py:32
  185.3 7.7 %collective-permute-start.42 = (bf16[512,256]{1,0:T(8,128)(2,1)S(1)}, bf16[512,256]{1,0:T(8,128)(2,1)S(1)}, u32[]{:S(2)}, u32[]{:S(2)}) collective-permute-start(bf16[512,256]{1,0:T(8,128)(2,1)S(1)} %get-tuple-element.14), channel_id=1, source_target_pairs={{0,2},{1,5},{2,0},{3,7},{4,6},{5,1},{6,4},{7,3},{8,10},{9,13},{10,... | collective-permute-start | bytes 786440 | tf_op jit(solution)/shard_map/ppermute | solution.py:32
  185.6 20.5 %collective-permute-start.48 = (bf16[512,256]{1,0:T(8,128)(2,1)S(1)}, bf16[512,256]{1,0:T(8,128)(2,1)S(1)}, u32[]{:S(2)}, u32[]{:S(2)}) collective-permute-start(bf16[512,256]{1,0:T(8,128)(2,1)S(1)} %get-tuple-element.11), channel_id=1, source_target_pairs={{0,4},{1,3},{2,6},{3,1},{4,0},{5,7},{6,2},{7,5},{8,12},{9,11},{10,... | collective-permute-start | bytes 786440 | tf_op jit(solution)/shard_map/ppermute | solution.py:32
  186.2 17.8 %collective-permute-start.47 = (bf16[512,256]{1,0:T(8,128)(2,1)S(1)}, bf16[512,256]{1,0:T(8,128)(2,1)S(1)}, u32[]{:S(2)}, u32[]{:S(2)}) collective-permute-start(bf16[512,256]{1,0:T(8,128)(2,1)S(1)} %get-tuple-element.11), channel_id=1, source_target_pairs={{0,2},{1,5},{2,0},{3,7},{4,6},{5,1},{6,4},{7,3},{8,10},{9,13},{10,... | collective-permute-start | bytes 786440 | tf_op jit(solution)/shard_map/ppermute | solution.py:32
  192.4 9.2 %collective-permute-start.52 = (bf16[512,256]{1,0:T(8,128)(2,1)S(1)}, bf16[512,256]{1,0:T(8,128)(2,1)S(1)}, u32[]{:S(2)}, u32[]{:S(2)}) collective-permute-start(bf16[512,256]{1,0:T(8,128)(2,1)S(1)} %get-tuple-element.10), channel_id=1, source_target_pairs={{0,2},{1,5},{2,0},{3,7},{4,6},{5,1},{6,4},{7,3},{8,10},{9,13},{10,... | collective-permute-start | bytes 786440 | tf_op jit(solution)/shard_map/ppermute | solution.py:32
  193.1 13.3 %collective-permute-start.53 = (bf16[512,256]{1,0:T(8,128)(2,1)S(1)}, bf16[512,256]{1,0:T(8,128)(2,1)S(1)}, u32[]{:S(2)}, u32[]{:S(2)}) collective-permute-start(bf16[512,256]{1,0:T(8,128)(2,1)S(1)} %get-tuple-element.10), channel_id=1, source_target_pairs={{0,4},{1,3},{2,6},{3,1},{4,0},{5,7},{6,2},{7,5},{8,12},{9,11},{10,... | collective-permute-start | bytes 786440 | tf_op jit(solution)/shard_map/ppermute | solution.py:32
  203.4 10.8 %collective-permute-start.54 = (bf16[512,256]{1,0:T(8,128)(2,1)S(1)}, bf16[512,256]{1,0:T(8,128)(2,1)S(1)}, u32[]{:S(2)}, u32[]{:S(2)}) collective-permute-start(bf16[512,256]{1,0:T(8,128)(2,1)S(1)} %collective-permute-done.52), channel_id=1, source_target_pairs={{0,4},{1,3},{2,6},{3,1},{4,0},{5,7},{6,2},{7,5},{8,12},{9,11},{10,... | collective-permute-start | bytes 786440 | tf_op jit(solution)/shard_map/ppermute | solution.py:32
  204.0 9.6 %collective-permute-start.49 = (bf16[512,256]{1,0:T(8,128)(2,1)S(1)}, bf16[512,256]{1,0:T(8,128)(2,1)S(1)}, u32[]{:S(2)}, u32[]{:S(2)}) collective-permute-start(bf16[512,256]{1,0:T(8,128)(2,1)S(1)} %collective-permute-done.47), channel_id=1, source_target_pairs={{0,4},{1,3},{2,6},{3,1},{4,0},{5,7},{6,2},{7,5},{8,12},{9,11},{10,... | collective-permute-start | bytes 786440 | tf_op jit(solution)/shard_map/ppermute | solution.py:32
  233.4 40.4 %reduce-scatter.3.cloned.1.call-start = ((), (), s32[]{:S(2)}) async-start(), calls=%async_computation.2 | async-start | bytes 6291456 | tf_op jit(solution)/shard_map/reduce_scatter | solution.py:169
  (42 other events, 374.2 us)
Sparse Core Ops, SparseCore 0:
  233.6 9.3 reduce-scatter.4
  252.4 9.3 reduce-scatter.2

commit v2 on v0

v2 whole, which is shorter than its diff:
```python
import functools

import jax
import jax.numpy as jnp
from jax import lax
from jax.experimental import pallas as pl
from jax.experimental.pallas import tpu as pltpu
from jax.sharding import PartitionSpec as P


F32, BF16 = jnp.float32, jnp.bfloat16
VMEM_BYTES = 24 * 1024 * 1024
LANES = 128


def after(x, *earlier):
    return lax.optimization_barrier((x, *earlier))[0]


class Grid:
    def __init__(self, lat, dp):
        self.lat, self.dp, self.slots = lat, dp, lat // 4
        self.me = lax.axis_index("lat")
        self.rank = lax.axis_index("dp")
        first = jnp.where(self.rank % 2 == 0, 1, 2)
        members = jnp.stack([jnp.zeros_like(first), first, 3 - first, jnp.full_like(first, 3)])
        self.across = (0, 2, 1, 3) if dp == 2 else (0, 1, 2, 3)
        side = self.rank // (dp // 2)
        orders = [self.me ^ (4 * s + members) for s in range(self.slots)]
        self.order = [jnp.append(o, side).astype(jnp.int32) for o in orders]
        self.every = jnp.concatenate(orders).astype(jnp.int32)

    def swap(self, x, even, odd):
        pairs = []
        for i in range(self.lat):
            for d in range(self.dp):
                pairs.append((i * self.dp + d, (i ^ (even if d % 2 == 0 else odd)) * self.dp + d))
        return lax.ppermute(x, ("lat", "dp"), pairs)

    def swap_first(self, x):
        return self.swap(x, 1, 2)

    def swap_second(self, x):
        return self.swap(x, 2, 1)

    def swap_plane(self, x, bit):
        return self.swap(x, 4 * bit, 4 * bit)

    def swap_core(self, x):
        pairs = []
        for i in range(self.lat):
            for d in range(self.dp):
                pairs.append((i * self.dp + d, i * self.dp + (d ^ self.dp // 2)))
        return lax.ppermute(x, ("lat", "dp"), pairs)

    def spread(self, x, axis):
        h = self.dp // 4
        while h >= 1:
            bit = self.rank // h % 2
            size = x.shape[axis] // 2
            mine = lax.dynamic_slice_in_dim(x, bit * size, size, axis)
            other = lax.dynamic_slice_in_dim(x, (1 - bit) * size, size, axis)
            x = mine + lax.ppermute(other, "dp", [(d, d ^ h) for d in range(self.dp)])
            h //= 2
        return x

    def gather(self, own, use):
        column = [own]
        for s in range(1, self.slots):
            column.append(self.swap_plane(column[s & (s - 1)], s & -s))
        out, done = [], []
        last = self.slots - 1
        for s, block in enumerate(column):
            if s == 1 and last > 1:
                block = after(block, column[2], *out[0][1:])
            a = self.swap_first(block)
            b = self.swap_second(block)
            c = a
            if s == 1 < last:
                c = after(a, done[0])
            if s == 2 < last:
                c = after(a, column[3])
            if s == last > 2:
                c = after(a, done[1])
            out.append((block, a, b, self.swap_second(c)))
            done.append(use(s, out[-1]))
        return out

    def scatter_sum(self, part):
        column = [None] * self.slots
        earlier = {}
        got = None
        for s in reversed(range(self.slots)):
            keep, send = part(s, earlier.get(s))
            there = self.swap_second(send)
            pair = keep + there.astype(F32)
            other = pair[1].astype(BF16)
            got = self.swap_first(other if got is None else after(other, got))
            if s == self.slots - 1:
                earlier = {s - 2: there, s - 3: got}
            column[s] = pair[0] + got.astype(F32)
        for s in reversed(range(1, self.slots)):
            t = s & (s - 1)
            column[t] = column[t] + self.swap_plane(column[s].astype(BF16), s & -s).astype(F32)
        return column[0]


def plain(width):
    return width % LANES != 0


def taken(x, index, width, axis):
    return lax.dynamic_slice_in_dim(x, index * width, width, axis)


def gate_of(active, lats):
    rows, blocks = active.shape
    block = lats // blocks
    return jnp.concatenate(
        [jnp.broadcast_to(active[:, b:b + 1].astype(F32), (rows, block)) for b in range(blocks)], axis=1
    )


def activate(total, active):
    positive = jnp.maximum(total, 0.0)
    gated = positive * gate_of(active, total.shape[1])
    return (positive * gated).astype(BF16), 2.0 * gated


def outer(a, b):
    return lax.dot_general(a, b, (((0,), (0,)), ((), ())), preferred_element_type=F32)


def call(body, order, operands, in_specs, out_shape, out_specs, flops, moved, name, scratch=(), steps=1):
    return pl.pallas_call(
        body,
        grid_spec=pltpu.PrefetchScalarGridSpec(
            num_scalar_prefetch=1, grid=(steps,), in_specs=in_specs, out_specs=out_specs, scratch_shapes=scratch
        ),
        out_shape=out_shape,
        compiler_params=pltpu.CompilerParams(vmem_limit_bytes=VMEM_BYTES),
        cost_estimate=pl.CostEstimate(flops=flops, bytes_accessed=moved, transcendentals=0),
        name=name,
    )(order, *operands)


def whole(shape):
    return pl.BlockSpec(shape, lambda i, order: (0,) * len(shape))


def encode_body(last, order, x0, x1, x2, x3, w0, w1, w2, w3, acc, *rest):
    *rest, turned = rest
    width = x0.shape[1]
    total = acc[...]
    for m, (x, w) in enumerate(((x0, w0), (x1, w1), (x2, w2), (x3, w3))):
        total = total + jnp.dot(x[...], w[...], preferred_element_type=F32)
        turned[m * width:(m + 1) * width, :] = x[...].T
    if not last:
        rest[0][...] = total
        return
    active, act, slope = rest
    act[...], slope[...] = activate(total, active[...])


def encode(order, blocks, weight, acc, active):
    rows, width = blocks[0].shape
    lats = weight.shape[1]
    last = active is not None
    if plain(width):
        total = acc
        for m in range(4):
            total = total + jnp.dot(blocks[m], taken(weight, order[m], width, 0), preferred_element_type=F32)
        turned = jnp.concatenate([x.T for x in blocks], axis=0)
        return (*activate(total, active), turned) if last else (total, turned)
    row_specs = [
        pl.BlockSpec((width, lats), functools.partial(lambda m, i, order: (order[m], 0), m)) for m in range(4)
    ]
    operands = list(blocks) + [weight] * 4 + [acc]
    specs = [whole((rows, width))] * 4 + row_specs + [whole(acc.shape)]
    if last:
        operands.append(active)
        specs.append(whole(active.shape))
        out = [jax.ShapeDtypeStruct((rows, lats), BF16), jax.ShapeDtypeStruct((rows, lats), F32)]
    else:
        out = [jax.ShapeDtypeStruct((rows, lats), F32)]
    out.append(jax.ShapeDtypeStruct((4 * width, rows), BF16))
    return call(
        functools.partial(encode_body, last), order, operands, specs, out, [whole(o.shape) for o in out],
        8 * rows * width * lats, 8 * rows * width + 8 * width * lats + 8 * rows * lats, "encode",
    )


def column_specs(lats, width):
    return [pl.BlockSpec((lats, width), functools.partial(lambda m, i, order: (0, order[m]), m)) for m in range(4)]


def decode_body(order, act, w0, w1, w2, w3, keep, send):
    a = act[...]
    keep[0] = jnp.dot(a, w0[...], preferred_element_type=F32)
    keep[1] = jnp.dot(a, w1[...], preferred_element_type=F32)
    send[0] = jnp.dot(a, w2[...], preferred_element_type=F32).astype(BF16)
    send[1] = jnp.dot(a, w3[...], preferred_element_type=F32).astype(BF16)


def decode(order, act, weight, width):
    rows, lats = act.shape
    if plain(width):
        terms = [jnp.dot(act, taken(weight, order[m], width, 1), preferred_element_type=F32) for m in range(4)]
        return jnp.stack(terms[:2]), jnp.stack(terms[2:]).astype(BF16)
    out = [jax.ShapeDtypeStruct((2, rows, width), F32), jax.ShapeDtypeStruct((2, rows, width), BF16)]
    return call(
        decode_body, order, [act] + [weight] * 4, [whole(act.shape)] + column_specs(lats, width), out,
        [whole((2, rows, width))] * 2, 8 * rows * width * lats, 12 * rows * width + 8 * width * lats, "decode",
    )


def backward_body(last, across, order, act, e0, e1, e2, e3, w0, w1, w2, w3, dact, squares, *rest):
    rows, width = e0.shape
    half = act.shape[1] // 2
    total = dact[...]
    square = squares[...]
    if last:
        slope, grad_keep, grad_send, dpre_keep, dpre_send, next_squares = rest
    else:
        grad_keep, grad_send, next_dact, next_squares = rest
    side = order[order.shape[0] - 1]
    mine_at = pl.ds(pl.multiple_of(side * half, half), half)
    other_at = pl.ds(pl.multiple_of((1 - side) * half, half), half)
    mine, other = act[:, mine_at], act[:, other_at]
    for m, (e, w) in enumerate(((e0, w0), (e1, w1), (e2, w2), (e3, w3))):
        block = e[...]
        total = total + lax.dot_general(block, w[...], (((1,), (1,)), ((), ())), preferred_element_type=F32)
        wide = block.astype(F32)
        square = square + jnp.sum((wide * wide).reshape(rows // 8, 8, width), axis=0)
        at, there = pl.ds(m * width, width), pl.ds(across[m] * width, width)
        grad_keep[:, at] = lax.dot_general(mine, block, (((0,), (0,)), ((), ())), preferred_element_type=F32)
        grad_send[:, there] = lax.dot_general(
            other, block, (((0,), (0,)), ((), ())), preferred_element_type=F32
        ).astype(BF16)
    if last:
        next_squares[...] = jnp.broadcast_to(jnp.sum(square, axis=(0, 1), keepdims=True), next_squares.shape)
        slope[...] = total * slope[...]
        dpre_keep[...] = slope[:, mine_at].astype(BF16)
        dpre_send[...] = slope[:, other_at].astype(BF16)
    else:
        next_dact[...] = total
        next_squares[...] = square


def backward(order, across, act, blocks, weight, dact, squares, slope):
    rows, width = blocks[0].shape
    lats = act.shape[1]
    last = slope is not None
    if plain(width):
        half, side = lats // 2, order[-1]
        mine, other = taken(act, side, half, 1), taken(act, 1 - side, half, 1)
        for e, m in zip(blocks, range(4)):
            w = taken(weight, order[m], width, 1)
            dact = dact + lax.dot_general(e, w, (((1,), (1,)), ((), ())), preferred_element_type=F32)
            squares = squares + jnp.sum(e.astype(F32) ** 2) / squares.size
        keep = jnp.concatenate([outer(mine, e) for e in blocks], axis=1)
        send = jnp.concatenate([outer(other, blocks[m]) for m in across], axis=1).astype(BF16)
        if not last:
            return keep, send, dact, squares
        dpre = (dact * slope).astype(BF16)
        squares = jnp.broadcast_to(jnp.sum(squares), (8, LANES))
        return keep, send, taken(dpre, side, half, 1), taken(dpre, 1 - side, half, 1), squares
    operands = [act] + list(blocks) + [weight] * 4 + [dact, squares]
    specs = [whole(act.shape)] + [whole((rows, width))] * 4 + column_specs(lats, width)
    specs += [whole(dact.shape), whole(squares.shape)]
    if last:
        operands.append(slope)
        specs.append(whole(slope.shape))
    out = [
        jax.ShapeDtypeStruct((lats // 2, 4 * width), F32),
        jax.ShapeDtypeStruct((lats // 2, 4 * width), BF16),
    ]
    if last:
        out += [jax.ShapeDtypeStruct((rows, lats // 2), BF16)] * 2
    else:
        out.append(jax.ShapeDtypeStruct((rows, lats), F32))
    out.append(jax.ShapeDtypeStruct((8, 128) if last else squares.shape, F32))
    return call(
        functools.partial(backward_body, last, across), order, operands, specs, out, [whole(o.shape) for o in out],
        16 * rows * width * lats, 8 * rows * width + 20 * width * lats + 8 * rows * lats, "backward",
    )


def decoder_gradient_body(slots, width, order, *refs):
    keeps, gots, out = refs[:slots], refs[slots:2 * slots], refs[-1]
    for s in range(slots):
        for m in range(4):
            at = pl.ds(m * width, width)
            there = pl.ds(pl.multiple_of(order[4 * s + m] * width, width), width)
            out[:, there] = keeps[s][:, at] + gots[s][:, at].astype(F32)


def decoder_gradient(order, keeps, gots, width):
    slots = len(keeps)
    half = keeps[0].shape[0]
    operands = keeps + gots
    size = half * 4 * slots * width
    if plain(width):
        out = jnp.zeros((half, 4 * slots * width), F32)
        for s in range(slots):
            part = keeps[s] + gots[s].astype(F32)
            for m in range(4):
                block = part[:, m * width:(m + 1) * width]
                out = lax.dynamic_update_slice_in_dim(out, block, order[4 * s + m] * width, 1)
        return out
    return call(
        functools.partial(decoder_gradient_body, slots, width), order, operands, [whole(o.shape) for o in operands],
        jax.ShapeDtypeStruct((half, 4 * slots * width), F32), whole((half, 4 * slots * width)), size, 10 * size,
        "decoder_gradient",
    )


def encoder_gradient_body(slots, width, across, order, *refs):
    mine, theirs = refs[:slots], refs[slots:2 * slots]
    dpre, got, out = refs[2 * slots:]
    d, g = dpre[...], got[...]
    for s in range(slots):
        for m in range(4):
            here = jnp.dot(mine[s][m * width:(m + 1) * width, :], d, preferred_element_type=F32)
            at = across[m] * width
            here += jnp.dot(theirs[s][at:at + width, :], g, preferred_element_type=F32)
            out[pl.ds(pl.multiple_of(order[4 * s + m] * width, width), width), :] = here


def encoder_gradient(order, across, mine, theirs, dpre, got, width):
    slots = len(mine)
    rows, half = dpre.shape
    operands = mine + theirs + [dpre, got]
    shape = (4 * slots * width, half)
    if plain(width):
        out = jnp.zeros(shape, F32)
        for s in range(slots):
            for m in range(4):
                a, b = m * width, across[m] * width
                block = jnp.dot(mine[s][a:a + width], dpre, preferred_element_type=F32)
                block += jnp.dot(theirs[s][b:b + width], got, preferred_element_type=F32)
                out = lax.dynamic_update_slice_in_dim(out, block, order[4 * s + m] * width, 0)
        return out
    return call(
        functools.partial(encoder_gradient_body, slots, width, across), order, operands,
        [whole(o.shape) for o in operands], jax.ShapeDtypeStruct(shape, F32), whole(shape),
        4 * shape[0] * rows * half, 4 * shape[0] * rows + 4 * shape[0] * half, "encoder_gradient",
    )


def local(lat, dp, inputs, dec_bias, enc_weight, enc_bias, dec_weight, other_recon, active_blocks):
    grid = Grid(lat, dp)
    rows, width = inputs.shape
    lats = enc_weight.shape[1]
    half = lats // 2
    slots = grid.slots
    bias = dec_bias.astype(F32)[None, :]
    x = inputs.astype(F32)
    sums = [enc_bias[None, :]]

    def enter(s, blocks):
        *sums[:], mine = encode(grid.order[s], blocks, enc_weight, sums[0], active_blocks if s == slots - 1 else None)
        turned.append(mine)
        return sums[0]

    turned = []
    grid.gather((x - bias).astype(BF16), enter)
    act, slope = sums
    theirs = [grid.swap_core(t) for t in turned]

    def part(s, earlier):
        wait = [] if earlier is None else [earlier]
        if s == 0:
            wait += theirs
        return decode(grid.order[s], after(act, *wait) if wait else act, dec_weight, width)

    recon = grid.scatter_sum(part)
    bias, x = (a.astype(F32) for a in lax.optimization_barrier((dec_bias, inputs, act))[:2])
    error_local = recon + (other_recon + bias[None, :]) - x
    state = [jnp.zeros((rows, lats), F32), jnp.zeros((8, width), F32)]
    keeps, gots = [], []

    def back(s, blocks):
        order = grid.order[s]
        if s >= 2:
            state[0] = after(state[0], gots[s - 2])
        keep, send, *state[:] = backward(
            order, grid.across, act, blocks, dec_weight, *state, slope if s == slots - 1 else None
        )
        keeps.append(keep)
        gots.append(grid.swap_core(send))
        return state[0]

    grid.gather(error_local.astype(BF16), back)
    mine, other, squares = state

    got = grid.swap_core(other)
    grad_dec = decoder_gradient(grid.every, keeps, gots, width)
    grad_enc = encoder_gradient(grid.every, grid.across, turned, theirs, mine, after(got, grad_dec), width)

    square = squares
    step = 1
    while step < dp:
        square = square + lax.ppermute(square, "dp", [(d, d ^ step) for d in range(dp)])
        step *= 2
    mse_loss = square[0, 0] / (rows * dp * width * lat)
    return (error_local, mse_loss, grid.spread(grad_dec, 0), grid.spread(grad_enc, 1))


def solution(mesh):
    placed = (
        P("dp", "lat"),
        P("lat"),
        P(None, "lat"),
        P("lat"),
        P("lat", None),
        P("dp", "lat"),
        P("dp", "lat"),
    )
    lat, dp = mesh.shape["lat"], mesh.shape["dp"]
    return jax.shard_map(
        functools.partial(local, lat, dp),
        mesh=mesh,
        in_specs=placed,
        out_specs=(P("dp", "lat"), P(), P(("lat", "dp"), None), P(None, ("lat", "dp"))),
        check_vma=False,
    )
```

time: 444 us -> 163 us (0.37)
  waiting for transfers between devices: 315 us -> 68.5 us
  blocking collectives: 81.1 us -> 0 us
  starting transfers between devices: 0.2 us -> 53.8 us
  matrix products: 25.2 us -> 0 us
  Pallas kernels: 0 us -> 23.1 us
  between operations: 15.6 us -> 2.75 us
  local copies, waits for them, and re-layouts: 2.01 us -> 10.9 us
    reduce_scatter x3 -> x0, waiting for transfers between devices: 176 us -> none  [the longest x1 176 us: local(): lax.psum_scatter(lax.dot_general(dec_weight, activations, (((0,), (1,)),...]
    all_gather x2 -> x0, waiting for transfers between devices: 139 us -> none  [the longest x1 90.2 us: local(): lax.all_gather(error_local.astype(jnp.bfloat16), 'lat', axis=1, tiled=True)]
    ppermute x0 -> x51, waiting for transfers between devices: none -> 68.5 us  [the longest x41 67.7 us: swap(): return lax.ppermute(x, ('lat', 'dp'), pairs)]
    ppermute x0 -> x51, starting transfers between devices: none -> 53.8 us  [the longest x41 50.6 us: swap(): return lax.ppermute(x, ('lat', 'dp'), pairs)]
    all_gather x1 -> x0, blocking collectives: 42.4 us -> none  [local(): lax.all_gather(dec_bias.reshape(1, -1), 'lat', axis=1, tiled=True)]
    psum x1 -> x0, blocking collectives: 38.6 us -> none  [local(): squares = lax.psum(jnp.sum(error_local * error_local), ('lat', 'dp'))]
    dot_general x4 -> x0, matrix products: 25.2 us -> none  [the longest x1 10.2 us: local(): lax.dot_general(centered, dpre, (((0,), (0,)), ((), ())), preferred_eleme...]
    pallas_call x0 -> x14, Pallas kernels: none -> 23.1 us  [call(): pl.pallas_call(body, grid_spec=pltpu.PrefetchScalarGridSpec(num_scalar_pr...]
  transfers between devices with their start and end apart: 5 -> 51, of which waited for: 3 -> 25; matrix products, arithmetic and copies ran while one was open for 2% -> 1% of each run, Pallas kernels for 0% -> 10%
where the time goes in v2:
time: 163 us
  waiting for transfers between devices  68.5 us (42%)
  starting transfers between devices  53.8 us (33%)
  Pallas kernels  23.1 us (14%)
  local copies, waits for them, and re-layouts  10.9 us (7%)
  other arithmetic  3.74 us (2%)
  between operations  2.75 us (2%)
    ppermute x41, waiting for transfers between devices, swap(): return lax.ppermute(x, ('lat', 'dp'), pairs)  67.7 us
    ppermute x41, starting transfers between devices, swap(): return lax.ppermute(x, ('lat', 'dp'), pairs)  50.6 us
    pallas_call x14, Pallas kernels, call(): pl.pallas_call(body, grid_spec=pltpu.PrefetchScalarGridSpec(num_scalar_pr...  23.1 us
    unnamed x37, local copies, waits for them, and re-layouts  10.2 us
  transfers between devices with their start and end apart: 51, of which 25 were waited for; matrix products, arithmetic and copies ran while one was open for 1% of the time, Pallas kernels for 10%

profile of v2, /device:TPU:0, one launch (start us, length us, event | category | flops | bytes accessed | tf_op | source)
XLA Modules:
  0.0 162.8 jit_solution(11364161002081416200)
XLA Ops:
  2.3 3.0 %collective-permute-start.5 = (bf16[512,256]{1,0:T(8,128)(2,1)S(1)}, bf16[512,256]{1,0:T(8,128)(2,1)S(1)}, u32[]{:S(2)}, u32[]{:S(2)}) collective-permute-start(bf16[512,256]{1,0:T(8,128)(2,1)S(1)} %subtract_convert_fusion.x0), channel_id=1, source_target_pairs={{0,2},{1,5},{2,0},{3,7},{4,6},{5,1},{6,4},{7,3},{8,10},{9,13},{10,... | collective-permute-start | bytes 786440 | tf_op jit(solution)/shard_map/ppermute | solution.py:38
  5.3 2.6 %collective-permute-start = (bf16[512,256]{1,0:T(8,128)(2,1)S(1)}, bf16[512,256]{1,0:T(8,128)(2,1)}, u32[]{:S(2)}, u32[]{:S(2)}) collective-permute-start(bf16[512,256]{1,0:T(8,128)(2,1)S(1)} %subtract_convert_fusion.x0), channel_id=1, source_target_pairs={{0,16},{1,17},{2,18},{3,19},{4,20},{5,21},{6,22},{7,23},{8,24},{9,... | collective-permute-start | bytes 786440 | tf_op jit(solution)/shard_map/ppermute | solution.py:38
  7.9 1.5 collective-permute-start.6
  9.4 1.6 collective-permute-start.4
  11.0 2.1 %collective-permute-start.7 = (bf16[512,256]{1,0:T(8,128)(2,1)S(1)}, bf16[512,256]{1,0:T(8,128)(2,1)S(1)}, u32[]{:S(2)}, u32[]{:S(2)}) collective-permute-start(bf16[512,256]{1,0:T(8,128)(2,1)S(1)} %collective-permute-done.5.x1), channel_id=1, source_target_pairs={{0,4},{1,3},{2,6},{3,1},{4,0},{5,7},{6,2},{7,5},{8,12},{9,11},{10,... | collective-permute-start | bytes 786440 | tf_op jit(solution)/shard_map/ppermute | solution.py:38
  13.8 6.0 %collective-permute-done.x0 = bf16[512,256]{1,0:T(8,128)(2,1)} collective-permute-done((bf16[512,256]{1,0:T(8,128)(2,1)S(1)}, bf16[512,256]{1,0:T(8,128)(2,1)}, u32[]{:S(2)}, u32[]{:S(2)}) %collective-permute-start) | collective-permute-done | bytes 262176 | tf_op jit(solution)/shard_map/ppermute | solution.py:38
  24.5 1.6 copy-done.1
  32.3 1.3 collective-permute-start.2
  35.7 1.6 collective-permute-start.3
  37.3 1.9 %collective-permute-done.10.x3 = bf16[512,256]{1,0:T(8,128)(2,1)S(1)} collective-permute-done((bf16[512,256]{1,0:T(8,128)(2,1)S(1)}, bf16[512,256]{1,0:T(8,128)(2,1)S(1)}, u32[]{:S(2)}, u32[]{:S(2)}) %collective-permute-start.10) | collective-permute-done | bytes 262176 | tf_op jit(solution)/shard_map/ppermute | solution.py:38
  39.1 1.9 %encode.5 = (f32[512,256]{1,0:T(8,128)S(1)}, bf16[1024,512]{1,0:T(8,128)(2,1)S(1)}) custom-call(s32[5]{0:T(128)S(1)} %pad_add_fusion.3.order, bf16[512,256]{1,0:T(8,128)(2,1)} %collective-permute-done.4.x0, bf16[512,256]{1,0:T(8,128)(2,1)S(1)} %collective-permute-done.8.x1, bf16[512,256]{1,0:T(8,128)(2,1)S(1)} %collective-permute-done.9.x2, ...), custom_call_target="tpu_custom_call" | custom-call | flops 268435456 | bytes 2621440 | tf_op jit(solution)/shard_map/encode/pallas_call | solution.py:135
  45.9 2.2 %encode.6 = (f32[512,256]{1,0:T(8,128)S(1)}, bf16[1024,512]{1,0:T(8,128)(2,1)S(1)}) custom-call(s32[5]{0:T(128)S(1)} %pad_add_fusion.4.order, bf16[512,256]{1,0:T(8,128)(2,1)} %collective-permute-done.x0, bf16[512,256]{1,0:T(8,128)(2,1)} %collective-permute-done.12.x1, bf16[512,256]{1,0:T(8,128)(2,1)} %collective-permute-done.13.x2, ...), custom_call_target="tpu_custom_call" | custom-call | flops 268435456 | bytes 2621440 | tf_op jit(solution)/shard_map/encode/pallas_call | solution.py:135
  48.1 2.4 %collective-permute-done.11.x3 = bf16[512,256]{1,0:T(8,128)(2,1)} collective-permute-done((bf16[512,256]{1,0:T(8,128)(2,1)}, bf16[512,256]{1,0:T(8,128)(2,1)}, u32[]{:S(2)}, u32[]{:S(2)}) %collective-permute-start.11) | collective-permute-done | bytes 262176 | tf_op jit(solution)/shard_map/ppermute | solution.py:38
  50.5 2.3 %encode.7 = (bf16[512,256]{1,0:T(8,128)(2,1)S(1)}, f32[512,256]{1,0:T(8,128)S(1)}, bf16[1024,512]{1,0:T(8,128)(2,1)S(1)}) custom-call(s32[5]{0:T(128)S(1)} %pad_add_fusion.2.order, bf16[512,256]{1,0:T(8,128)(2,1)} %collective-permute-done.1.x0, bf16[512,256]{1,0:T(8,128)(2,1)} %collective-permute-done.2.x1, bf16[512,256]{1,0:T(8,128)(2,1)} %collective-permute-done.3.x2, ...), custom_call_target="tpu_custom_call" | custom-call | flops 268435456 | bytes 2621440 | tf_op jit(solution)/shard_map/encode/pallas_call | solution.py:135
  56.9 6.2 %collective-permute-done.15 = bf16[2,512,256]{2,1,0:T(8,128)(2,1)S(1)} collective-permute-done((bf16[2,512,256]{2,1,0:T(8,128)(2,1)S(1)}, bf16[2,512,256]{2,1,0:T(8,128)(2,1)S(1)}, u32[]{:S(2)}, u32[]{:S(2)}) %collective-permute-start.15) | collective-permute-done | bytes 524320 | tf_op jit(solution)/shard_map/ppermute | solution.py:38
  63.7 8.6 %collective-permute-done.23 = bf16[2,512,256]{2,1,0:T(8,128)(2,1)S(1)} collective-permute-done((bf16[2,512,256]{2,1,0:T(8,128)(2,1)S(1)}, bf16[2,512,256]{2,1,0:T(8,128)(2,1)S(1)}, u32[]{:S(2)}, u32[]{:S(2)}) %collective-permute-start.23) | collective-permute-done | bytes 524320 | tf_op jit(solution)/shard_map/ppermute | solution.py:38
  72.3 1.5 collective-permute-start.16
  74.8 3.9 %collective-permute-done.16 = bf16[512,256]{1,0:T(8,128)(2,1)S(1)} collective-permute-done((bf16[512,256]{1,0:T(8,128)(2,1)S(1)}, bf16[512,256]{1,0:T(8,128)(2,1)S(1)}, u32[]{:S(2)}, u32[]{:S(2)}) %collective-permute-start.16) | collective-permute-done | bytes 262176 | tf_op jit(solution)/shard_map/ppermute | solution.py:38
  79.4 1.5 collective-permute-start.24
  80.9 1.4 collective-permute-start.27
  83.2 1.7 %collective-permute-start.21 = (bf16[2,512,256]{2,1,0:T(8,128)(2,1)S(1)}, bf16[2,512,256]{2,1,0:T(8,128)(2,1)S(1)}, u32[]{:S(2)}, u32[]{:S(2)}) collective-permute-start(bf16[2,512,256]{2,1,0:T(8,128)(2,1)S(1)} %get-tuple-element.72), channel_id=1, source_target_pairs={{0,4},{1,3},{2,6},{3,1},{4,0},{5,7},{6,2},{7,5},{8,12},{9,11},{10,... | collective-permute-start | bytes 1572872 | tf_op jit(solution)/shard_map/ppermute | solution.py:38
  85.0 3.8 %collective-permute-done.22 = bf16[2,512,256]{2,1,0:T(8,128)(2,1)S(1)} collective-permute-done((bf16[2,512,256]{2,1,0:T(8,128)(2,1)S(1)}, bf16[2,512,256]{2,1,0:T(8,128)(2,1)S(1)}, u32[]{:S(2)}, u32[]{:S(2)}) %collective-permute-start.22) | collective-permute-done | bytes 524320 | tf_op jit(solution)/shard_map/ppermute | solution.py:38
  90.2 3.5 %collective-permute-start.28 = (bf16[512,256]{1,0:T(8,128)(2,1)S(1)}, bf16[512,256]{1,0:T(8,128)(2,1)S(1)}, u32[]{:S(2)}, u32[]{:S(2)}) collective-permute-start(bf16[512,256]{1,0:T(8,128)(2,1)S(1)} %fusion.6), channel_id=1, source_target_pairs={{0,16},{1,17},{2,18},{3,19},{4,20},{5,21},{6,22},{7,23},{8,24},{9,... | collective-permute-start | bytes 786440 | tf_op jit(solution)/shard_map/ppermute | solution.py:38
  93.8 2.2 %collective-permute-done.25 = bf16[512,256]{1,0:T(8,128)(2,1)S(1)} collective-permute-done((bf16[512,256]{1,0:T(8,128)(2,1)S(1)}, bf16[512,256]{1,0:T(8,128)(2,1)S(1)}, u32[]{:S(2)}, u32[]{:S(2)}) %collective-permute-start.25) | collective-permute-done | bytes 262176 | tf_op jit(solution)/shard_map/ppermute | solution.py:38
  96.0 1.4 collective-permute-start.29
  97.6 1.6 collective-permute-start.26
  99.1 3.2 %collective-permute-done.28 = bf16[512,256]{1,0:T(8,128)(2,1)S(1)} collective-permute-done((bf16[512,256]{1,0:T(8,128)(2,1)S(1)}, bf16[512,256]{1,0:T(8,128)(2,1)S(1)}, u32[]{:S(2)}, u32[]{:S(2)}) %collective-permute-start.28) | collective-permute-done | bytes 262176 | tf_op jit(solution)/shard_map/ppermute | solution.py:38
  102.4 4.9 %collective-permute-done.29 = bf16[512,256]{1,0:T(8,128)(2,1)S(1)} collective-permute-done((bf16[512,256]{1,0:T(8,128)(2,1)S(1)}, bf16[512,256]{1,0:T(8,128)(2,1)S(1)}, u32[]{:S(2)}, u32[]{:S(2)}) %collective-permute-start.29) | collective-permute-done | bytes 262176 | tf_op jit(solution)/shard_map/ppermute | solution.py:38
  108.2 1.3 collective-permute-start.35
  110.8 2.1 %collective-permute-start.30 = (bf16[512,256]{1,0:T(8,128)(2,1)S(1)}, bf16[512,256]{1,0:T(8,128)(2,1)S(1)}, u32[]{:S(2)}, u32[]{:S(2)}) collective-permute-start(bf16[512,256]{1,0:T(8,128)(2,1)S(1)} %get-tuple-element.108.e0), channel_id=1, source_target_pairs={{0,16},{1,17},{2,18},{3,19},{4,20},{5,21},{6,22},{7,23},{8,24},{9,... | collective-permute-start | bytes 786440 | tf_op jit(solution)/shard_map/ppermute | solution.py:38
  112.9 2.9 %collective-permute-done.35.e1 = bf16[512,256]{1,0:T(8,128)(2,1)S(1)} collective-permute-done((bf16[512,256]{1,0:T(8,128)(2,1)S(1)}, bf16[512,256]{1,0:T(8,128)(2,1)S(1)}, u32[]{:S(2)}, u32[]{:S(2)}) %collective-permute-start.35) | collective-permute-done | bytes 262176 | tf_op jit(solution)/shard_map/ppermute | solution.py:38
  115.8 2.1 %collective-permute-start.37 = (bf16[512,256]{1,0:T(8,128)(2,1)S(1)}, bf16[512,256]{1,0:T(8,128)(2,1)S(1)}, u32[]{:S(2)}, u32[]{:S(2)}) collective-permute-start(bf16[512,256]{1,0:T(8,128)(2,1)S(1)} %collective-permute-done.35.e1), channel_id=1, source_target_pairs={{0,4},{1,3},{2,6},{3,1},{4,0},{5,7},{6,2},{7,5},{8,12},{9,11},{10,... | collective-permute-start | bytes 786440 | tf_op jit(solution)/shard_map/ppermute | solution.py:38
  117.8 3.7 %collective-permute-done.34.e0 = bf16[512,256]{1,0:T(8,128)(2,1)S(1)} collective-permute-done((bf16[512,256]{1,0:T(8,128)(2,1)S(1)}, bf16[512,256]{1,0:T(8,128)(2,1)S(1)}, u32[]{:S(2)}, u32[]{:S(2)}) %collective-permute-start.34) | collective-permute-done | bytes 262176 | tf_op jit(solution)/shard_map/ppermute | solution.py:38
  121.6 2.2 %collective-permute-done.30.e0 = bf16[512,256]{1,0:T(8,128)(2,1)S(1)} collective-permute-done((bf16[512,256]{1,0:T(8,128)(2,1)S(1)}, bf16[512,256]{1,0:T(8,128)(2,1)S(1)}, u32[]{:S(2)}, u32[]{:S(2)}) %collective-permute-start.30) | collective-permute-done | bytes 262176 | tf_op jit(solution)/shard_map/ppermute | solution.py:38
  124.2 1.6 collective-permute-start.42
  125.8 1.4 collective-permute-start.39
  128.5 3.9 %collective-permute-done.38.e1 = bf16[512,256]{1,0:T(8,128)(2,1)S(1)} collective-permute-done((bf16[512,256]{1,0:T(8,128)(2,1)S(1)}, bf16[512,256]{1,0:T(8,128)(2,1)S(1)}, u32[]{:S(2)}, u32[]{:S(2)}) %collective-permute-start.38) | collective-permute-done | bytes 262176 | tf_op jit(solution)/shard_map/ppermute | solution.py:38
  132.4 1.4 collective-permute-start.40
  134.3 1.8 %collective-permute-done.42.e1 = bf16[512,256]{1,0:T(8,128)(2,1)S(1)} collective-permute-done((bf16[512,256]{1,0:T(8,128)(2,1)S(1)}, bf16[512,256]{1,0:T(8,128)(2,1)S(1)}, u32[]{:S(2)}, u32[]{:S(2)}) %collective-permute-start.42) | collective-permute-done | bytes 262176 | tf_op jit(solution)/shard_map/ppermute | solution.py:38
  136.1 1.6 collective-permute-start.43
  138.8 1.4 collective-permute-start.33
  140.2 1.3 backward.5
  141.5 1.5 collective-permute-done.32.e1
  143.7 1.6 collective-permute-done.44.e3
  148.1 2.8 %collective-permute-done.41.e3 = bf16[512,256]{1,0:T(8,128)(2,1)S(1)} collective-permute-done((bf16[512,256]{1,0:T(8,128)(2,1)S(1)}, bf16[512,256]{1,0:T(8,128)(2,1)S(1)}, u32[]{:S(2)}, u32[]{:S(2)}) %collective-permute-start.41) | collective-permute-done | bytes 262176 | tf_op jit(solution)/shard_map/ppermute | solution.py:38
  150.9 1.3 backward.7
  155.2 2.2 %decoder_gradient.1 = f32[128,4096]{1,0:T(8,128)} custom-call(s32[16]{0:T(128)S(1)} %pad_add_fusion.5.order, f32[128,1024]{1,0:T(8,128)S(1)} %get-tuple-element.99.refs_0_, f32[128,1024]{1,0:T(8,128)S(1)} %get-tuple-element.100.refs_1_, f32[128,1024]{1,0:T(8,128)S(1)} %get-tuple-element.101.refs_2_, f32[128,1024]{1,0:T(8,128)S(1)} %get-tuple-element.102.refs_3_, ...), custom_call_target="tpu_custom_call" | custom-call | flops 524288 | bytes 5242880 | tf_op jit(solution)/shard_map/decoder_gradient/pallas_call | solution.py:135
  157.4 4.2 %encoder_gradient.1 = f32[4096,128]{1,0:T(8,128)} custom-call(s32[16]{0:T(128)S(1)} %pad_add_fusion.5.order, bf16[1024,512]{1,0:T(8,128)(2,1)S(1)} %get-tuple-element.66.refs_0_, bf16[1024,512]{1,0:T(8,128)(2,1)S(1)} %copy-done.4, bf16[1024,512]{1,0:T(8,128)(2,1)S(1)} %get-tuple-element.68.refs_2_, bf16[1024,512]{1,0:T(8,128)(2,1)S(1)} %get-tuple-element.69.refs_3_, ...), custom_call_target="tpu_custom_call" | custom-call | flops 1073741824 | bytes 10485760 | tf_op jit(solution)/shard_map/encoder_gradient/pallas_call | solution.py:135
  (131 shorter events, 40.3 us)
Async XLA Ops:
  2.3 8.7 %collective-permute-start.5 = (bf16[512,256]{1,0:T(8,128)(2,1)S(1)}, bf16[512,256]{1,0:T(8,128)(2,1)S(1)}, u32[]{:S(2)}, u32[]{:S(2)}) collective-permute-start(bf16[512,256]{1,0:T(8,128)(2,1)S(1)} %subtract_convert_fusion.x0), channel_id=1, source_target_pairs={{0,2},{1,5},{2,0},{3,7},{4,6},{5,1},{6,4},{7,3},{8,10},{9,13},{10,... | collective-permute-start | bytes 786440 | tf_op jit(solution)/shard_map/ppermute | solution.py:38
  5.3 14.5 %collective-permute-start = (bf16[512,256]{1,0:T(8,128)(2,1)S(1)}, bf16[512,256]{1,0:T(8,128)(2,1)}, u32[]{:S(2)}, u32[]{:S(2)}) collective-permute-start(bf16[512,256]{1,0:T(8,128)(2,1)S(1)} %subtract_convert_fusion.x0), channel_id=1, source_target_pairs={{0,16},{1,17},{2,18},{3,19},{4,20},{5,21},{6,22},{7,23},{8,24},{9,... | collective-permute-start | bytes 786440 | tf_op jit(solution)/shard_map/ppermute | solution.py:38
  7.9 12.4 %collective-permute-start.6 = (bf16[512,256]{1,0:T(8,128)(2,1)S(1)}, bf16[512,256]{1,0:T(8,128)(2,1)S(1)}, u32[]{:S(2)}, u32[]{:S(2)}) collective-permute-start(bf16[512,256]{1,0:T(8,128)(2,1)S(1)} %subtract_convert_fusion.x0), channel_id=1, source_target_pairs={{0,4},{1,3},{2,6},{3,1},{4,0},{5,7},{6,2},{7,5},{8,12},{9,11},{10,... | collective-permute-start | bytes 786440 | tf_op jit(solution)/shard_map/ppermute | solution.py:38
  9.4 11.8 %collective-permute-start.4 = (bf16[512,256]{1,0:T(8,128)(2,1)S(1)}, bf16[512,256]{1,0:T(8,128)(2,1)}, u32[]{:S(2)}, u32[]{:S(2)}) collective-permute-start(bf16[512,256]{1,0:T(8,128)(2,1)S(1)} %subtract_convert_fusion.x0), channel_id=1, source_target_pairs={{0,8},{1,9},{2,10},{3,11},{4,12},{5,13},{6,14},{7,15},{8,0},{9,1},... | collective-permute-start | bytes 786440 | tf_op jit(solution)/shard_map/ppermute | solution.py:38
  11.0 10.2 %collective-permute-start.7 = (bf16[512,256]{1,0:T(8,128)(2,1)S(1)}, bf16[512,256]{1,0:T(8,128)(2,1)S(1)}, u32[]{:S(2)}, u32[]{:S(2)}) collective-permute-start(bf16[512,256]{1,0:T(8,128)(2,1)S(1)} %collective-permute-done.5.x1), channel_id=1, source_target_pairs={{0,4},{1,3},{2,6},{3,1},{4,0},{5,7},{6,2},{7,5},{8,12},{9,11},{10,... | collective-permute-start | bytes 786440 | tf_op jit(solution)/shard_map/ppermute | solution.py:38
  19.8 12.5 %collective-permute-start.1 = (bf16[512,256]{1,0:T(8,128)(2,1)}, bf16[512,256]{1,0:T(8,128)(2,1)}, u32[]{:S(2)}, u32[]{:S(2)}) collective-permute-start(bf16[512,256]{1,0:T(8,128)(2,1)} %collective-permute-done.x0), channel_id=1, source_target_pairs={{0,8},{1,9},{2,10},{3,11},{4,12},{5,13},{6,14},{7,15},{8,0},{9,1},... | collective-permute-start | bytes 786440 | tf_op jit(solution)/shard_map/ppermute | solution.py:38
  21.9 9.3 %collective-permute-start.8 = (bf16[512,256]{1,0:T(8,128)(2,1)}, bf16[512,256]{1,0:T(8,128)(2,1)S(1)}, u32[]{:S(2)}, u32[]{:S(2)}) collective-permute-start(bf16[512,256]{1,0:T(8,128)(2,1)} %collective-permute-done.4.x0), channel_id=1, source_target_pairs={{0,2},{1,5},{2,0},{3,7},{4,6},{5,1},{6,4},{7,3},{8,10},{9,13},{10,... | collective-permute-start | bytes 786440 | tf_op jit(solution)/shard_map/ppermute | solution.py:38
  23.3 11.9 %collective-permute-start.12 = (bf16[512,256]{1,0:T(8,128)(2,1)}, bf16[512,256]{1,0:T(8,128)(2,1)}, u32[]{:S(2)}, u32[]{:S(2)}) collective-permute-start(bf16[512,256]{1,0:T(8,128)(2,1)} %collective-permute-done.x0), channel_id=1, source_target_pairs={{0,2},{1,5},{2,0},{3,7},{4,6},{5,1},{6,4},{7,3},{8,10},{9,13},{10,... | collective-permute-start | bytes 786440 | tf_op jit(solution)/shard_map/ppermute | solution.py:38
  24.0 11.7 %collective-permute-start.9 = (bf16[512,256]{1,0:T(8,128)(2,1)}, bf16[512,256]{1,0:T(8,128)(2,1)S(1)}, u32[]{:S(2)}, u32[]{:S(2)}) collective-permute-start(bf16[512,256]{1,0:T(8,128)(2,1)} %collective-permute-done.4.x0), channel_id=1, source_target_pairs={{0,4},{1,3},{2,6},{3,1},{4,0},{5,7},{6,2},{7,5},{8,12},{9,11},{10,... | collective-permute-start | bytes 786440 | tf_op jit(solution)/shard_map/ppermute | solution.py:38
  31.2 8.0 %collective-permute-start.10 = (bf16[512,256]{1,0:T(8,128)(2,1)S(1)}, bf16[512,256]{1,0:T(8,128)(2,1)S(1)}, u32[]{:S(2)}, u32[]{:S(2)}) collective-permute-start(bf16[512,256]{1,0:T(8,128)(2,1)S(1)} %collective-permute-done.8.x1), channel_id=1, source_target_pairs={{0,4},{1,3},{2,6},{3,1},{4,0},{5,7},{6,2},{7,5},{8,12},{9,11},{10,... | collective-permute-start | bytes 786440 | tf_op jit(solution)/shard_map/ppermute | solution.py:38
  32.3 10.6 %collective-permute-start.2 = (bf16[512,256]{1,0:T(8,128)(2,1)}, bf16[512,256]{1,0:T(8,128)(2,1)}, u32[]{:S(2)}, u32[]{:S(2)}) collective-permute-start(bf16[512,256]{1,0:T(8,128)(2,1)} %collective-permute-done.1.x0), channel_id=1, source_target_pairs={{0,2},{1,5},{2,0},{3,7},{4,6},{5,1},{6,4},{7,3},{8,10},{9,13},{10,... | collective-permute-start | bytes 786440 | tf_op jit(solution)/shard_map/ppermute | solution.py:38
  33.7 10.0 %collective-permute-start.13 = (bf16[512,256]{1,0:T(8,128)(2,1)}, bf16[512,256]{1,0:T(8,128)(2,1)}, u32[]{:S(2)}, u32[]{:S(2)}) collective-permute-start(bf16[512,256]{1,0:T(8,128)(2,1)} %collective-permute-done.x0), channel_id=1, source_target_pairs={{0,4},{1,3},{2,6},{3,1},{4,0},{5,7},{6,2},{7,5},{8,12},{9,11},{10,... | collective-permute-start | bytes 786440 | tf_op jit(solution)/shard_map/ppermute | solution.py:38
  35.2 9.6 %collective-permute-start.14 = (bf16[512,256]{1,0:T(8,128)(2,1)}, bf16[512,256]{1,0:T(8,128)(2,1)}, u32[]{:S(2)}, u32[]{:S(2)}) collective-permute-start(bf16[512,256]{1,0:T(8,128)(2,1)} %collective-permute-done.12.x1), channel_id=1, source_target_pairs={{0,4},{1,3},{2,6},{3,1},{4,0},{5,7},{6,2},{7,5},{8,12},{9,11},{10,... | collective-permute-start | bytes 786440 | tf_op jit(solution)/shard_map/ppermute | solution.py:38
  35.7 12.4 %collective-permute-start.3 = (bf16[512,256]{1,0:T(8,128)(2,1)}, bf16[512,256]{1,0:T(8,128)(2,1)}, u32[]{:S(2)}, u32[]{:S(2)}) collective-permute-start(bf16[512,256]{1,0:T(8,128)(2,1)} %collective-permute-done.1.x0), channel_id=1, source_target_pairs={{0,4},{1,3},{2,6},{3,1},{4,0},{5,7},{6,2},{7,5},{8,12},{9,11},{10,... | collective-permute-start | bytes 786440 | tf_op jit(solution)/shard_map/ppermute | solution.py:38
  42.9 7.6 %collective-permute-start.11 = (bf16[512,256]{1,0:T(8,128)(2,1)}, bf16[512,256]{1,0:T(8,128)(2,1)}, u32[]{:S(2)}, u32[]{:S(2)}) collective-permute-start(bf16[512,256]{1,0:T(8,128)(2,1)} %collective-permute-done.2.x1), channel_id=1, source_target_pairs={{0,4},{1,3},{2,6},{3,1},{4,0},{5,7},{6,2},{7,5},{8,12},{9,11},{10,... | collective-permute-start | bytes 786440 | tf_op jit(solution)/shard_map/ppermute | solution.py:38
  53.9 9.2 %collective-permute-start.15 = (bf16[2,512,256]{2,1,0:T(8,128)(2,1)S(1)}, bf16[2,512,256]{2,1,0:T(8,128)(2,1)S(1)}, u32[]{:S(2)}, u32[]{:S(2)}) collective-permute-start(bf16[2,512,256]{2,1,0:T(8,128)(2,1)S(1)} %get-tuple-element.65), channel_id=1, source_target_pairs={{0,4},{1,3},{2,6},{3,1},{4,0},{5,7},{6,2},{7,5},{8,12},{9,11},{10,... | collective-permute-start | bytes 1572872 | tf_op jit(solution)/shard_map/ppermute | solution.py:38
  54.4 24.9 %collective-permute-start.17 = (bf16[1024,512]{1,0:T(8,128)(2,1)S(1)}, bf16[1024,512]{1,0:T(8,128)(2,1)S(1)}, u32[]{:S(2)}, u32[]{:S(2)}) collective-permute-start(bf16[1024,512]{1,0:T(8,128)(2,1)S(1)} %get-tuple-element.66.refs_0_), channel_id=1, source_target_pairs={{0,1},{1,0},{2,3},{3,2},{4,5},{5,4},{6,7},{7,6},{8,9},{9,8},{10,11... | collective-permute-start | bytes 3145736 | tf_op jit(solution)/shard_map/ppermute | solution.py:54
  55.3 25.5 %collective-permute-start.19 = (bf16[1024,512]{1,0:T(8,128)(2,1)S(1)}, bf16[1024,512]{1,0:T(8,128)(2,1)S(1)}, u32[]{:S(2)}, u32[]{:S(2)}) collective-permute-start(bf16[1024,512]{1,0:T(8,128)(2,1)S(1)} %get-tuple-element.68.refs_2_), channel_id=1, source_target_pairs={{0,1},{1,0},{2,3},{3,2},{4,5},{5,4},{6,7},{7,6},{8,9},{9,8},{10,11... | collective-permute-start | bytes 3145736 | tf_op jit(solution)/shard_map/ppermute | solution.py:54
  55.4 26.9 %collective-permute-start.18 = (bf16[1024,512]{1,0:T(8,128)(2,1)S(1)}, bf16[1024,512]{1,0:T(8,128)(2,1)S(1)}, u32[]{:S(2)}, u32[]{:S(2)}) collective-permute-start(bf16[1024,512]{1,0:T(8,128)(2,1)S(1)} %copy-done.4), channel_id=1, source_target_pairs={{0,1},{1,0},{2,3},{3,2},{4,5},{5,4},{6,7},{7,6},{8,9},{9,8},{10,11... | collective-permute-start | bytes 3145736 | tf_op jit(solution)/shard_map/ppermute | solution.py:54
  55.9 26.4 %collective-permute-start.20 = (bf16[1024,512]{1,0:T(8,128)(2,1)S(1)}, bf16[1024,512]{1,0:T(8,128)(2,1)S(1)}, u32[]{:S(2)}, u32[]{:S(2)}) collective-permute-start(bf16[1024,512]{1,0:T(8,128)(2,1)S(1)} %get-tuple-element.69.refs_3_), channel_id=1, source_target_pairs={{0,1},{1,0},{2,3},{3,2},{4,5},{5,4},{6,7},{7,6},{8,9},{9,8},{10,11... | collective-permute-start | bytes 3145736 | tf_op jit(solution)/shard_map/ppermute | solution.py:54
  63.1 9.2 %collective-permute-start.23 = (bf16[2,512,256]{2,1,0:T(8,128)(2,1)S(1)}, bf16[2,512,256]{2,1,0:T(8,128)(2,1)S(1)}, u32[]{:S(2)}, u32[]{:S(2)}) collective-permute-start(bf16[2,512,256]{2,1,0:T(8,128)(2,1)S(1)} %get-tuple-element.77), channel_id=1, source_target_pairs={{0,4},{1,3},{2,6},{3,1},{4,0},{5,7},{6,2},{7,5},{8,12},{9,11},{10,... | collective-permute-start | bytes 1572872 | tf_op jit(solution)/shard_map/ppermute | solution.py:38
  72.3 6.4 %collective-permute-start.16 = (bf16[512,256]{1,0:T(8,128)(2,1)S(1)}, bf16[512,256]{1,0:T(8,128)(2,1)S(1)}, u32[]{:S(2)}, u32[]{:S(2)}) collective-permute-start(bf16[512,256]{1,0:T(8,128)(2,1)S(1)} %fusion.12), channel_id=1, source_target_pairs={{0,2},{1,5},{2,0},{3,7},{4,6},{5,1},{6,4},{7,3},{8,10},{9,13},{10,... | collective-permute-start | bytes 786440 | tf_op jit(solution)/shard_map/ppermute | solution.py:38
  78.7 10.2 %collective-permute-start.22 = (bf16[2,512,256]{2,1,0:T(8,128)(2,1)S(1)}, bf16[2,512,256]{2,1,0:T(8,128)(2,1)S(1)}, u32[]{:S(2)}, u32[]{:S(2)}) collective-permute-start(bf16[2,512,256]{2,1,0:T(8,128)(2,1)S(1)} %get-tuple-element.75), channel_id=1, source_target_pairs={{0,4},{1,3},{2,6},{3,1},{4,0},{5,7},{6,2},{7,5},{8,12},{9,11},{10,... | collective-permute-start | bytes 1572872 | tf_op jit(solution)/shard_map/ppermute | solution.py:38
  79.4 9.6 %collective-permute-start.24 = (bf16[512,256]{1,0:T(8,128)(2,1)S(1)}, bf16[512,256]{1,0:T(8,128)(2,1)S(1)}, u32[]{:S(2)}, u32[]{:S(2)}) collective-permute-start(bf16[512,256]{1,0:T(8,128)(2,1)S(1)} %fusion.15), channel_id=1, source_target_pairs={{0,2},{1,5},{2,0},{3,7},{4,6},{5,1},{6,4},{7,3},{8,10},{9,13},{10,... | collective-permute-start | bytes 786440 | tf_op jit(solution)/shard_map/ppermute | solution.py:38
  80.9 9.2 %collective-permute-start.27 = (bf16[512,256]{1,0:T(8,128)(2,1)S(1)}, bf16[512,256]{1,0:T(8,128)(2,1)S(1)}, u32[]{:S(2)}, u32[]{:S(2)}) collective-permute-start(bf16[512,256]{1,0:T(8,128)(2,1)S(1)} %fusion.3), channel_id=1, source_target_pairs={{0,8},{1,9},{2,10},{3,11},{4,12},{5,13},{6,14},{7,15},{8,0},{9,1},... | collective-permute-start | bytes 786440 | tf_op jit(solution)/shard_map/ppermute | solution.py:38
  83.2 14.2 %collective-permute-start.21 = (bf16[2,512,256]{2,1,0:T(8,128)(2,1)S(1)}, bf16[2,512,256]{2,1,0:T(8,128)(2,1)S(1)}, u32[]{:S(2)}, u32[]{:S(2)}) collective-permute-start(bf16[2,512,256]{2,1,0:T(8,128)(2,1)S(1)} %get-tuple-element.72), channel_id=1, source_target_pairs={{0,4},{1,3},{2,6},{3,1},{4,0},{5,7},{6,2},{7,5},{8,12},{9,11},{10,... | collective-permute-start | bytes 1572872 | tf_op jit(solution)/shard_map/ppermute | solution.py:38
  89.0 7.0 %collective-permute-start.25 = (bf16[512,256]{1,0:T(8,128)(2,1)S(1)}, bf16[512,256]{1,0:T(8,128)(2,1)S(1)}, u32[]{:S(2)}, u32[]{:S(2)}) collective-permute-start(bf16[512,256]{1,0:T(8,128)(2,1)S(1)} %fusion.14), channel_id=1, source_target_pairs={{0,2},{1,5},{2,0},{3,7},{4,6},{5,1},{6,4},{7,3},{8,10},{9,13},{10,... | collective-permute-start | bytes 786440 | tf_op jit(solution)/shard_map/ppermute | solution.py:38
  90.2 12.1 %collective-permute-start.28 = (bf16[512,256]{1,0:T(8,128)(2,1)S(1)}, bf16[512,256]{1,0:T(8,128)(2,1)S(1)}, u32[]{:S(2)}, u32[]{:S(2)}) collective-permute-start(bf16[512,256]{1,0:T(8,128)(2,1)S(1)} %fusion.6), channel_id=1, source_target_pairs={{0,16},{1,17},{2,18},{3,19},{4,20},{5,21},{6,22},{7,23},{8,24},{9,... | collective-permute-start | bytes 786440 | tf_op jit(solution)/shard_map/ppermute | solution.py:38
  96.0 11.2 %collective-permute-start.29 = (bf16[512,256]{1,0:T(8,128)(2,1)S(1)}, bf16[512,256]{1,0:T(8,128)(2,1)S(1)}, u32[]{:S(2)}, u32[]{:S(2)}) collective-permute-start(bf16[512,256]{1,0:T(8,128)(2,1)S(1)} %fusion.1), channel_id=1, source_target_pairs={{0,8},{1,9},{2,10},{3,11},{4,12},{5,13},{6,14},{7,15},{8,0},{9,1},... | collective-permute-start | bytes 786440 | tf_op jit(solution)/shard_map/ppermute | solution.py:38
  97.6 9.7 %collective-permute-start.26 = (bf16[512,256]{1,0:T(8,128)(2,1)S(1)}, bf16[512,256]{1,0:T(8,128)(2,1)S(1)}, u32[]{:S(2)}, u32[]{:S(2)}) collective-permute-start(bf16[512,256]{1,0:T(8,128)(2,1)S(1)} %fusion.13), channel_id=1, source_target_pairs={{0,2},{1,5},{2,0},{3,7},{4,6},{5,1},{6,4},{7,3},{8,10},{9,13},{10,... | collective-permute-start | bytes 786440 | tf_op jit(solution)/shard_map/ppermute | solution.py:38
  108.2 7.5 %collective-permute-start.35 = (bf16[512,256]{1,0:T(8,128)(2,1)S(1)}, bf16[512,256]{1,0:T(8,128)(2,1)S(1)}, u32[]{:S(2)}, u32[]{:S(2)}) collective-permute-start(bf16[512,256]{1,0:T(8,128)(2,1)S(1)} %get-tuple-element.108.e0), channel_id=1, source_target_pairs={{0,2},{1,5},{2,0},{3,7},{4,6},{5,1},{6,4},{7,3},{8,10},{9,13},{10,... | collective-permute-start | bytes 786440 | tf_op jit(solution)/shard_map/ppermute | solution.py:38
  109.6 8.3 %collective-permute-start.36 = (bf16[512,256]{1,0:T(8,128)(2,1)S(1)}, bf16[512,256]{1,0:T(8,128)(2,1)S(1)}, u32[]{:S(2)}, u32[]{:S(2)}) collective-permute-start(bf16[512,256]{1,0:T(8,128)(2,1)S(1)} %get-tuple-element.108.e0), channel_id=1, source_target_pairs={{0,4},{1,3},{2,6},{3,1},{4,0},{5,7},{6,2},{7,5},{8,12},{9,11},{10,... | collective-permute-start | bytes 786440 | tf_op jit(solution)/shard_map/ppermute | solution.py:38
  110.8 10.8 %collective-permute-start.34 = (bf16[512,256]{1,0:T(8,128)(2,1)S(1)}, bf16[512,256]{1,0:T(8,128)(2,1)S(1)}, u32[]{:S(2)}, u32[]{:S(2)}) collective-permute-start(bf16[512,256]{1,0:T(8,128)(2,1)S(1)} %get-tuple-element.108.e0), channel_id=1, source_target_pairs={{0,8},{1,9},{2,10},{3,11},{4,12},{5,13},{6,14},{7,15},{8,0},{9,1},... | collective-permute-start | bytes 786440 | tf_op jit(solution)/shard_map/ppermute | solution.py:38
  110.8 13.0 %collective-permute-start.30 = (bf16[512,256]{1,0:T(8,128)(2,1)S(1)}, bf16[512,256]{1,0:T(8,128)(2,1)S(1)}, u32[]{:S(2)}, u32[]{:S(2)}) collective-permute-start(bf16[512,256]{1,0:T(8,128)(2,1)S(1)} %get-tuple-element.108.e0), channel_id=1, source_target_pairs={{0,16},{1,17},{2,18},{3,19},{4,20},{5,21},{6,22},{7,23},{8,24},{9,... | collective-permute-start | bytes 786440 | tf_op jit(solution)/shard_map/ppermute | solution.py:38
  115.8 8.0 %collective-permute-start.37 = (bf16[512,256]{1,0:T(8,128)(2,1)S(1)}, bf16[512,256]{1,0:T(8,128)(2,1)S(1)}, u32[]{:S(2)}, u32[]{:S(2)}) collective-permute-start(bf16[512,256]{1,0:T(8,128)(2,1)S(1)} %collective-permute-done.35.e1), channel_id=1, source_target_pairs={{0,4},{1,3},{2,6},{3,1},{4,0},{5,7},{6,2},{7,5},{8,12},{9,11},{10,... | collective-permute-start | bytes 786440 | tf_op jit(solution)/shard_map/ppermute | solution.py:38
  123.8 8.7 %collective-permute-start.38 = (bf16[512,256]{1,0:T(8,128)(2,1)S(1)}, bf16[512,256]{1,0:T(8,128)(2,1)S(1)}, u32[]{:S(2)}, u32[]{:S(2)}) collective-permute-start(bf16[512,256]{1,0:T(8,128)(2,1)S(1)} %collective-permute-done.34.e0), channel_id=1, source_target_pairs={{0,2},{1,5},{2,0},{3,7},{4,6},{5,1},{6,4},{7,3},{8,10},{9,13},{10,... | collective-permute-start | bytes 786440 | tf_op jit(solution)/shard_map/ppermute | solution.py:38
  124.2 9.7 %collective-permute-start.31 = (bf16[512,256]{1,0:T(8,128)(2,1)S(1)}, bf16[512,256]{1,0:T(8,128)(2,1)S(1)}, u32[]{:S(2)}, u32[]{:S(2)}) collective-permute-start(bf16[512,256]{1,0:T(8,128)(2,1)S(1)} %collective-permute-done.30.e0), channel_id=1, source_target_pairs={{0,8},{1,9},{2,10},{3,11},{4,12},{5,13},{6,14},{7,15},{8,0},{9,1},... | collective-permute-start | bytes 786440 | tf_op jit(solution)/shard_map/ppermute | solution.py:38
  124.2 11.9 %collective-permute-start.42 = (bf16[512,256]{1,0:T(8,128)(2,1)S(1)}, bf16[512,256]{1,0:T(8,128)(2,1)S(1)}, u32[]{:S(2)}, u32[]{:S(2)}) collective-permute-start(bf16[512,256]{1,0:T(8,128)(2,1)S(1)} %collective-permute-done.30.e0), channel_id=1, source_target_pairs={{0,2},{1,5},{2,0},{3,7},{4,6},{5,1},{6,4},{7,3},{8,10},{9,13},{10,... | collective-permute-start | bytes 786440 | tf_op jit(solution)/shard_map/ppermute | solution.py:38
  125.8 11.9 %collective-permute-start.39 = (bf16[512,256]{1,0:T(8,128)(2,1)S(1)}, bf16[512,256]{1,0:T(8,128)(2,1)S(1)}, u32[]{:S(2)}, u32[]{:S(2)}) collective-permute-start(bf16[512,256]{1,0:T(8,128)(2,1)S(1)} %collective-permute-done.34.e0), channel_id=1, source_target_pairs={{0,4},{1,3},{2,6},{3,1},{4,0},{5,7},{6,2},{7,5},{8,12},{9,11},{10,... | collective-permute-start | bytes 786440 | tf_op jit(solution)/shard_map/ppermute | solution.py:38
  132.4 6.4 %collective-permute-start.40 = (bf16[512,256]{1,0:T(8,128)(2,1)S(1)}, bf16[512,256]{1,0:T(8,128)(2,1)S(1)}, u32[]{:S(2)}, u32[]{:S(2)}) collective-permute-start(bf16[512,256]{1,0:T(8,128)(2,1)S(1)} %collective-permute-done.38.e1), channel_id=1, source_target_pairs={{0,4},{1,3},{2,6},{3,1},{4,0},{5,7},{6,2},{7,5},{8,12},{9,11},{10,... | collective-permute-start | bytes 786440 | tf_op jit(solution)/shard_map/ppermute | solution.py:38
  133.8 9.2 %collective-permute-start.32 = (bf16[512,256]{1,0:T(8,128)(2,1)S(1)}, bf16[512,256]{1,0:T(8,128)(2,1)S(1)}, u32[]{:S(2)}, u32[]{:S(2)}) collective-permute-start(bf16[512,256]{1,0:T(8,128)(2,1)S(1)} %collective-permute-done.31.e0), channel_id=1, source_target_pairs={{0,2},{1,5},{2,0},{3,7},{4,6},{5,1},{6,4},{7,3},{8,10},{9,13},{10,... | collective-permute-start | bytes 786440 | tf_op jit(solution)/shard_map/ppermute | solution.py:38
  134.3 8.8 %collective-permute-start.45 = (bf16[128,1024]{1,0:T(8,128)(2,1)S(1)}, bf16[128,1024]{1,0:T(8,128)(2,1)S(1)}, u32[]{:S(2)}, u32[]{:S(2)}) collective-permute-start(bf16[128,1024]{1,0:T(8,128)(2,1)S(1)} %get-tuple-element.90), channel_id=1, source_target_pairs={{0,1},{1,0},{2,3},{3,2},{4,5},{5,4},{6,7},{7,6},{8,9},{9,8},{10,11... | collective-permute-start | bytes 786440 | tf_op jit(solution)/shard_map/ppermute | solution.py:54
  136.1 7.6 %collective-permute-start.43 = (bf16[512,256]{1,0:T(8,128)(2,1)S(1)}, bf16[512,256]{1,0:T(8,128)(2,1)S(1)}, u32[]{:S(2)}, u32[]{:S(2)}) collective-permute-start(bf16[512,256]{1,0:T(8,128)(2,1)S(1)} %collective-permute-done.30.e0), channel_id=1, source_target_pairs={{0,4},{1,3},{2,6},{3,1},{4,0},{5,7},{6,2},{7,5},{8,12},{9,11},{10,... | collective-permute-start | bytes 786440 | tf_op jit(solution)/shard_map/ppermute | solution.py:38
  137.7 7.6 %collective-permute-start.44 = (bf16[512,256]{1,0:T(8,128)(2,1)S(1)}, bf16[512,256]{1,0:T(8,128)(2,1)S(1)}, u32[]{:S(2)}, u32[]{:S(2)}) collective-permute-start(bf16[512,256]{1,0:T(8,128)(2,1)S(1)} %collective-permute-done.42.e1), channel_id=1, source_target_pairs={{0,4},{1,3},{2,6},{3,1},{4,0},{5,7},{6,2},{7,5},{8,12},{9,11},{10,... | collective-permute-start | bytes 786440 | tf_op jit(solution)/shard_map/ppermute | solution.py:38
  138.8 9.2 %collective-permute-start.33 = (bf16[512,256]{1,0:T(8,128)(2,1)S(1)}, bf16[512,256]{1,0:T(8,128)(2,1)S(1)}, u32[]{:S(2)}, u32[]{:S(2)}) collective-permute-start(bf16[512,256]{1,0:T(8,128)(2,1)S(1)} %collective-permute-done.31.e0), channel_id=1, source_target_pairs={{0,4},{1,3},{2,6},{3,1},{4,0},{5,7},{6,2},{7,5},{8,12},{9,11},{10,... | collective-permute-start | bytes 786440 | tf_op jit(solution)/shard_map/ppermute | solution.py:38
  143.0 7.8 %collective-permute-start.41 = (bf16[512,256]{1,0:T(8,128)(2,1)S(1)}, bf16[512,256]{1,0:T(8,128)(2,1)S(1)}, u32[]{:S(2)}, u32[]{:S(2)}) collective-permute-start(bf16[512,256]{1,0:T(8,128)(2,1)S(1)} %collective-permute-done.32.e1), channel_id=1, source_target_pairs={{0,4},{1,3},{2,6},{3,1},{4,0},{5,7},{6,2},{7,5},{8,12},{9,11},{10,... | collective-permute-start | bytes 786440 | tf_op jit(solution)/shard_map/ppermute | solution.py:38
  146.5 8.6 %collective-permute-start.48 = (bf16[128,1024]{1,0:T(8,128)(2,1)S(1)}, bf16[128,1024]{1,0:T(8,128)(2,1)S(1)}, u32[]{:S(2)}, u32[]{:S(2)}) collective-permute-start(bf16[128,1024]{1,0:T(8,128)(2,1)S(1)} %get-tuple-element.103), channel_id=1, source_target_pairs={{0,1},{1,0},{2,3},{3,2},{4,5},{5,4},{6,7},{7,6},{8,9},{9,8},{10,11... | collective-permute-start | bytes 786440 | tf_op jit(solution)/shard_map/ppermute | solution.py:54
  152.7 4.8 %collective-permute-start.50 = (bf16[512,128]{1,0:T(8,128)(2,1)S(1)}, bf16[512,128]{1,0:T(8,128)(2,1)S(1)}, u32[]{:S(2)}, u32[]{:S(2)}) collective-permute-start(bf16[512,128]{1,0:T(8,128)(2,1)S(1)} %get-tuple-element.106), channel_id=1, source_target_pairs={{0,1},{1,0},{2,3},{3,2},{4,5},{5,4},{6,7},{7,6},{8,9},{9,8},{10,11... | collective-permute-start | bytes 393224 | tf_op jit(solution)/shard_map/ppermute | solution.py:54
  (21 other events, 85.6 us)

commit v3 on v2

v3 whole, which is shorter than its diff:
```python
import functools

import jax
import jax.numpy as jnp
from jax import lax
from jax.experimental import pallas as pl
from jax.experimental.pallas import tpu as pltpu
from jax.sharding import PartitionSpec as P


F32, BF16 = jnp.float32, jnp.bfloat16
VMEM_BYTES = 24 * 1024 * 1024
LANES = 128


class Grid:
    def __init__(self, lat, dp):
        self.lat, self.dp, self.slots = lat, dp, lat // 4
        self.me = lax.axis_index("lat")
        self.rank = lax.axis_index("dp")
        first = jnp.where(self.rank % 2 == 0, 1, 2)
        members = jnp.stack([jnp.zeros_like(first), first, 3 - first, jnp.full_like(first, 3)])
        self.across = (0, 2, 1, 3) if dp == 2 else (0, 1, 2, 3)
        side = self.rank // (dp // 2)
        orders = [self.me ^ (4 * s + members) for s in range(self.slots)]
        self.order = [jnp.append(o, side).astype(jnp.int32) for o in orders]
        self.every = jnp.concatenate(orders).astype(jnp.int32)

    def swap(self, x, even, odd):
        pairs = []
        for i in range(self.lat):
            for d in range(self.dp):
                pairs.append((i * self.dp + d, (i ^ (even if d % 2 == 0 else odd)) * self.dp + d))
        return lax.ppermute(x, ("lat", "dp"), pairs)

    def swap_first(self, x):
        return self.swap(x, 1, 2)

    def swap_second(self, x):
        return self.swap(x, 2, 1)

    def swap_plane(self, x, bit):
        return self.swap(x, 4 * bit, 4 * bit)

    def swap_core(self, x):
        pairs = []
        for i in range(self.lat):
            for d in range(self.dp):
                pairs.append((i * self.dp + d, i * self.dp + (d ^ self.dp // 2)))
        return lax.ppermute(x, ("lat", "dp"), pairs)

    def spread(self, x, axis):
        h = self.dp // 4
        while h >= 1:
            bit = self.rank // h % 2
            size = x.shape[axis] // 2
            mine = lax.dynamic_slice_in_dim(x, bit * size, size, axis)
            other = lax.dynamic_slice_in_dim(x, (1 - bit) * size, size, axis)
            x = mine + lax.ppermute(other, "dp", [(d, d ^ h) for d in range(self.dp)])
            h //= 2
        return x

    def gather(self, own):
        column = [own]
        for s in range(1, self.slots):
            column.append(self.swap_plane(column[s & (s - 1)], s & -s))
        seconds = []
        for s, block in enumerate(column):
            seconds.append(self.swap_plane(seconds[-1], 1) if s % 2 else self.swap_first(block))
        return [(b, a, self.swap_second(b), self.swap_second(a)) for b, a in zip(column, seconds)]

    def scatter_sum(self, part):
        column = [None] * self.slots
        earlier = {}
        last = self.slots - 1
        moved = None
        for s in reversed(range(self.slots)):
            keep, send = part(s, earlier.get(s))
            there = self.swap_second(send)
            pair = keep + there.astype(F32)
            if s == last > 1:
                other = self.swap_plane(pair[1].astype(BF16), 1)
                moved = (self.swap_plane(pair[0].astype(BF16), 1), other)
                earlier = {s - 2: there, s - 3: other}
                continue
            mine, other = pair[0], pair[1]
            if s == last - 1:
                mine, other = mine + moved[0].astype(F32), other + moved[1].astype(F32)
            got = self.swap_first(other.astype(BF16))
            column[s] = mine + got.astype(F32)
        for s in reversed(range(1, self.slots)):
            if column[s] is not None:
                t = s & (s - 1)
                send = column[s].astype(BF16)
                column[t] = column[t] + self.swap_plane(send, s & -s).astype(F32)
        return column[0]


def plain(width):
    return width % LANES != 0


def taken(x, index, width, axis):
    return lax.dynamic_slice_in_dim(x, index * width, width, axis)


def gate_of(active, lats):
    blocks, rows = active.shape
    turned = active.astype(F32).T
    return jnp.concatenate(
        [jnp.broadcast_to(turned[:, b:b + 1], (rows, lats // blocks)) for b in range(blocks)], axis=1
    )


def activate(total, active):
    positive = jnp.maximum(total, 0.0)
    gated = positive * gate_of(active, total.shape[1])
    return (positive * gated).astype(BF16), 2.0 * gated


def outer(a, b):
    return lax.dot_general(a, b, (((0,), (0,)), ((), ())), preferred_element_type=F32)


def call(body, order, operands, in_specs, out_shape, out_specs, flops, moved, name, scratch=()):
    return pl.pallas_call(
        body,
        grid_spec=pltpu.PrefetchScalarGridSpec(
            num_scalar_prefetch=1, grid=(1,), in_specs=in_specs, out_specs=out_specs, scratch_shapes=scratch
        ),
        out_shape=out_shape,
        compiler_params=pltpu.CompilerParams(vmem_limit_bytes=VMEM_BYTES),
        cost_estimate=pl.CostEstimate(flops=flops, bytes_accessed=moved, transcendentals=0),
        name=name,
    )(order, *operands)


ANYWHERE = pl.BlockSpec(memory_space=pl.ANY)
FAR = pl.BlockSpec(memory_space=pltpu.HBM)


def whole(shape):
    return pl.BlockSpec(shape, lambda i, order: (0,) * len(shape))


def encode_body(count, last, order, *refs):
    xs, (weight, start, *refs) = refs[:count], refs[count:]
    width = xs[0].shape[1]
    if last:
        active, act, slope, held, rows_of, begun, gates, sems = refs
        pairs = [(active, gates)]
    else:
        total_out, held, rows_of, begun, sems = refs
        pairs = []
    pairs.append((start, begun))
    for b in range(count):
        at = pl.ds(pl.multiple_of(order[b] * width, width), width)
        pairs += [(xs[b], held.at[b]), (weight.at[at], rows_of.at[b])]
    loads = [pltpu.make_async_copy(a, b, sems.at[n]) for n, (a, b) in enumerate(pairs)]
    for load in loads:
        load.start()
    for load in loads[:-2 * count]:
        load.wait()
    total = begun[...]
    for b in range(count):
        loads[2 * (b - count)].wait()
        loads[2 * (b - count) + 1].wait()
        total = total + jnp.dot(held[b], rows_of[b], preferred_element_type=F32)
    if last:
        act[...], slope[...] = activate(total, gates[...])
    else:
        total_out[...] = total


def encode(order, blocks, weight, start, active):
    count = len(blocks)
    rows, width = blocks[0].shape
    lats = weight.shape[1]
    last = active is not None
    if plain(width):
        total = start
        for b in range(count):
            total = total + jnp.dot(blocks[b], taken(weight, order[b], width, 0), preferred_element_type=F32)
        return activate(total, active) if last else [total]
    out = [jax.ShapeDtypeStruct((rows, lats), F32)]
    operands = blocks + [weight, start]
    scratch = [pltpu.VMEM((count, rows, width), BF16), pltpu.VMEM((count, width, lats), BF16)]
    scratch.append(pltpu.VMEM(start.shape, F32))
    if last:
        out = [jax.ShapeDtypeStruct((rows, lats), BF16)] + out
        operands.append(active)
        scratch.append(pltpu.VMEM(active.shape, active.dtype))
    scratch.append(pltpu.SemaphoreType.DMA((2 * count + 2,)))
    return call(
        functools.partial(encode_body, count, last), order, operands, [FAR] * len(operands), out,
        [whole(o.shape) for o in out],
        2 * count * rows * width * lats, 2 * count * width * (rows + lats) + 8 * rows * lats, "encode", scratch,
    )


def bring_body(order, x, out, sem):
    copy = pltpu.make_async_copy(x, out, sem)
    copy.start()
    copy.wait()


def bring(order, x):
    return call(
        bring_body, order, [x], [FAR], jax.ShapeDtypeStruct(x.shape, x.dtype),
        pl.BlockSpec(memory_space=pltpu.VMEM), 0, 4 * x.size, "bring", [pltpu.SemaphoreType.DMA],
    )


def turn_body(count, order, *refs):
    xs, (out, held, turned, in_sems, out_sems) = refs[:count], refs[count:]
    width = held.shape[2]
    loads = [pltpu.make_async_copy(xs[b], held.at[b], in_sems.at[b]) for b in range(count)]
    for load in loads:
        load.start()
    stores = []
    for b in range(count):
        loads[b].wait()
        turned[b] = held[b].T
        stores.append(pltpu.make_async_copy(turned.at[b], out.at[b], out_sems.at[b]))
        stores[-1].start()
    for store in stores:
        store.wait()


def turn(order, blocks):
    count = len(blocks)
    rows, width = blocks[0].shape
    if plain(width):
        return jnp.stack([x.T for x in blocks])
    shape = (count, width, rows)
    return call(
        functools.partial(turn_body, count), order, blocks, [FAR] * count, jax.ShapeDtypeStruct(shape, BF16), FAR,
        0, 4 * count * rows * width, "turn",
        [pltpu.VMEM((count, rows, width), BF16), pltpu.VMEM(shape, BF16),
         pltpu.SemaphoreType.DMA((count,)), pltpu.SemaphoreType.DMA((count,))],
    )


def column_specs(lats, width):
    return [pl.BlockSpec((lats, width), functools.partial(lambda m, i, order: (0, order[m]), m)) for m in range(4)]


def decode_body(order, act, w0, w1, w2, w3, *rest):
    *_, keep, send = rest
    a = act[...]
    keep[0] = jnp.dot(a, w0[...], preferred_element_type=F32)
    keep[1] = jnp.dot(a, w1[...], preferred_element_type=F32)
    send[0] = jnp.dot(a, w2[...], preferred_element_type=F32).astype(BF16)
    send[1] = jnp.dot(a, w3[...], preferred_element_type=F32).astype(BF16)


def decode(order, act, weight, width, earlier):
    rows, lats = act.shape
    if plain(width):
        terms = [jnp.dot(act, taken(weight, order[m], width, 1), preferred_element_type=F32) for m in range(4)]
        return jnp.stack(terms[:2]), jnp.stack(terms[2:]).astype(BF16)
    out = [jax.ShapeDtypeStruct((2, rows, width), F32), jax.ShapeDtypeStruct((2, rows, width), BF16)]
    return call(
        decode_body, order, [act] + [weight] * 4 + earlier,
        [whole(act.shape)] + column_specs(lats, width) + [ANYWHERE] * len(earlier), out,
        [whole((2, rows, width))] * 2, 8 * rows * width * lats, 12 * rows * width + 8 * width * lats, "decode",
    )


def backward_body(last, across, order, act, e0, e1, e2, e3, w0, w1, w2, w3, dact, squares, *rest):
    rows, width = e0.shape
    half = act.shape[1] // 2
    total = dact[...]
    square = squares[...]
    if last:
        slope, grad_keep, grad_send, dpre_keep, dpre_send, next_squares = rest
    else:
        grad_keep, grad_send, next_dact, next_squares = rest
    side = order[order.shape[0] - 1]
    mine_at = pl.ds(pl.multiple_of(side * half, half), half)
    other_at = pl.ds(pl.multiple_of((1 - side) * half, half), half)
    mine, other = act[:, mine_at], act[:, other_at]
    for m, (e, w) in enumerate(((e0, w0), (e1, w1), (e2, w2), (e3, w3))):
        block = e[...]
        total = total + lax.dot_general(block, w[...], (((1,), (1,)), ((), ())), preferred_element_type=F32)
        wide = block.astype(F32)
        square = square + jnp.sum((wide * wide).reshape(rows // 8, 8, width), axis=0)
        at, there = pl.ds(m * width, width), pl.ds(across[m] * width, width)
        grad_keep[:, at] = lax.dot_general(mine, block, (((0,), (0,)), ((), ())), preferred_element_type=F32)
        grad_send[:, there] = lax.dot_general(
            other, block, (((0,), (0,)), ((), ())), preferred_element_type=F32
        ).astype(BF16)
    if last:
        next_squares[...] = jnp.broadcast_to(jnp.sum(square, axis=(0, 1), keepdims=True), next_squares.shape)
        slope[...] = total * slope[...]
        dpre_keep[...] = slope[:, mine_at].astype(BF16)
        dpre_send[...] = slope[:, other_at].astype(BF16)
    else:
        next_dact[...] = total
        next_squares[...] = square


def backward(order, across, act, blocks, weight, dact, squares, slope):
    rows, width = blocks[0].shape
    lats = act.shape[1]
    last = slope is not None
    if plain(width):
        half, side = lats // 2, order[-1]
        mine, other = taken(act, side, half, 1), taken(act, 1 - side, half, 1)
        for e, m in zip(blocks, range(4)):
            w = taken(weight, order[m], width, 1)
            dact = dact + lax.dot_general(e, w, (((1,), (1,)), ((), ())), preferred_element_type=F32)
            squares = squares + jnp.sum(e.astype(F32) ** 2) / squares.size
        keep = jnp.concatenate([outer(mine, e) for e in blocks], axis=1)
        send = jnp.concatenate([outer(other, blocks[m]) for m in across], axis=1).astype(BF16)
        if not last:
            return keep, send, dact, squares
        dpre = (dact * slope).astype(BF16)
        squares = jnp.broadcast_to(jnp.sum(squares), (8, LANES))
        return keep, send, taken(dpre, side, half, 1), taken(dpre, 1 - side, half, 1), squares
    operands = [act] + list(blocks) + [weight] * 4 + [dact, squares]
    specs = [whole(act.shape)] + [whole((rows, width))] * 4 + column_specs(lats, width)
    specs += [whole(dact.shape), whole(squares.shape)]
    if last:
        operands.append(slope)
        specs.append(whole(slope.shape))
    out = [
        jax.ShapeDtypeStruct((lats // 2, 4 * width), F32),
        jax.ShapeDtypeStruct((lats // 2, 4 * width), BF16),
    ]
    if last:
        out += [jax.ShapeDtypeStruct((rows, lats // 2), BF16)] * 2
    else:
        out.append(jax.ShapeDtypeStruct((rows, lats), F32))
    out.append(jax.ShapeDtypeStruct((8, 128) if last else squares.shape, F32))
    return call(
        functools.partial(backward_body, last, across), order, operands, specs, out, [whole(o.shape) for o in out],
        16 * rows * width * lats, 8 * rows * width + 20 * width * lats + 8 * rows * lats, "backward",
    )


def decoder_gradient_body(slots, width, scale, order, *refs):
    keeps, gots, (square, square_got, out, mean) = refs[:slots], refs[slots:2 * slots], refs[2 * slots:]
    mean[...] = (square[0:1, 0:1] + square_got[0:1, 0:1]) * scale
    for s in range(slots):
        for m in range(4):
            at = pl.ds(m * width, width)
            there = pl.ds(pl.multiple_of(order[4 * s + m] * width, width), width)
            out[:, there] = keeps[s][:, at] + gots[s][:, at].astype(F32)


def decoder_gradient(order, keeps, gots, width, squares, count):
    slots = len(keeps)
    half = keeps[0].shape[0]
    operands = keeps + gots + list(squares)
    size = half * 4 * slots * width
    if plain(width):
        out = jnp.zeros((half, 4 * slots * width), F32)
        for s in range(slots):
            part = keeps[s] + gots[s].astype(F32)
            for m in range(4):
                block = part[:, m * width:(m + 1) * width]
                out = lax.dynamic_update_slice_in_dim(out, block, order[4 * s + m] * width, 1)
        return out, (squares[0] + squares[1])[:1, :1] / count
    return call(
        functools.partial(decoder_gradient_body, slots, width, 1.0 / count), order, operands,
        [whole(o.shape) for o in operands],
        [jax.ShapeDtypeStruct((half, 4 * slots * width), F32), jax.ShapeDtypeStruct((1, 1), F32)],
        [whole((half, 4 * slots * width)), whole((1, 1))], size, 10 * size,
        "decoder_gradient",
    )


def encoder_send_body(slots, width, across, order, mine, dpre, out):
    d = dpre[...]
    for s in range(slots):
        for m in range(4):
            here = jnp.dot(mine[4 * s + m], d, preferred_element_type=F32)
            at = (4 * s + across[m]) * width
            out[at:at + width, :] = here.astype(BF16)


def encoder_send(order, across, mine, dpre, width):
    slots = mine.shape[0] // 4
    rows, half = dpre.shape
    operands = [mine, dpre]
    shape = (4 * slots * width, half)
    if plain(width):
        blocks = [mine[4 * s + m] for s in range(slots) for m in across]
        return jnp.dot(jnp.concatenate(blocks), dpre, preferred_element_type=F32).astype(BF16)
    return call(
        functools.partial(encoder_send_body, slots, width, across), order, operands,
        [whole(o.shape) for o in operands], jax.ShapeDtypeStruct(shape, BF16), whole(shape),
        2 * shape[0] * rows * half, 2 * shape[0] * rows + 2 * shape[0] * half, "encoder_send",
    )


def encoder_gradient_body(slots, width, order, mine, dpre, got, out):
    d = dpre[...]
    for s in range(slots):
        for m in range(4):
            here = jnp.dot(mine[4 * s + m], d, preferred_element_type=F32)
            at = (4 * s + m) * width
            there = pl.ds(pl.multiple_of(order[4 * s + m] * width, width), width)
            out[there, :] = here + got[at:at + width, :].astype(F32)


def encoder_gradient(order, mine, dpre, got, width):
    slots = mine.shape[0] // 4
    rows, half = dpre.shape
    operands = [mine, dpre, got]
    shape = (4 * slots * width, half)
    if plain(width):
        out = jnp.zeros(shape, F32)
        total = jnp.dot(mine.reshape(shape[0], rows), dpre, preferred_element_type=F32) + got.astype(F32)
        for b in range(4 * slots):
            out = lax.dynamic_update_slice_in_dim(out, total[b * width:(b + 1) * width], order[b] * width, 0)
        return out
    return call(
        functools.partial(encoder_gradient_body, slots, width), order, operands,
        [whole(o.shape) for o in operands], jax.ShapeDtypeStruct(shape, F32), whole(shape),
        2 * shape[0] * rows * half, 2 * shape[0] * rows + 6 * shape[0] * half, "encoder_gradient",
    )


def local(lat, dp, inputs, dec_bias, enc_weight, enc_bias, dec_weight, other_recon, active_blocks):
    grid = Grid(lat, dp)
    rows, width = inputs.shape
    lats = enc_weight.shape[1]
    half = lats // 2
    slots = grid.slots
    centered = grid.gather((inputs.astype(F32) - dec_bias.astype(F32)[None, :]).astype(BF16))
    centered = [block for slot in centered for block in slot]
    near = dec_weight if plain(width) else bring(grid.every, dec_weight)
    (pre_act,) = encode(grid.every[:-4], centered[:-4], enc_weight, enc_bias[None, :], None)
    act, slope = encode(grid.every[-4:], centered[-4:], enc_weight, pre_act, active_blocks.T)
    turned = turn(grid.every, centered)

    def part(s, earlier):
        earlier = [] if earlier is None else [earlier]
        if s == slots // 2 - 1:
            earlier.append(turned)
        return decode(grid.order[s], act, near, width, earlier)

    recon = grid.scatter_sum(part)
    bias, x = dec_bias.astype(F32), inputs.astype(F32)
    error_local = recon + (other_recon + bias[None, :]) - x
    state = [jnp.zeros((rows, lats), F32), jnp.zeros((8, width), F32)]
    keeps, gots = [], []

    for s, blocks in enumerate(grid.gather(error_local.astype(BF16))):
        order = grid.order[s]
        keep, send, *state[:] = backward(
            order, grid.across, act, blocks, near, *state, slope if s == slots - 1 else None
        )
        keeps.append(keep)
        gots.append(grid.swap_core(send))

    mine, other, squares = state

    square, step = squares, 1
    while step < dp:
        square_got = lax.ppermute(square, "dp", [(d, d ^ step) for d in range(dp)])
        step *= 2
        if step < dp:
            square = square + square_got
    got = grid.swap_core(encoder_send(grid.every, grid.across, turned, other, width))
    grad_dec, mean = decoder_gradient(
        grid.every, keeps, gots, width, (square, square_got), rows * dp * width * lat
    )
    mse_loss = mean.reshape(())
    grad_enc = encoder_gradient(grid.every, turned, mine, got, width)

    return (error_local, mse_loss, grid.spread(grad_dec, 0), grid.spread(grad_enc, 1))


def solution(mesh):
    placed = (
        P("dp", "lat"),
        P("lat"),
        P(None, "lat"),
        P("lat"),
        P("lat", None),
        P("dp", "lat"),
        P("dp", "lat"),
    )
    lat, dp = mesh.shape["lat"], mesh.shape["dp"]
    return jax.shard_map(
        functools.partial(local, lat, dp),
        mesh=mesh,
        in_specs=placed,
        out_specs=(P("dp", "lat"), P(), P(("lat", "dp"), None), P(None, ("lat", "dp"))),
        check_vma=False,
    )
```

time: 163 us -> 144 us (0.88)
  waiting for transfers between devices: 68.5 us -> 58.4 us
  local copies, waits for them, and re-layouts: 10.9 us -> 1.75 us
  Pallas kernels: 23.1 us -> 28.2 us
  starting transfers between devices: 53.8 us -> 51.2 us
  between operations: 2.75 us -> 0.91 us
    ppermute x41, waiting for transfers between devices: 67.7 us -> 55.4 us  [swap(): return lax.ppermute(x, ('lat', 'dp'), pairs)]
    unnamed x37 -> x12, local copies, waits for them, and re-layouts: 10.2 us -> 1.62 us
    pallas_call x14 -> x15, Pallas kernels: 23.1 us -> 28.2 us  [call(): pl.pallas_call(body, grid_spec=pltpu.PrefetchScalarGridSpec(num_scalar_pr...]
    ppermute x9 -> x5, waiting for transfers between devices: 0.02 us -> 2.55 us  [swap_core(): return lax.ppermute(x, ('lat', 'dp'), pairs)]
  transfers between devices with their start and end apart: 51 -> 47, of which waited for: 25 -> 25; matrix products, arithmetic and copies ran while one was open for 1% -> 1% of each run, Pallas kernels for 10% -> 13%
where the time goes in v3:
time: 144 us
  waiting for transfers between devices  58.4 us (41%)
  starting transfers between devices  51.2 us (36%)
  Pallas kernels  28.2 us (20%)
  other arithmetic  3.87 us (3%)
  local copies, waits for them, and re-layouts  1.75 us (1%)
    ppermute x41, waiting for transfers between devices, swap(): return lax.ppermute(x, ('lat', 'dp'), pairs)  55.4 us
    ppermute x41, starting transfers between devices, swap(): return lax.ppermute(x, ('lat', 'dp'), pairs)  49.9 us
    pallas_call x15, Pallas kernels, call(): pl.pallas_call(body, grid_spec=pltpu.PrefetchScalarGridSpec(num_scalar_pr...  28.2 us
  transfers between devices with their start and end apart: 47, of which 25 were waited for; matrix products, arithmetic and copies ran while one was open for 1% of the time, Pallas kernels for 13%

profile of v3, /device:TPU:0, one launch (start us, length us, event | category | flops | bytes accessed | tf_op | source)
XLA Modules:
  0.0 144.3 jit_solution(1222003857724839962)
XLA Ops:
  2.3 4.1 %collective-permute-start = (bf16[512,256]{1,0:T(8,128)(2,1)S(1)}, bf16[512,256]{1,0:T(8,128)(2,1)S(1)}, u32[]{:S(2)}, u32[]{:S(2)}) collective-permute-start(bf16[512,256]{1,0:T(8,128)(2,1)S(1)} %fusion.refs_0_), channel_id=1, source_target_pairs={{0,16},{1,17},{2,18},{3,19},{4,20},{5,21},{6,22},{7,23},{8,24},{9,... | collective-permute-start | bytes 786440 | tf_op jit(solution)/shard_map/ppermute | solution.py:34
  6.4 1.5 %collective-permute-start.6 = (bf16[512,256]{1,0:T(8,128)(2,1)S(1)}, bf16[512,256]{1,0:T(8,128)(2,1)S(1)}, u32[]{:S(2)}, u32[]{:S(2)}) collective-permute-start(bf16[512,256]{1,0:T(8,128)(2,1)S(1)} %fusion.refs_0_), channel_id=1, source_target_pairs={{0,2},{1,5},{2,0},{3,7},{4,6},{5,1},{6,4},{7,3},{8,10},{9,13},{10,... | collective-permute-start | bytes 786440 | tf_op jit(solution)/shard_map/ppermute | solution.py:34
  7.9 1.5 %collective-permute-start.7 = (bf16[512,256]{1,0:T(8,128)(2,1)S(1)}, bf16[512,256]{1,0:T(8,128)(2,1)S(1)}, u32[]{:S(2)}, u32[]{:S(2)}) collective-permute-start(bf16[512,256]{1,0:T(8,128)(2,1)S(1)} %fusion.refs_0_), channel_id=1, source_target_pairs={{0,4},{1,3},{2,6},{3,1},{4,0},{5,7},{6,2},{7,5},{8,12},{9,11},{10,... | collective-permute-start | bytes 786440 | tf_op jit(solution)/shard_map/ppermute | solution.py:34
  9.4 1.6 %collective-permute-start.9 = (bf16[512,256]{1,0:T(8,128)(2,1)S(1)}, bf16[512,256]{1,0:T(8,128)(2,1)S(1)}, u32[]{:S(2)}, u32[]{:S(2)}) collective-permute-start(bf16[512,256]{1,0:T(8,128)(2,1)S(1)} %fusion.refs_0_), channel_id=1, source_target_pairs={{0,8},{1,9},{2,10},{3,11},{4,12},{5,13},{6,14},{7,15},{8,0},{9,1},... | collective-permute-start | bytes 786440 | tf_op jit(solution)/shard_map/ppermute | solution.py:34
  11.0 7.4 %collective-permute-done.refs_8_ = bf16[512,256]{1,0:T(8,128)(2,1)S(1)} collective-permute-done((bf16[512,256]{1,0:T(8,128)(2,1)S(1)}, bf16[512,256]{1,0:T(8,128)(2,1)S(1)}, u32[]{:S(2)}, u32[]{:S(2)}) %collective-permute-start) | collective-permute-done | bytes 262176 | tf_op jit(solution)/shard_map/ppermute | solution.py:34
  18.4 1.5 %collective-permute-start.2 = (bf16[512,256]{1,0:T(8,128)(2,1)S(1)}, bf16[512,256]{1,0:T(8,128)(2,1)S(1)}, u32[]{:S(2)}, u32[]{:S(2)}) collective-permute-start(bf16[512,256]{1,0:T(8,128)(2,1)S(1)} %collective-permute-done.refs_8_), channel_id=1, source_target_pairs={{0,2},{1,5},{2,0},{3,7},{4,6},{5,1},{6,4},{7,3},{8,10},{9,13},{10,... | collective-permute-start | bytes 786440 | tf_op jit(solution)/shard_map/ppermute | solution.py:34
  20.6 1.5 %collective-permute-start.8 = (bf16[512,256]{1,0:T(8,128)(2,1)S(1)}, bf16[512,256]{1,0:T(8,128)(2,1)S(1)}, u32[]{:S(2)}, u32[]{:S(2)}) collective-permute-start(bf16[512,256]{1,0:T(8,128)(2,1)S(1)} %collective-permute-done.6.refs_1_), channel_id=1, source_target_pairs={{0,4},{1,3},{2,6},{3,1},{4,0},{5,7},{6,2},{7,5},{8,12},{9,11},{10,... | collective-permute-start | bytes 786440 | tf_op jit(solution)/shard_map/ppermute | solution.py:34
  22.1 1.5 %collective-permute-start.10 = (bf16[512,256]{1,0:T(8,128)(2,1)S(1)}, bf16[512,256]{1,0:T(8,128)(2,1)S(1)}, u32[]{:S(2)}, u32[]{:S(2)}) collective-permute-start(bf16[512,256]{1,0:T(8,128)(2,1)S(1)} %collective-permute-done.6.refs_1_), channel_id=1, source_target_pairs={{0,8},{1,9},{2,10},{3,11},{4,12},{5,13},{6,14},{7,15},{8,0},{9,1},... | collective-permute-start | bytes 786440 | tf_op jit(solution)/shard_map/ppermute | solution.py:34
  24.1 2.9 %collective-permute-done.2.refs_9_ = bf16[512,256]{1,0:T(8,128)(2,1)S(1)} collective-permute-done((bf16[512,256]{1,0:T(8,128)(2,1)S(1)}, bf16[512,256]{1,0:T(8,128)(2,1)S(1)}, u32[]{:S(2)}, u32[]{:S(2)}) %collective-permute-start.2) | collective-permute-done | bytes 262176 | tf_op jit(solution)/shard_map/ppermute | solution.py:34
  27.9 1.3 collective-permute-done.1.refs_0_.refs_12_
  29.2 1.5 %collective-permute-start.13 = (bf16[512,256]{1,0:T(8,128)(2,1)S(1)}, bf16[512,256]{1,0:T(8,128)(2,1)S(1)}, u32[]{:S(2)}, u32[]{:S(2)}) collective-permute-start(bf16[512,256]{1,0:T(8,128)(2,1)S(1)} %collective-permute-done.refs_8_), channel_id=1, source_target_pairs={{0,4},{1,3},{2,6},{3,1},{4,0},{5,7},{6,2},{7,5},{8,12},{9,11},{10,... | collective-permute-start | bytes 786440 | tf_op jit(solution)/shard_map/ppermute | solution.py:34
  31.2 3.6 %collective-permute-done.10.refs_5_ = bf16[512,256]{1,0:T(8,128)(2,1)S(1)} collective-permute-done((bf16[512,256]{1,0:T(8,128)(2,1)S(1)}, bf16[512,256]{1,0:T(8,128)(2,1)S(1)}, u32[]{:S(2)}, u32[]{:S(2)}) %collective-permute-start.10) | collective-permute-done | bytes 262176 | tf_op jit(solution)/shard_map/ppermute | solution.py:34
  36.1 1.6 %copy-done.1 = bf16[256,4096]{1,0:T(8,128)(2,1)S(1)} copy-done((bf16[256,4096]{1,0:T(8,128)(2,1)S(1)}, bf16[256,4096]{1,0:T(8,128)(2,1)}, u32[]{:S(2)}) %copy-start.1) | copy-done | bytes 2097176
  39.3 1.2 collective-permute-start.5
  41.2 5.3 %encode.2.refs_5_ = f32[512,256]{1,0:T(8,128)S(1)} custom-call(s32[12]{0:T(128)S(1)} %pad_add_fusion.2.order, bf16[512,256]{1,0:T(8,128)(2,1)S(1)} %fusion.refs_0_, bf16[512,256]{1,0:T(8,128)(2,1)S(1)} %collective-permute-done.6.refs_1_, bf16[512,256]{1,0:T(8,128)(2,1)S(1)} %collective-permute-done.7.refs_2_, ...), custom_call_target="tpu_custom_call" | custom-call | flops 805306368 | bytes 5767168 | tf_op jit(solution)/shard_map/encode/pallas_call | solution.py:126
  47.7 2.4 %encode.3 = (bf16[512,256]{1,0:T(8,128)(2,1)S(1)}, f32[512,256]{1,0:T(8,128)S(1)}) custom-call(s32[4]{0:T(128)S(1)} %get-tuple-element.70.order, bf16[512,256]{1,0:T(8,128)(2,1)S(1)} %collective-permute-done.1.refs_0_.refs_12_, bf16[512,256]{1,0:T(8,128)(2,1)S(1)} %collective-permute-done.3.refs_1_.refs_13_, ...), custom_call_target="tpu_custom_call" | custom-call | flops 268435456 | bytes 2621440 | tf_op jit(solution)/shard_map/encode/pallas_call | solution.py:126
  53.1 1.3 collective-permute-start.19
  54.4 3.6 %turn.1.rest_1_.mine = bf16[16,256,512]{2,1,0:T(8,128)(2,1)S(1)} custom-call(s32[16]{0:T(128)S(1)} %pad_add_fusion.3.order, bf16[512,256]{1,0:T(8,128)(2,1)S(1)} %fusion.refs_0_, bf16[512,256]{1,0:T(8,128)(2,1)S(1)} %collective-permute-done.6.refs_1_, bf16[512,256]{1,0:T(8,128)(2,1)S(1)} %collective-permute-done.7.refs_2_, ...), custom_call_target="tpu_custom_call" | custom-call | bytes 8388608 | tf_op jit(solution)/shard_map/turn/pallas_call | solution.py:126
  58.0 2.4 %collective-permute-done.15.rest_0_ = bf16[2,512,256]{2,1,0:T(8,128)(2,1)S(1)} collective-permute-done((bf16[2,512,256]{2,1,0:T(8,128)(2,1)S(1)}, bf16[2,512,256]{2,1,0:T(8,128)(2,1)S(1)}, u32[]{:S(2)}, u32[]{:S(2)}) %collective-permute-start.15) | collective-permute-done | bytes 524320 | tf_op jit(solution)/shard_map/ppermute | solution.py:34
  63.1 1.5 %collective-permute-start.20 = (bf16[512,256]{1,0:T(8,128)(2,1)S(1)}, bf16[512,256]{1,0:T(8,128)(2,1)S(1)}, u32[]{:S(2)}, u32[]{:S(2)}) collective-permute-start(bf16[512,256]{1,0:T(8,128)(2,1)S(1)} %get-tuple-element.66), channel_id=1, source_target_pairs={{0,8},{1,9},{2,10},{3,11},{4,12},{5,13},{6,14},{7,15},{8,0},{9,1},... | collective-permute-start | bytes 786440 | tf_op jit(solution)/shard_map/ppermute | solution.py:34
  64.5 1.4 %collective-permute-done.19 = bf16[2,512,256]{2,1,0:T(8,128)(2,1)S(1)} collective-permute-done((bf16[2,512,256]{2,1,0:T(8,128)(2,1)S(1)}, bf16[2,512,256]{2,1,0:T(8,128)(2,1)S(1)}, u32[]{:S(2)}, u32[]{:S(2)}) %collective-permute-start.19) | collective-permute-done | bytes 524320 | tf_op jit(solution)/shard_map/ppermute | solution.py:34
  66.1 3.9 %collective-permute-done.16.rest_0_ = bf16[512,256]{1,0:T(8,128)(2,1)S(1)} collective-permute-done((bf16[512,256]{1,0:T(8,128)(2,1)S(1)}, bf16[512,256]{1,0:T(8,128)(2,1)S(1)}, u32[]{:S(2)}, u32[]{:S(2)}) %collective-permute-start.16) | collective-permute-done | bytes 262176 | tf_op jit(solution)/shard_map/ppermute | solution.py:34
  71.6 1.2 collective-permute-start.17
  72.9 3.0 %collective-permute-done.23 = bf16[2,512,256]{2,1,0:T(8,128)(2,1)S(1)} collective-permute-done((bf16[2,512,256]{2,1,0:T(8,128)(2,1)S(1)}, bf16[2,512,256]{2,1,0:T(8,128)(2,1)S(1)}, u32[]{:S(2)}, u32[]{:S(2)}) %collective-permute-start.23) | collective-permute-done | bytes 524320 | tf_op jit(solution)/shard_map/ppermute | solution.py:34
  76.0 1.3 collective-permute-start.24
  77.7 2.0 %collective-permute-start.22 = (bf16[512,256]{1,0:T(8,128)(2,1)S(1)}, bf16[512,256]{1,0:T(8,128)(2,1)S(1)}, u32[]{:S(2)}, u32[]{:S(2)}) collective-permute-start(bf16[512,256]{1,0:T(8,128)(2,1)S(1)} %fusion.7), channel_id=1, source_target_pairs={{0,16},{1,17},{2,18},{3,19},{4,20},{5,21},{6,22},{7,23},{8,24},{9,... | collective-permute-start | bytes 786440 | tf_op jit(solution)/shard_map/ppermute | solution.py:34
  79.7 2.7 %collective-permute-done.24 = bf16[512,256]{1,0:T(8,128)(2,1)S(1)} collective-permute-done((bf16[512,256]{1,0:T(8,128)(2,1)S(1)}, bf16[512,256]{1,0:T(8,128)(2,1)S(1)}, u32[]{:S(2)}, u32[]{:S(2)}) %collective-permute-start.24) | collective-permute-done | bytes 262176 | tf_op jit(solution)/shard_map/ppermute | solution.py:34
  82.5 1.2 collective-permute-start.25
  84.9 3.1 %collective-permute-done.22 = bf16[512,256]{1,0:T(8,128)(2,1)S(1)} collective-permute-done((bf16[512,256]{1,0:T(8,128)(2,1)S(1)}, bf16[512,256]{1,0:T(8,128)(2,1)S(1)}, u32[]{:S(2)}, u32[]{:S(2)}) %collective-permute-start.22) | collective-permute-done | bytes 262176 | tf_op jit(solution)/shard_map/ppermute | solution.py:34
  88.0 2.7 %collective-permute-done.25 = bf16[512,256]{1,0:T(8,128)(2,1)S(1)} collective-permute-done((bf16[512,256]{1,0:T(8,128)(2,1)S(1)}, bf16[512,256]{1,0:T(8,128)(2,1)S(1)}, u32[]{:S(2)}, u32[]{:S(2)}) %collective-permute-start.25) | collective-permute-done | bytes 262176 | tf_op jit(solution)/shard_map/ppermute | solution.py:34
  91.8 2.9 %collective-permute-start.33 = (bf16[512,256]{1,0:T(8,128)(2,1)S(1)}, bf16[512,256]{1,0:T(8,128)(2,1)S(1)}, u32[]{:S(2)}, u32[]{:S(2)}) collective-permute-start(bf16[512,256]{1,0:T(8,128)(2,1)S(1)} %get-tuple-element.62.e0), channel_id=1, source_target_pairs={{0,16},{1,17},{2,18},{3,19},{4,20},{5,21},{6,22},{7,23},{8,24},{9,... | collective-permute-start | bytes 786440 | tf_op jit(solution)/shard_map/ppermute | solution.py:34
  94.9 2.8 %collective-permute-start.29 = (bf16[512,256]{1,0:T(8,128)(2,1)S(1)}, bf16[512,256]{1,0:T(8,128)(2,1)S(1)}, u32[]{:S(2)}, u32[]{:S(2)}) collective-permute-start(bf16[512,256]{1,0:T(8,128)(2,1)S(1)} %get-tuple-element.62.e0), channel_id=1, source_target_pairs={{0,8},{1,9},{2,10},{3,11},{4,12},{5,13},{6,14},{7,15},{8,0},{9,1},... | collective-permute-start | bytes 786440 | tf_op jit(solution)/shard_map/ppermute | solution.py:34
  98.7 4.7 %collective-permute-done.33.e0 = bf16[512,256]{1,0:T(8,128)(2,1)S(1)} collective-permute-done((bf16[512,256]{1,0:T(8,128)(2,1)S(1)}, bf16[512,256]{1,0:T(8,128)(2,1)S(1)}, u32[]{:S(2)}, u32[]{:S(2)}) %collective-permute-start.33) | collective-permute-done | bytes 262176 | tf_op jit(solution)/shard_map/ppermute | solution.py:34
  103.4 1.4 collective-permute-start.34
  106.8 2.0 %collective-permute-start.37 = (bf16[512,256]{1,0:T(8,128)(2,1)S(1)}, bf16[512,256]{1,0:T(8,128)(2,1)S(1)}, u32[]{:S(2)}, u32[]{:S(2)}) collective-permute-start(bf16[512,256]{1,0:T(8,128)(2,1)S(1)} %collective-permute-done.33.e0), channel_id=1, source_target_pairs={{0,8},{1,9},{2,10},{3,11},{4,12},{5,13},{6,14},{7,15},{8,0},{9,1},... | collective-permute-start | bytes 786440 | tf_op jit(solution)/shard_map/ppermute | solution.py:34
  108.9 3.7 %collective-permute-done.34.e1 = bf16[512,256]{1,0:T(8,128)(2,1)S(1)} collective-permute-done((bf16[512,256]{1,0:T(8,128)(2,1)S(1)}, bf16[512,256]{1,0:T(8,128)(2,1)S(1)}, u32[]{:S(2)}, u32[]{:S(2)}) %collective-permute-start.34) | collective-permute-done | bytes 262176 | tf_op jit(solution)/shard_map/ppermute | solution.py:34
  112.6 1.5 %collective-permute-done.30.e1 = bf16[512,256]{1,0:T(8,128)(2,1)S(1)} collective-permute-done((bf16[512,256]{1,0:T(8,128)(2,1)S(1)}, bf16[512,256]{1,0:T(8,128)(2,1)S(1)}, u32[]{:S(2)}, u32[]{:S(2)}) %collective-permute-start.30) | collective-permute-done | bytes 262176 | tf_op jit(solution)/shard_map/ppermute | solution.py:34
  117.2 2.5 %collective-permute-done.37.e0 = bf16[512,256]{1,0:T(8,128)(2,1)S(1)} collective-permute-done((bf16[512,256]{1,0:T(8,128)(2,1)S(1)}, bf16[512,256]{1,0:T(8,128)(2,1)S(1)}, u32[]{:S(2)}, u32[]{:S(2)}) %collective-permute-start.37) | collective-permute-done | bytes 262176 | tf_op jit(solution)/shard_map/ppermute | solution.py:34
  120.8 2.9 %collective-permute-done.38.e1 = bf16[512,256]{1,0:T(8,128)(2,1)S(1)} collective-permute-done((bf16[512,256]{1,0:T(8,128)(2,1)S(1)}, bf16[512,256]{1,0:T(8,128)(2,1)S(1)}, u32[]{:S(2)}, u32[]{:S(2)}) %collective-permute-start.38) | collective-permute-done | bytes 262176 | tf_op jit(solution)/shard_map/ppermute | solution.py:34
  124.0 1.3 backward.4
  125.3 1.3 backward.5
  126.6 1.3 backward.6
  128.8 2.8 %collective-permute-done.40.e3 = bf16[512,256]{1,0:T(8,128)(2,1)S(1)} collective-permute-done((bf16[512,256]{1,0:T(8,128)(2,1)S(1)}, bf16[512,256]{1,0:T(8,128)(2,1)S(1)}, u32[]{:S(2)}, u32[]{:S(2)}) %collective-permute-start.40) | collective-permute-done | bytes 262176 | tf_op jit(solution)/shard_map/ppermute | solution.py:34
  131.7 1.3 backward.7
  133.0 1.8 %encoder_send.1 = bf16[4096,128]{1,0:T(8,128)(2,1)S(1)} custom-call(s32[16]{0:T(128)S(1)} %pad_add_fusion.3.order, bf16[16,256,512]{2,1,0:T(8,128)(2,1)S(1)} %turn.1.rest_1_.mine, bf16[512,128]{1,0:T(8,128)(2,1)S(1)} %get-tuple-element.61.dpre), custom_call_target="tpu_custom_call" | custom-call | flops 536870912 | bytes 5242880 | tf_op jit(solution)/shard_map/encoder_send/pallas_call | solution.py:126
  136.0 1.9 %collective-permute-done.41.refs_4_ = bf16[128,1024]{1,0:T(8,128)(2,1)S(1)} collective-permute-done((bf16[128,1024]{1,0:T(8,128)(2,1)S(1)}, bf16[128,1024]{1,0:T(8,128)(2,1)S(1)}, u32[]{:S(2)}, u32[]{:S(2)}) %collective-permute-start.41) | collective-permute-done | bytes 262176 | tf_op jit(solution)/shard_map/ppermute | solution.py:50
  139.1 2.1 %decoder_gradient.1 = (f32[128,4096]{1,0:T(8,128)}, f32[1,1]{1,0:T(1,128)}) custom-call(s32[16]{0:T(128)S(1)} %pad_add_fusion.3.order, f32[128,1024]{1,0:T(8,128)S(1)} %get-tuple-element.42.refs_0_, f32[128,1024]{1,0:T(8,128)S(1)} %get-tuple-element.45.refs_1_, f32[128,1024]{1,0:T(8,128)S(1)} %get-tuple-element.48.refs_2_, ...), custom_call_target="tpu_custom_call" | custom-call | flops 524288 | bytes 5242880 | tf_op jit(solution)/shard_map/decoder_gradient/pallas_call | solution.py:126
  141.1 3.1 %encoder_gradient.1 = f32[4096,128]{1,0:T(8,128)} custom-call(s32[16]{0:T(128)S(1)} %pad_add_fusion.3.order, bf16[16,256,512]{2,1,0:T(8,128)(2,1)S(1)} %turn.1.rest_1_.mine, bf16[512,128]{1,0:T(8,128)(2,1)S(1)} %get-tuple-element.60.dpre, bf16[4096,128]{1,0:T(8,128)(2,1)S(1)} %collective-permute-done.46.got), custom_call_target="tpu_custom_call" | custom-call | flops 536870912 | bytes 7340032 | tf_op jit(solution)/shard_map/encoder_gradient/pallas_call | solution.py:126
  (95 shorter events, 30.2 us)
Async XLA Ops:
  2.3 16.1 %collective-permute-start = (bf16[512,256]{1,0:T(8,128)(2,1)S(1)}, bf16[512,256]{1,0:T(8,128)(2,1)S(1)}, u32[]{:S(2)}, u32[]{:S(2)}) collective-permute-start(bf16[512,256]{1,0:T(8,128)(2,1)S(1)} %fusion.refs_0_), channel_id=1, source_target_pairs={{0,16},{1,17},{2,18},{3,19},{4,20},{5,21},{6,22},{7,23},{8,24},{9,... | collective-permute-start | bytes 786440 | tf_op jit(solution)/shard_map/ppermute | solution.py:34
  6.4 14.2 %collective-permute-start.6 = (bf16[512,256]{1,0:T(8,128)(2,1)S(1)}, bf16[512,256]{1,0:T(8,128)(2,1)S(1)}, u32[]{:S(2)}, u32[]{:S(2)}) collective-permute-start(bf16[512,256]{1,0:T(8,128)(2,1)S(1)} %fusion.refs_0_), channel_id=1, source_target_pairs={{0,2},{1,5},{2,0},{3,7},{4,6},{5,1},{6,4},{7,3},{8,10},{9,13},{10,... | collective-permute-start | bytes 786440 | tf_op jit(solution)/shard_map/ppermute | solution.py:34
  7.9 14.2 %collective-permute-start.7 = (bf16[512,256]{1,0:T(8,128)(2,1)S(1)}, bf16[512,256]{1,0:T(8,128)(2,1)S(1)}, u32[]{:S(2)}, u32[]{:S(2)}) collective-permute-start(bf16[512,256]{1,0:T(8,128)(2,1)S(1)} %fusion.refs_0_), channel_id=1, source_target_pairs={{0,4},{1,3},{2,6},{3,1},{4,0},{5,7},{6,2},{7,5},{8,12},{9,11},{10,... | collective-permute-start | bytes 786440 | tf_op jit(solution)/shard_map/ppermute | solution.py:34
  9.4 14.2 %collective-permute-start.9 = (bf16[512,256]{1,0:T(8,128)(2,1)S(1)}, bf16[512,256]{1,0:T(8,128)(2,1)S(1)}, u32[]{:S(2)}, u32[]{:S(2)}) collective-permute-start(bf16[512,256]{1,0:T(8,128)(2,1)S(1)} %fusion.refs_0_), channel_id=1, source_target_pairs={{0,8},{1,9},{2,10},{3,11},{4,12},{5,13},{6,14},{7,15},{8,0},{9,1},... | collective-permute-start | bytes 786440 | tf_op jit(solution)/shard_map/ppermute | solution.py:34
  18.4 8.6 %collective-permute-start.2 = (bf16[512,256]{1,0:T(8,128)(2,1)S(1)}, bf16[512,256]{1,0:T(8,128)(2,1)S(1)}, u32[]{:S(2)}, u32[]{:S(2)}) collective-permute-start(bf16[512,256]{1,0:T(8,128)(2,1)S(1)} %collective-permute-done.refs_8_), channel_id=1, source_target_pairs={{0,2},{1,5},{2,0},{3,7},{4,6},{5,1},{6,4},{7,3},{8,10},{9,13},{10,... | collective-permute-start | bytes 786440 | tf_op jit(solution)/shard_map/ppermute | solution.py:34
  20.0 9.2 %collective-permute-start.1 = (bf16[512,256]{1,0:T(8,128)(2,1)S(1)}, bf16[512,256]{1,0:T(8,128)(2,1)S(1)}, u32[]{:S(2)}, u32[]{:S(2)}) collective-permute-start(bf16[512,256]{1,0:T(8,128)(2,1)S(1)} %collective-permute-done.refs_8_), channel_id=1, source_target_pairs={{0,8},{1,9},{2,10},{3,11},{4,12},{5,13},{6,14},{7,15},{8,0},{9,1},... | collective-permute-start | bytes 786440 | tf_op jit(solution)/shard_map/ppermute | solution.py:34
  20.6 10.2 %collective-permute-start.8 = (bf16[512,256]{1,0:T(8,128)(2,1)S(1)}, bf16[512,256]{1,0:T(8,128)(2,1)S(1)}, u32[]{:S(2)}, u32[]{:S(2)}) collective-permute-start(bf16[512,256]{1,0:T(8,128)(2,1)S(1)} %collective-permute-done.6.refs_1_), channel_id=1, source_target_pairs={{0,4},{1,3},{2,6},{3,1},{4,0},{5,7},{6,2},{7,5},{8,12},{9,11},{10,... | collective-permute-start | bytes 786440 | tf_op jit(solution)/shard_map/ppermute | solution.py:34
  22.1 12.8 %collective-permute-start.10 = (bf16[512,256]{1,0:T(8,128)(2,1)S(1)}, bf16[512,256]{1,0:T(8,128)(2,1)S(1)}, u32[]{:S(2)}, u32[]{:S(2)}) collective-permute-start(bf16[512,256]{1,0:T(8,128)(2,1)S(1)} %collective-permute-done.6.refs_1_), channel_id=1, source_target_pairs={{0,8},{1,9},{2,10},{3,11},{4,12},{5,13},{6,14},{7,15},{8,0},{9,1},... | collective-permute-start | bytes 786440 | tf_op jit(solution)/shard_map/ppermute | solution.py:34
  23.6 14.8 %collective-permute-start.11 = (bf16[512,256]{1,0:T(8,128)(2,1)S(1)}, bf16[512,256]{1,0:T(8,128)(2,1)S(1)}, u32[]{:S(2)}, u32[]{:S(2)}) collective-permute-start(bf16[512,256]{1,0:T(8,128)(2,1)S(1)} %collective-permute-done.9.refs_4_), channel_id=1, source_target_pairs={{0,4},{1,3},{2,6},{3,1},{4,0},{5,7},{6,2},{7,5},{8,12},{9,11},{10,... | collective-permute-start | bytes 786440 | tf_op jit(solution)/shard_map/ppermute | solution.py:34
  27.0 12.3 %collective-permute-start.3 = (bf16[512,256]{1,0:T(8,128)(2,1)S(1)}, bf16[512,256]{1,0:T(8,128)(2,1)S(1)}, u32[]{:S(2)}, u32[]{:S(2)}) collective-permute-start(bf16[512,256]{1,0:T(8,128)(2,1)S(1)} %collective-permute-done.2.refs_9_), channel_id=1, source_target_pairs={{0,8},{1,9},{2,10},{3,11},{4,12},{5,13},{6,14},{7,15},{8,0},{9,1},... | collective-permute-start | bytes 786440 | tf_op jit(solution)/shard_map/ppermute | solution.py:34
  29.2 11.4 %collective-permute-start.13 = (bf16[512,256]{1,0:T(8,128)(2,1)S(1)}, bf16[512,256]{1,0:T(8,128)(2,1)S(1)}, u32[]{:S(2)}, u32[]{:S(2)}) collective-permute-start(bf16[512,256]{1,0:T(8,128)(2,1)S(1)} %collective-permute-done.refs_8_), channel_id=1, source_target_pairs={{0,4},{1,3},{2,6},{3,1},{4,0},{5,7},{6,2},{7,5},{8,12},{9,11},{10,... | collective-permute-start | bytes 786440 | tf_op jit(solution)/shard_map/ppermute | solution.py:34
  30.7 10.5 %collective-permute-start.14 = (bf16[512,256]{1,0:T(8,128)(2,1)S(1)}, bf16[512,256]{1,0:T(8,128)(2,1)S(1)}, u32[]{:S(2)}, u32[]{:S(2)}) collective-permute-start(bf16[512,256]{1,0:T(8,128)(2,1)S(1)} %collective-permute-done.2.refs_9_), channel_id=1, source_target_pairs={{0,4},{1,3},{2,6},{3,1},{4,0},{5,7},{6,2},{7,5},{8,12},{9,11},{10,... | collective-permute-start | bytes 786440 | tf_op jit(solution)/shard_map/ppermute | solution.py:34
  34.8 6.4 %collective-permute-start.12 = (bf16[512,256]{1,0:T(8,128)(2,1)S(1)}, bf16[512,256]{1,0:T(8,128)(2,1)S(1)}, u32[]{:S(2)}, u32[]{:S(2)}) collective-permute-start(bf16[512,256]{1,0:T(8,128)(2,1)S(1)} %collective-permute-done.10.refs_5_), channel_id=1, source_target_pairs={{0,4},{1,3},{2,6},{3,1},{4,0},{5,7},{6,2},{7,5},{8,12},{9,11},{10,... | collective-permute-start | bytes 786440 | tf_op jit(solution)/shard_map/ppermute | solution.py:34
  38.4 8.1 %collective-permute-start.4 = (bf16[512,256]{1,0:T(8,128)(2,1)S(1)}, bf16[512,256]{1,0:T(8,128)(2,1)S(1)}, u32[]{:S(2)}, u32[]{:S(2)}) collective-permute-start(bf16[512,256]{1,0:T(8,128)(2,1)S(1)} %collective-permute-done.1.refs_0_.refs_12_), channel_id=1, source_target_pairs={{0,4},{1,3},{2,6},{3,1},{4,0},{5,7},{6,2},{7,5},{8,12},{9,11},{10,... | collective-permute-start | bytes 786440 | tf_op jit(solution)/shard_map/ppermute | solution.py:34
  39.3 8.3 %collective-permute-start.5 = (bf16[512,256]{1,0:T(8,128)(2,1)S(1)}, bf16[512,256]{1,0:T(8,128)(2,1)S(1)}, u32[]{:S(2)}, u32[]{:S(2)}) collective-permute-start(bf16[512,256]{1,0:T(8,128)(2,1)S(1)} %collective-permute-done.3.refs_1_.refs_13_), channel_id=1, source_target_pairs={{0,4},{1,3},{2,6},{3,1},{4,0},{5,7},{6,2},{7,5},{8,12},{9,11},{10,... | collective-permute-start | bytes 786440 | tf_op jit(solution)/shard_map/ppermute | solution.py:34
  51.1 9.2 %collective-permute-start.15 = (bf16[2,512,256]{2,1,0:T(8,128)(2,1)S(1)}, bf16[2,512,256]{2,1,0:T(8,128)(2,1)S(1)}, u32[]{:S(2)}, u32[]{:S(2)}) collective-permute-start(bf16[2,512,256]{2,1,0:T(8,128)(2,1)S(1)} %get-tuple-element.35), channel_id=1, source_target_pairs={{0,4},{1,3},{2,6},{3,1},{4,0},{5,7},{6,2},{7,5},{8,12},{9,11},{10,... | collective-permute-start | bytes 1572872 | tf_op jit(solution)/shard_map/ppermute | solution.py:34
  53.1 12.8 %collective-permute-start.19 = (bf16[2,512,256]{2,1,0:T(8,128)(2,1)S(1)}, bf16[2,512,256]{2,1,0:T(8,128)(2,1)S(1)}, u32[]{:S(2)}, u32[]{:S(2)}) collective-permute-start(bf16[2,512,256]{2,1,0:T(8,128)(2,1)S(1)} %get-tuple-element.39), channel_id=1, source_target_pairs={{0,4},{1,3},{2,6},{3,1},{4,0},{5,7},{6,2},{7,5},{8,12},{9,11},{10,... | collective-permute-start | bytes 1572872 | tf_op jit(solution)/shard_map/ppermute | solution.py:34
  61.4 14.5 %collective-permute-start.23 = (bf16[2,512,256]{2,1,0:T(8,128)(2,1)S(1)}, bf16[2,512,256]{2,1,0:T(8,128)(2,1)S(1)}, u32[]{:S(2)}, u32[]{:S(2)}) collective-permute-start(bf16[2,512,256]{2,1,0:T(8,128)(2,1)S(1)} %get-tuple-element.41), channel_id=1, source_target_pairs={{0,4},{1,3},{2,6},{3,1},{4,0},{5,7},{6,2},{7,5},{8,12},{9,11},{10,... | collective-permute-start | bytes 1572872 | tf_op jit(solution)/shard_map/ppermute | solution.py:34
  62.4 7.6 %collective-permute-start.16 = (bf16[512,256]{1,0:T(8,128)(2,1)S(1)}, bf16[512,256]{1,0:T(8,128)(2,1)S(1)}, u32[]{:S(2)}, u32[]{:S(2)}) collective-permute-start(bf16[512,256]{1,0:T(8,128)(2,1)S(1)} %get-tuple-element.67), channel_id=1, source_target_pairs={{0,8},{1,9},{2,10},{3,11},{4,12},{5,13},{6,14},{7,15},{8,0},{9,1},... | collective-permute-start | bytes 786440 | tf_op jit(solution)/shard_map/ppermute | solution.py:34
  63.1 14.2 %collective-permute-start.20 = (bf16[512,256]{1,0:T(8,128)(2,1)S(1)}, bf16[512,256]{1,0:T(8,128)(2,1)S(1)}, u32[]{:S(2)}, u32[]{:S(2)}) collective-permute-start(bf16[512,256]{1,0:T(8,128)(2,1)S(1)} %get-tuple-element.66), channel_id=1, source_target_pairs={{0,8},{1,9},{2,10},{3,11},{4,12},{5,13},{6,14},{7,15},{8,0},{9,1},... | collective-permute-start | bytes 786440 | tf_op jit(solution)/shard_map/ppermute | solution.py:34
  70.1 7.5 %collective-permute-start.21 = (bf16[512,256]{1,0:T(8,128)(2,1)S(1)}, bf16[512,256]{1,0:T(8,128)(2,1)S(1)}, u32[]{:S(2)}, u32[]{:S(2)}) collective-permute-start(bf16[512,256]{1,0:T(8,128)(2,1)S(1)} %fusion.4), channel_id=1, source_target_pairs={{0,2},{1,5},{2,0},{3,7},{4,6},{5,1},{6,4},{7,3},{8,10},{9,13},{10,... | collective-permute-start | bytes 786440 | tf_op jit(solution)/shard_map/ppermute | solution.py:34
  71.6 12.1 %collective-permute-start.17 = (bf16[2,512,256]{2,1,0:T(8,128)(2,1)S(1)}, bf16[2,512,256]{2,1,0:T(8,128)(2,1)S(1)}, u32[]{:S(2)}, u32[]{:S(2)}) collective-permute-start(bf16[2,512,256]{2,1,0:T(8,128)(2,1)S(1)} %get-tuple-element.37), channel_id=1, source_target_pairs={{0,4},{1,3},{2,6},{3,1},{4,0},{5,7},{6,2},{7,5},{8,12},{9,11},{10,... | collective-permute-start | bytes 1572872 | tf_op jit(solution)/shard_map/ppermute | solution.py:34
  76.0 6.4 %collective-permute-start.24 = (bf16[512,256]{1,0:T(8,128)(2,1)S(1)}, bf16[512,256]{1,0:T(8,128)(2,1)S(1)}, u32[]{:S(2)}, u32[]{:S(2)}) collective-permute-start(bf16[512,256]{1,0:T(8,128)(2,1)S(1)} %fusion.13), channel_id=1, source_target_pairs={{0,2},{1,5},{2,0},{3,7},{4,6},{5,1},{6,4},{7,3},{8,10},{9,13},{10,... | collective-permute-start | bytes 786440 | tf_op jit(solution)/shard_map/ppermute | solution.py:34
  77.7 13.1 %copy-start.4 = (bf16[512,256]{1,0:T(8,128)(2,1)S(1)}, bf16[512,256]{1,0:T(8,128)(2,1)}, u32[]{:S(2)}) copy-start(bf16[512,256]{1,0:T(8,128)(2,1)} %param.7) | copy-start | bytes 786436
  77.7 10.3 %collective-permute-start.22 = (bf16[512,256]{1,0:T(8,128)(2,1)S(1)}, bf16[512,256]{1,0:T(8,128)(2,1)S(1)}, u32[]{:S(2)}, u32[]{:S(2)}) collective-permute-start(bf16[512,256]{1,0:T(8,128)(2,1)S(1)} %fusion.7), channel_id=1, source_target_pairs={{0,16},{1,17},{2,18},{3,19},{4,20},{5,21},{6,22},{7,23},{8,24},{9,... | collective-permute-start | bytes 786440 | tf_op jit(solution)/shard_map/ppermute | solution.py:34
  82.5 8.2 %collective-permute-start.25 = (bf16[512,256]{1,0:T(8,128)(2,1)S(1)}, bf16[512,256]{1,0:T(8,128)(2,1)S(1)}, u32[]{:S(2)}, u32[]{:S(2)}) collective-permute-start(bf16[512,256]{1,0:T(8,128)(2,1)S(1)} %fusion.2), channel_id=1, source_target_pairs={{0,8},{1,9},{2,10},{3,11},{4,12},{5,13},{6,14},{7,15},{8,0},{9,1},... | collective-permute-start | bytes 786440 | tf_op jit(solution)/shard_map/ppermute | solution.py:34
  83.9 6.8 %collective-permute-start.18 = (bf16[512,256]{1,0:T(8,128)(2,1)S(1)}, bf16[512,256]{1,0:T(8,128)(2,1)S(1)}, u32[]{:S(2)}, u32[]{:S(2)}) collective-permute-start(bf16[512,256]{1,0:T(8,128)(2,1)S(1)} %fusion.12), channel_id=1, source_target_pairs={{0,2},{1,5},{2,0},{3,7},{4,6},{5,1},{6,4},{7,3},{8,10},{9,13},{10,... | collective-permute-start | bytes 786440 | tf_op jit(solution)/shard_map/ppermute | solution.py:34
  91.8 11.6 %collective-permute-start.33 = (bf16[512,256]{1,0:T(8,128)(2,1)S(1)}, bf16[512,256]{1,0:T(8,128)(2,1)S(1)}, u32[]{:S(2)}, u32[]{:S(2)}) collective-permute-start(bf16[512,256]{1,0:T(8,128)(2,1)S(1)} %get-tuple-element.62.e0), channel_id=1, source_target_pairs={{0,16},{1,17},{2,18},{3,19},{4,20},{5,21},{6,22},{7,23},{8,24},{9,... | collective-permute-start | bytes 786440 | tf_op jit(solution)/shard_map/ppermute | solution.py:34
  94.7 10.1 %collective-permute-start.26 = (bf16[512,256]{1,0:T(8,128)(2,1)S(1)}, bf16[512,256]{1,0:T(8,128)(2,1)S(1)}, u32[]{:S(2)}, u32[]{:S(2)}) collective-permute-start(bf16[512,256]{1,0:T(8,128)(2,1)S(1)} %get-tuple-element.62.e0), channel_id=1, source_target_pairs={{0,2},{1,5},{2,0},{3,7},{4,6},{5,1},{6,4},{7,3},{8,10},{9,13},{10,... | collective-permute-start | bytes 786440 | tf_op jit(solution)/shard_map/ppermute | solution.py:34
  94.9 11.0 %collective-permute-start.29 = (bf16[512,256]{1,0:T(8,128)(2,1)S(1)}, bf16[512,256]{1,0:T(8,128)(2,1)S(1)}, u32[]{:S(2)}, u32[]{:S(2)}) collective-permute-start(bf16[512,256]{1,0:T(8,128)(2,1)S(1)} %get-tuple-element.62.e0), channel_id=1, source_target_pairs={{0,8},{1,9},{2,10},{3,11},{4,12},{5,13},{6,14},{7,15},{8,0},{9,1},... | collective-permute-start | bytes 786440 | tf_op jit(solution)/shard_map/ppermute | solution.py:34
  97.7 9.1 %collective-permute-start.27 = (bf16[512,256]{1,0:T(8,128)(2,1)S(1)}, bf16[512,256]{1,0:T(8,128)(2,1)S(1)}, u32[]{:S(2)}, u32[]{:S(2)}) collective-permute-start(bf16[512,256]{1,0:T(8,128)(2,1)S(1)} %get-tuple-element.62.e0), channel_id=1, source_target_pairs={{0,4},{1,3},{2,6},{3,1},{4,0},{5,7},{6,2},{7,5},{8,12},{9,11},{10,... | collective-permute-start | bytes 786440 | tf_op jit(solution)/shard_map/ppermute | solution.py:34
  103.4 9.2 %collective-permute-start.34 = (bf16[512,256]{1,0:T(8,128)(2,1)S(1)}, bf16[512,256]{1,0:T(8,128)(2,1)S(1)}, u32[]{:S(2)}, u32[]{:S(2)}) collective-permute-start(bf16[512,256]{1,0:T(8,128)(2,1)S(1)} %collective-permute-done.33.e0), channel_id=1, source_target_pairs={{0,2},{1,5},{2,0},{3,7},{4,6},{5,1},{6,4},{7,3},{8,10},{9,13},{10,... | collective-permute-start | bytes 786440 | tf_op jit(solution)/shard_map/ppermute | solution.py:34
  104.8 9.2 %collective-permute-start.30 = (bf16[512,256]{1,0:T(8,128)(2,1)S(1)}, bf16[512,256]{1,0:T(8,128)(2,1)S(1)}, u32[]{:S(2)}, u32[]{:S(2)}) collective-permute-start(bf16[512,256]{1,0:T(8,128)(2,1)S(1)} %collective-permute-done.26.e1), channel_id=1, source_target_pairs={{0,8},{1,9},{2,10},{3,11},{4,12},{5,13},{6,14},{7,15},{8,0},{9,1},... | collective-permute-start | bytes 786440 | tf_op jit(solution)/shard_map/ppermute | solution.py:34
  104.8 10.4 %collective-permute-start.28 = (bf16[512,256]{1,0:T(8,128)(2,1)S(1)}, bf16[512,256]{1,0:T(8,128)(2,1)S(1)}, u32[]{:S(2)}, u32[]{:S(2)}) collective-permute-start(bf16[512,256]{1,0:T(8,128)(2,1)S(1)} %collective-permute-done.26.e1), channel_id=1, source_target_pairs={{0,4},{1,3},{2,6},{3,1},{4,0},{5,7},{6,2},{7,5},{8,12},{9,11},{10,... | collective-permute-start | bytes 786440 | tf_op jit(solution)/shard_map/ppermute | solution.py:34
  105.9 10.2 %collective-permute-start.31 = (bf16[512,256]{1,0:T(8,128)(2,1)S(1)}, bf16[512,256]{1,0:T(8,128)(2,1)S(1)}, u32[]{:S(2)}, u32[]{:S(2)}) collective-permute-start(bf16[512,256]{1,0:T(8,128)(2,1)S(1)} %collective-permute-done.29.e0), channel_id=1, source_target_pairs={{0,4},{1,3},{2,6},{3,1},{4,0},{5,7},{6,2},{7,5},{8,12},{9,11},{10,... | collective-permute-start | bytes 786440 | tf_op jit(solution)/shard_map/ppermute | solution.py:34
  106.8 12.8 %collective-permute-start.37 = (bf16[512,256]{1,0:T(8,128)(2,1)S(1)}, bf16[512,256]{1,0:T(8,128)(2,1)S(1)}, u32[]{:S(2)}, u32[]{:S(2)}) collective-permute-start(bf16[512,256]{1,0:T(8,128)(2,1)S(1)} %collective-permute-done.33.e0), channel_id=1, source_target_pairs={{0,8},{1,9},{2,10},{3,11},{4,12},{5,13},{6,14},{7,15},{8,0},{9,1},... | collective-permute-start | bytes 786440 | tf_op jit(solution)/shard_map/ppermute | solution.py:34
  112.6 11.1 %collective-permute-start.38 = (bf16[512,256]{1,0:T(8,128)(2,1)S(1)}, bf16[512,256]{1,0:T(8,128)(2,1)S(1)}, u32[]{:S(2)}, u32[]{:S(2)}) collective-permute-start(bf16[512,256]{1,0:T(8,128)(2,1)S(1)} %collective-permute-done.34.e1), channel_id=1, source_target_pairs={{0,8},{1,9},{2,10},{3,11},{4,12},{5,13},{6,14},{7,15},{8,0},{9,1},... | collective-permute-start | bytes 786440 | tf_op jit(solution)/shard_map/ppermute | solution.py:34
  114.1 11.3 %collective-permute-start.32 = (bf16[512,256]{1,0:T(8,128)(2,1)S(1)}, bf16[512,256]{1,0:T(8,128)(2,1)S(1)}, u32[]{:S(2)}, u32[]{:S(2)}) collective-permute-start(bf16[512,256]{1,0:T(8,128)(2,1)S(1)} %collective-permute-done.30.e1), channel_id=1, source_target_pairs={{0,4},{1,3},{2,6},{3,1},{4,0},{5,7},{6,2},{7,5},{8,12},{9,11},{10,... | collective-permute-start | bytes 786440 | tf_op jit(solution)/shard_map/ppermute | solution.py:34
  115.2 11.5 %collective-permute-start.35 = (bf16[512,256]{1,0:T(8,128)(2,1)S(1)}, bf16[512,256]{1,0:T(8,128)(2,1)S(1)}, u32[]{:S(2)}, u32[]{:S(2)}) collective-permute-start(bf16[512,256]{1,0:T(8,128)(2,1)S(1)} %collective-permute-done.33.e0), channel_id=1, source_target_pairs={{0,4},{1,3},{2,6},{3,1},{4,0},{5,7},{6,2},{7,5},{8,12},{9,11},{10,... | collective-permute-start | bytes 786440 | tf_op jit(solution)/shard_map/ppermute | solution.py:34
  116.1 10.6 %collective-permute-start.36 = (bf16[512,256]{1,0:T(8,128)(2,1)S(1)}, bf16[512,256]{1,0:T(8,128)(2,1)S(1)}, u32[]{:S(2)}, u32[]{:S(2)}) collective-permute-start(bf16[512,256]{1,0:T(8,128)(2,1)S(1)} %collective-permute-done.34.e1), channel_id=1, source_target_pairs={{0,4},{1,3},{2,6},{3,1},{4,0},{5,7},{6,2},{7,5},{8,12},{9,11},{10,... | collective-permute-start | bytes 786440 | tf_op jit(solution)/shard_map/ppermute | solution.py:34
  119.7 9.2 %collective-permute-start.39 = (bf16[512,256]{1,0:T(8,128)(2,1)S(1)}, bf16[512,256]{1,0:T(8,128)(2,1)S(1)}, u32[]{:S(2)}, u32[]{:S(2)}) collective-permute-start(bf16[512,256]{1,0:T(8,128)(2,1)S(1)} %collective-permute-done.37.e0), channel_id=1, source_target_pairs={{0,4},{1,3},{2,6},{3,1},{4,0},{5,7},{6,2},{7,5},{8,12},{9,11},{10,... | collective-permute-start | bytes 786440 | tf_op jit(solution)/shard_map/ppermute | solution.py:34
  123.7 8.0 %collective-permute-start.40 = (bf16[512,256]{1,0:T(8,128)(2,1)S(1)}, bf16[512,256]{1,0:T(8,128)(2,1)S(1)}, u32[]{:S(2)}, u32[]{:S(2)}) collective-permute-start(bf16[512,256]{1,0:T(8,128)(2,1)S(1)} %collective-permute-done.38.e1), channel_id=1, source_target_pairs={{0,4},{1,3},{2,6},{3,1},{4,0},{5,7},{6,2},{7,5},{8,12},{9,11},{10,... | collective-permute-start | bytes 786440 | tf_op jit(solution)/shard_map/ppermute | solution.py:34
  134.8 6.4 %collective-permute-start.46 = (bf16[4096,128]{1,0:T(8,128)(2,1)S(1)}, bf16[4096,128]{1,0:T(8,128)(2,1)S(1)}, u32[]{:S(2)}, u32[]{:S(2)}) collective-permute-start(bf16[4096,128]{1,0:T(8,128)(2,1)S(1)} %encoder_send.1), channel_id=1, source_target_pairs={{0,1},{1,0},{2,3},{3,2},{4,5},{5,4},{6,7},{7,6},{8,9},{9,8},{10,11... | collective-permute-start | bytes 3145736 | tf_op jit(solution)/shard_map/ppermute | solution.py:50
  134.9 3.0 %collective-permute-start.41 = (bf16[128,1024]{1,0:T(8,128)(2,1)S(1)}, bf16[128,1024]{1,0:T(8,128)(2,1)S(1)}, u32[]{:S(2)}, u32[]{:S(2)}) collective-permute-start(bf16[128,1024]{1,0:T(8,128)(2,1)S(1)} %get-tuple-element.53), channel_id=1, source_target_pairs={{0,1},{1,0},{2,3},{3,2},{4,5},{5,4},{6,7},{7,6},{8,9},{9,8},{10,11... | collective-permute-start | bytes 786440 | tf_op jit(solution)/shard_map/ppermute | solution.py:50
  135.4 2.9 %collective-permute-start.42 = (bf16[128,1024]{1,0:T(8,128)(2,1)S(1)}, bf16[128,1024]{1,0:T(8,128)(2,1)S(1)}, u32[]{:S(2)}, u32[]{:S(2)}) collective-permute-start(bf16[128,1024]{1,0:T(8,128)(2,1)S(1)} %get-tuple-element.54), channel_id=1, source_target_pairs={{0,1},{1,0},{2,3},{3,2},{4,5},{5,4},{6,7},{7,6},{8,9},{9,8},{10,11... | collective-permute-start | bytes 786440 | tf_op jit(solution)/shard_map/ppermute | solution.py:50
  135.4 3.2 %collective-permute-start.43 = (bf16[128,1024]{1,0:T(8,128)(2,1)S(1)}, bf16[128,1024]{1,0:T(8,128)(2,1)S(1)}, u32[]{:S(2)}, u32[]{:S(2)}) collective-permute-start(bf16[128,1024]{1,0:T(8,128)(2,1)S(1)} %get-tuple-element.55), channel_id=1, source_target_pairs={{0,1},{1,0},{2,3},{3,2},{4,5},{5,4},{6,7},{7,6},{8,9},{9,8},{10,11... | collective-permute-start | bytes 786440 | tf_op jit(solution)/shard_map/ppermute | solution.py:50
  135.9 3.2 %collective-permute-start.44 = (bf16[128,1024]{1,0:T(8,128)(2,1)S(1)}, bf16[128,1024]{1,0:T(8,128)(2,1)S(1)}, u32[]{:S(2)}, u32[]{:S(2)}) collective-permute-start(bf16[128,1024]{1,0:T(8,128)(2,1)S(1)} %get-tuple-element.56), channel_id=1, source_target_pairs={{0,1},{1,0},{2,3},{3,2},{4,5},{5,4},{6,7},{7,6},{8,9},{9,8},{10,11... | collective-permute-start | bytes 786440 | tf_op jit(solution)/shard_map/ppermute | solution.py:50
  137.9 1.2 collective-permute-start.45
  (5 other events, 28.1 us)

commit v4 on v3

--- a/solution.py
+++ b/solution.py
@@ -267,7 +267,7 @@
     )
 
 
-def backward_body(last, across, order, act, e0, e1, e2, e3, w0, w1, w2, w3, dact, squares, *rest):
+def backward_body(last, across, order, act, e0, e1, e2, e3, w0, w1, w2, w3, dact, squares, earlier, *rest):
     rows, width = e0.shape
     half = act.shape[1] // 2
     total = dact[...]
@@ -300,7 +300,7 @@
         next_squares[...] = square
 
 
-def backward(order, across, act, blocks, weight, dact, squares, slope):
+def backward(order, across, act, blocks, weight, dact, squares, earlier, slope):
     rows, width = blocks[0].shape
     lats = act.shape[1]
     last = slope is not None
@@ -318,9 +318,9 @@
         dpre = (dact * slope).astype(BF16)
         squares = jnp.broadcast_to(jnp.sum(squares), (8, LANES))
         return keep, send, taken(dpre, side, half, 1), taken(dpre, 1 - side, half, 1), squares
-    operands = [act] + list(blocks) + [weight] * 4 + [dact, squares]
+    operands = [act] + list(blocks) + [weight] * 4 + [dact, squares, earlier]
     specs = [whole(act.shape)] + [whole((rows, width))] * 4 + column_specs(lats, width)
-    specs += [whole(dact.shape), whole(squares.shape)]
+    specs += [whole(dact.shape), whole(squares.shape), ANYWHERE]
     if last:
         operands.append(slope)
         specs.append(whole(slope.shape))
@@ -371,55 +371,31 @@
     )
 
 
-def encoder_send_body(slots, width, across, order, mine, dpre, out):
-    d = dpre[...]
+def encoder_gradient_body(slots, width, across, order, mine, theirs, dpre, got, out):
+    d, g = dpre[...], got[...]
     for s in range(slots):
         for m in range(4):
             here = jnp.dot(mine[4 * s + m], d, preferred_element_type=F32)
-            at = (4 * s + across[m]) * width
-            out[at:at + width, :] = here.astype(BF16)
-
-
-def encoder_send(order, across, mine, dpre, width):
-    slots = mine.shape[0] // 4
-    rows, half = dpre.shape
-    operands = [mine, dpre]
-    shape = (4 * slots * width, half)
-    if plain(width):
-        blocks = [mine[4 * s + m] for s in range(slots) for m in across]
-        return jnp.dot(jnp.concatenate(blocks), dpre, preferred_element_type=F32).astype(BF16)
-    return call(
-        functools.partial(encoder_send_body, slots, width, across), order, operands,
-        [whole(o.shape) for o in operands], jax.ShapeDtypeStruct(shape, BF16), whole(shape),
-        2 * shape[0] * rows * half, 2 * shape[0] * rows + 2 * shape[0] * half, "encoder_send",
-    )
-
-
-def encoder_gradient_body(slots, width, order, mine, dpre, got, out):
-    d = dpre[...]
-    for s in range(slots):
-        for m in range(4):
-            here = jnp.dot(mine[4 * s + m], d, preferred_element_type=F32)
-            at = (4 * s + m) * width
-            there = pl.ds(pl.multiple_of(order[4 * s + m] * width, width), width)
-            out[there, :] = here + got[at:at + width, :].astype(F32)
-
-
-def encoder_gradient(order, mine, dpre, got, width):
-    slots = mine.shape[0] // 4
-    rows, half = dpre.shape
-    operands = [mine, dpre, got]
-    shape = (4 * slots * width, half)
+            here += jnp.dot(theirs[4 * s + across[m]], g, preferred_element_type=F32)
+            out[pl.ds(pl.multiple_of(order[4 * s + m] * width, width), width), :] = here
+
+
+def encoder_gradient(order, across, mine, theirs, dpre, got):
+    count, width, rows = mine.shape
+    slots, half = count // 4, dpre.shape[1]
+    operands = [mine, theirs, dpre, got]
+    shape = (count * width, half)
     if plain(width):
         out = jnp.zeros(shape, F32)
-        total = jnp.dot(mine.reshape(shape[0], rows), dpre, preferred_element_type=F32) + got.astype(F32)
-        for b in range(4 * slots):
-            out = lax.dynamic_update_slice_in_dim(out, total[b * width:(b + 1) * width], order[b] * width, 0)
+        for b in range(count):
+            block = jnp.dot(mine[b], dpre, preferred_element_type=F32)
+            block += jnp.dot(theirs[b - b % 4 + across[b % 4]], got, preferred_element_type=F32)
+            out = lax.dynamic_update_slice_in_dim(out, block, order[b] * width, 0)
         return out
     return call(
-        functools.partial(encoder_gradient_body, slots, width), order, operands,
+        functools.partial(encoder_gradient_body, slots, width, across), order, operands,
         [whole(o.shape) for o in operands], jax.ShapeDtypeStruct(shape, F32), whole(shape),
-        2 * shape[0] * rows * half, 2 * shape[0] * rows + 6 * shape[0] * half, "encoder_gradient",
+        4 * shape[0] * rows * half, 4 * shape[0] * (rows + half), "encoder_gradient",
     )
 
 
@@ -435,6 +411,7 @@
     (pre_act,) = encode(grid.every[:-4], centered[:-4], enc_weight, enc_bias[None, :], None)
     act, slope = encode(grid.every[-4:], centered[-4:], enc_weight, pre_act, active_blocks.T)
     turned = turn(grid.every, centered)
+    theirs = grid.swap_core(turned)
 
     def part(s, earlier):
         earlier = [] if earlier is None else [earlier]
@@ -451,7 +428,7 @@
     for s, blocks in enumerate(grid.gather(error_local.astype(BF16))):
         order = grid.order[s]
         keep, send, *state[:] = backward(
-            order, grid.across, act, blocks, near, *state, slope if s == slots - 1 else None
+            order, grid.across, act, blocks, near, *state, theirs if s == 0 else order, slope if s == slots - 1 else None
         )
         keeps.append(keep)
         gots.append(grid.swap_core(send))
@@ -464,12 +441,12 @@
         step *= 2
         if step < dp:
             square = square + square_got
-    got = grid.swap_core(encoder_send(grid.every, grid.across, turned, other, width))
+    got = grid.swap_core(other)
     grad_dec, mean = decoder_gradient(
         grid.every, keeps, gots, width, (square, square_got), rows * dp * width * lat
     )
     mse_loss = mean.reshape(())
-    grad_enc = encoder_gradient(grid.every, turned, mine, got, width)
+    grad_enc = encoder_gradient(grid.every, grid.across, turned, theirs, mine, got)
 
     return (error_local, mse_loss, grid.spread(grad_dec, 0), grid.spread(grad_enc, 1))
 

time: 144 us -> 142 us (0.986)
  waiting for transfers between devices: 58.4 us -> 56.2 us
    pallas_call x15 -> x14, Pallas kernels: 28.2 us -> 27.5 us  [call(): pl.pallas_call(body, grid_spec=pltpu.PrefetchScalarGridSpec(num_scalar_pr...]
  transfers between devices with their start and end apart: 47 -> 48, of which waited for: 25 -> 25; matrix products, arithmetic and copies ran while one was open for 1% -> 2% of each run, Pallas kernels for 13% -> 16%
where the time goes in v4:
time: 142 us
  waiting for transfers between devices  56.2 us (40%)
  starting transfers between devices  51.3 us (36%)
  Pallas kernels  27.5 us (19%)
  other arithmetic  3.86 us (3%)
  local copies, waits for them, and re-layouts  1.75 us (1%)
    ppermute x41, waiting for transfers between devices, swap(): return lax.ppermute(x, ('lat', 'dp'), pairs)  55 us
    ppermute x41, starting transfers between devices, swap(): return lax.ppermute(x, ('lat', 'dp'), pairs)  49.8 us
    pallas_call x14, Pallas kernels, call(): pl.pallas_call(body, grid_spec=pltpu.PrefetchScalarGridSpec(num_scalar_pr...  27.5 us
  transfers between devices with their start and end apart: 48, of which 25 were waited for; matrix products, arithmetic and copies ran while one was open for 2% of the time, Pallas kernels for 16%

profile of v4, /device:TPU:0, one launch (start us, length us, event | category | flops | bytes accessed | tf_op | source)
XLA Modules:
  0.0 141.5 jit_solution(10725138138277195533)
XLA Ops:
  2.3 4.1 %collective-permute-start = (bf16[512,256]{1,0:T(8,128)(2,1)S(1)}, bf16[512,256]{1,0:T(8,128)(2,1)S(1)}, u32[]{:S(2)}, u32[]{:S(2)}) collective-permute-start(bf16[512,256]{1,0:T(8,128)(2,1)S(1)} %fusion.refs_0_), channel_id=1, source_target_pairs={{0,16},{1,17},{2,18},{3,19},{4,20},{5,21},{6,22},{7,23},{8,24},{9,... | collective-permute-start | bytes 786440 | tf_op jit(solution)/shard_map/ppermute | solution.py:34
  6.4 1.5 %collective-permute-start.6 = (bf16[512,256]{1,0:T(8,128)(2,1)S(1)}, bf16[512,256]{1,0:T(8,128)(2,1)S(1)}, u32[]{:S(2)}, u32[]{:S(2)}) collective-permute-start(bf16[512,256]{1,0:T(8,128)(2,1)S(1)} %fusion.refs_0_), channel_id=1, source_target_pairs={{0,2},{1,5},{2,0},{3,7},{4,6},{5,1},{6,4},{7,3},{8,10},{9,13},{10,... | collective-permute-start | bytes 786440 | tf_op jit(solution)/shard_map/ppermute | solution.py:34
  7.9 1.5 %collective-permute-start.7 = (bf16[512,256]{1,0:T(8,128)(2,1)S(1)}, bf16[512,256]{1,0:T(8,128)(2,1)S(1)}, u32[]{:S(2)}, u32[]{:S(2)}) collective-permute-start(bf16[512,256]{1,0:T(8,128)(2,1)S(1)} %fusion.refs_0_), channel_id=1, source_target_pairs={{0,4},{1,3},{2,6},{3,1},{4,0},{5,7},{6,2},{7,5},{8,12},{9,11},{10,... | collective-permute-start | bytes 786440 | tf_op jit(solution)/shard_map/ppermute | solution.py:34
  9.4 1.6 %collective-permute-start.9 = (bf16[512,256]{1,0:T(8,128)(2,1)S(1)}, bf16[512,256]{1,0:T(8,128)(2,1)S(1)}, u32[]{:S(2)}, u32[]{:S(2)}) collective-permute-start(bf16[512,256]{1,0:T(8,128)(2,1)S(1)} %fusion.refs_0_), channel_id=1, source_target_pairs={{0,8},{1,9},{2,10},{3,11},{4,12},{5,13},{6,14},{7,15},{8,0},{9,1},... | collective-permute-start | bytes 786440 | tf_op jit(solution)/shard_map/ppermute | solution.py:34
  11.0 7.4 %collective-permute-done.refs_8_ = bf16[512,256]{1,0:T(8,128)(2,1)S(1)} collective-permute-done((bf16[512,256]{1,0:T(8,128)(2,1)S(1)}, bf16[512,256]{1,0:T(8,128)(2,1)S(1)}, u32[]{:S(2)}, u32[]{:S(2)}) %collective-permute-start) | collective-permute-done | bytes 262176 | tf_op jit(solution)/shard_map/ppermute | solution.py:34
  18.4 1.5 %collective-permute-start.2 = (bf16[512,256]{1,0:T(8,128)(2,1)S(1)}, bf16[512,256]{1,0:T(8,128)(2,1)S(1)}, u32[]{:S(2)}, u32[]{:S(2)}) collective-permute-start(bf16[512,256]{1,0:T(8,128)(2,1)S(1)} %collective-permute-done.refs_8_), channel_id=1, source_target_pairs={{0,2},{1,5},{2,0},{3,7},{4,6},{5,1},{6,4},{7,3},{8,10},{9,13},{10,... | collective-permute-start | bytes 786440 | tf_op jit(solution)/shard_map/ppermute | solution.py:34
  20.6 1.5 %collective-permute-start.8 = (bf16[512,256]{1,0:T(8,128)(2,1)S(1)}, bf16[512,256]{1,0:T(8,128)(2,1)S(1)}, u32[]{:S(2)}, u32[]{:S(2)}) collective-permute-start(bf16[512,256]{1,0:T(8,128)(2,1)S(1)} %collective-permute-done.6.refs_1_), channel_id=1, source_target_pairs={{0,4},{1,3},{2,6},{3,1},{4,0},{5,7},{6,2},{7,5},{8,12},{9,11},{10,... | collective-permute-start | bytes 786440 | tf_op jit(solution)/shard_map/ppermute | solution.py:34
  22.1 1.5 %collective-permute-start.10 = (bf16[512,256]{1,0:T(8,128)(2,1)S(1)}, bf16[512,256]{1,0:T(8,128)(2,1)S(1)}, u32[]{:S(2)}, u32[]{:S(2)}) collective-permute-start(bf16[512,256]{1,0:T(8,128)(2,1)S(1)} %collective-permute-done.6.refs_1_), channel_id=1, source_target_pairs={{0,8},{1,9},{2,10},{3,11},{4,12},{5,13},{6,14},{7,15},{8,0},{9,1},... | collective-permute-start | bytes 786440 | tf_op jit(solution)/shard_map/ppermute | solution.py:34
  24.1 2.9 %collective-permute-done.2.refs_9_ = bf16[512,256]{1,0:T(8,128)(2,1)S(1)} collective-permute-done((bf16[512,256]{1,0:T(8,128)(2,1)S(1)}, bf16[512,256]{1,0:T(8,128)(2,1)S(1)}, u32[]{:S(2)}, u32[]{:S(2)}) %collective-permute-start.2) | collective-permute-done | bytes 262176 | tf_op jit(solution)/shard_map/ppermute | solution.py:34
  27.9 1.3 collective-permute-done.1.refs_0_.refs_12_
  29.2 1.5 %collective-permute-start.13 = (bf16[512,256]{1,0:T(8,128)(2,1)S(1)}, bf16[512,256]{1,0:T(8,128)(2,1)S(1)}, u32[]{:S(2)}, u32[]{:S(2)}) collective-permute-start(bf16[512,256]{1,0:T(8,128)(2,1)S(1)} %collective-permute-done.refs_8_), channel_id=1, source_target_pairs={{0,4},{1,3},{2,6},{3,1},{4,0},{5,7},{6,2},{7,5},{8,12},{9,11},{10,... | collective-permute-start | bytes 786440 | tf_op jit(solution)/shard_map/ppermute | solution.py:34
  31.2 3.6 %collective-permute-done.10.refs_5_ = bf16[512,256]{1,0:T(8,128)(2,1)S(1)} collective-permute-done((bf16[512,256]{1,0:T(8,128)(2,1)S(1)}, bf16[512,256]{1,0:T(8,128)(2,1)S(1)}, u32[]{:S(2)}, u32[]{:S(2)}) %collective-permute-start.10) | collective-permute-done | bytes 262176 | tf_op jit(solution)/shard_map/ppermute | solution.py:34
  36.1 1.6 %copy-done.1 = bf16[256,4096]{1,0:T(8,128)(2,1)S(1)} copy-done((bf16[256,4096]{1,0:T(8,128)(2,1)S(1)}, bf16[256,4096]{1,0:T(8,128)(2,1)}, u32[]{:S(2)}) %copy-start.1) | copy-done | bytes 2097176
  41.2 5.3 %encode.2.refs_5_ = f32[512,256]{1,0:T(8,128)S(1)} custom-call(s32[12]{0:T(128)S(1)} %pad_add_fusion.2.order, bf16[512,256]{1,0:T(8,128)(2,1)S(1)} %fusion.refs_0_, bf16[512,256]{1,0:T(8,128)(2,1)S(1)} %collective-permute-done.6.refs_1_, bf16[512,256]{1,0:T(8,128)(2,1)S(1)} %collective-permute-done.7.refs_2_, ...), custom_call_target="tpu_custom_call" | custom-call | flops 805306368 | bytes 5767168 | tf_op jit(solution)/shard_map/encode/pallas_call | solution.py:126
  47.7 2.4 %encode.3 = (bf16[512,256]{1,0:T(8,128)(2,1)S(1)}, f32[512,256]{1,0:T(8,128)S(1)}) custom-call(s32[4]{0:T(128)S(1)} %get-tuple-element.70.order, bf16[512,256]{1,0:T(8,128)(2,1)S(1)} %collective-permute-done.1.refs_0_.refs_12_, bf16[512,256]{1,0:T(8,128)(2,1)S(1)} %collective-permute-done.3.refs_1_.refs_13_, ...), custom_call_target="tpu_custom_call" | custom-call | flops 268435456 | bytes 2621440 | tf_op jit(solution)/shard_map/encode/pallas_call | solution.py:126
  52.1 3.6 %turn.1.rest_1_.mine = bf16[16,256,512]{2,1,0:T(8,128)(2,1)S(1)} custom-call(s32[16]{0:T(128)S(1)} %pad_add_fusion.3.order, bf16[512,256]{1,0:T(8,128)(2,1)S(1)} %fusion.refs_0_, bf16[512,256]{1,0:T(8,128)(2,1)S(1)} %collective-permute-done.6.refs_1_, bf16[512,256]{1,0:T(8,128)(2,1)S(1)} %collective-permute-done.7.refs_2_, ...), custom_call_target="tpu_custom_call" | custom-call | bytes 8388608 | tf_op jit(solution)/shard_map/turn/pallas_call | solution.py:126
  56.8 1.3 collective-permute-start.19
  58.1 2.3 %collective-permute-done.15.rest_0_ = bf16[2,512,256]{2,1,0:T(8,128)(2,1)S(1)} collective-permute-done((bf16[2,512,256]{2,1,0:T(8,128)(2,1)S(1)}, bf16[2,512,256]{2,1,0:T(8,128)(2,1)S(1)}, u32[]{:S(2)}, u32[]{:S(2)}) %collective-permute-start.15) | collective-permute-done | bytes 524320 | tf_op jit(solution)/shard_map/ppermute | solution.py:34
  63.1 1.5 %collective-permute-start.20 = (bf16[512,256]{1,0:T(8,128)(2,1)S(1)}, bf16[512,256]{1,0:T(8,128)(2,1)S(1)}, u32[]{:S(2)}, u32[]{:S(2)}) collective-permute-start(bf16[512,256]{1,0:T(8,128)(2,1)S(1)} %get-tuple-element.66), channel_id=1, source_target_pairs={{0,8},{1,9},{2,10},{3,11},{4,12},{5,13},{6,14},{7,15},{8,0},{9,1},... | collective-permute-start | bytes 786440 | tf_op jit(solution)/shard_map/ppermute | solution.py:34
  64.5 1.5 %collective-permute-done.19 = bf16[2,512,256]{2,1,0:T(8,128)(2,1)S(1)} collective-permute-done((bf16[2,512,256]{2,1,0:T(8,128)(2,1)S(1)}, bf16[2,512,256]{2,1,0:T(8,128)(2,1)S(1)}, u32[]{:S(2)}, u32[]{:S(2)}) %collective-permute-start.19) | collective-permute-done | bytes 524320 | tf_op jit(solution)/shard_map/ppermute | solution.py:34
  66.2 5.0 %collective-permute-done.16.rest_0_ = bf16[512,256]{1,0:T(8,128)(2,1)S(1)} collective-permute-done((bf16[512,256]{1,0:T(8,128)(2,1)S(1)}, bf16[512,256]{1,0:T(8,128)(2,1)S(1)}, u32[]{:S(2)}, u32[]{:S(2)}) %collective-permute-start.16) | collective-permute-done | bytes 262176 | tf_op jit(solution)/shard_map/ppermute | solution.py:34
  72.8 1.7 %collective-permute-start.17 = (bf16[2,512,256]{2,1,0:T(8,128)(2,1)S(1)}, bf16[2,512,256]{2,1,0:T(8,128)(2,1)S(1)}, u32[]{:S(2)}, u32[]{:S(2)}) collective-permute-start(bf16[2,512,256]{2,1,0:T(8,128)(2,1)S(1)} %get-tuple-element.37), channel_id=1, source_target_pairs={{0,4},{1,3},{2,6},{3,1},{4,0},{5,7},{6,2},{7,5},{8,12},{9,11},{10,... | collective-permute-start | bytes 1572872 | tf_op jit(solution)/shard_map/ppermute | solution.py:34
  76.0 3.6 %collective-permute-done.21 = bf16[512,256]{1,0:T(8,128)(2,1)S(1)} collective-permute-done((bf16[512,256]{1,0:T(8,128)(2,1)S(1)}, bf16[512,256]{1,0:T(8,128)(2,1)S(1)}, u32[]{:S(2)}, u32[]{:S(2)}) %collective-permute-start.21) | collective-permute-done | bytes 262176 | tf_op jit(solution)/shard_map/ppermute | solution.py:34
  79.7 2.4 %collective-permute-start.22 = (bf16[512,256]{1,0:T(8,128)(2,1)S(1)}, bf16[512,256]{1,0:T(8,128)(2,1)S(1)}, u32[]{:S(2)}, u32[]{:S(2)}) collective-permute-start(bf16[512,256]{1,0:T(8,128)(2,1)S(1)} %fusion.7), channel_id=1, source_target_pairs={{0,16},{1,17},{2,18},{3,19},{4,20},{5,21},{6,22},{7,23},{8,24},{9,... | collective-permute-start | bytes 786440 | tf_op jit(solution)/shard_map/ppermute | solution.py:34
  82.5 1.5 %collective-permute-start.25 = (bf16[512,256]{1,0:T(8,128)(2,1)S(1)}, bf16[512,256]{1,0:T(8,128)(2,1)S(1)}, u32[]{:S(2)}, u32[]{:S(2)}) collective-permute-start(bf16[512,256]{1,0:T(8,128)(2,1)S(1)} %fusion.2), channel_id=1, source_target_pairs={{0,8},{1,9},{2,10},{3,11},{4,12},{5,13},{6,14},{7,15},{8,0},{9,1},... | collective-permute-start | bytes 786440 | tf_op jit(solution)/shard_map/ppermute | solution.py:34
  85.3 4.7 %collective-permute-done.22 = bf16[512,256]{1,0:T(8,128)(2,1)S(1)} collective-permute-done((bf16[512,256]{1,0:T(8,128)(2,1)S(1)}, bf16[512,256]{1,0:T(8,128)(2,1)S(1)}, u32[]{:S(2)}, u32[]{:S(2)}) %collective-permute-start.22) | collective-permute-done | bytes 262176 | tf_op jit(solution)/shard_map/ppermute | solution.py:34
  90.0 1.3 collective-permute-done.25
  92.9 2.5 %collective-permute-start.34 = (bf16[512,256]{1,0:T(8,128)(2,1)S(1)}, bf16[512,256]{1,0:T(8,128)(2,1)S(1)}, u32[]{:S(2)}, u32[]{:S(2)}) collective-permute-start(bf16[512,256]{1,0:T(8,128)(2,1)S(1)} %get-tuple-element.62.e0), channel_id=1, source_target_pairs={{0,16},{1,17},{2,18},{3,19},{4,20},{5,21},{6,22},{7,23},{8,24},{9,... | collective-permute-start | bytes 786440 | tf_op jit(solution)/shard_map/ppermute | solution.py:34
  96.7 2.5 %collective-permute-start.30 = (bf16[512,256]{1,0:T(8,128)(2,1)S(1)}, bf16[512,256]{1,0:T(8,128)(2,1)S(1)}, u32[]{:S(2)}, u32[]{:S(2)}) collective-permute-start(bf16[512,256]{1,0:T(8,128)(2,1)S(1)} %get-tuple-element.62.e0), channel_id=1, source_target_pairs={{0,8},{1,9},{2,10},{3,11},{4,12},{5,13},{6,14},{7,15},{8,0},{9,1},... | collective-permute-start | bytes 786440 | tf_op jit(solution)/shard_map/ppermute | solution.py:34
  99.2 1.2 collective-permute-done.26.e1
  100.4 1.3 collective-permute-start.28
  101.7 2.3 %collective-permute-done.34.e0 = bf16[512,256]{1,0:T(8,128)(2,1)S(1)} collective-permute-done((bf16[512,256]{1,0:T(8,128)(2,1)S(1)}, bf16[512,256]{1,0:T(8,128)(2,1)S(1)}, u32[]{:S(2)}, u32[]{:S(2)}) %collective-permute-start.34) | collective-permute-done | bytes 262176 | tf_op jit(solution)/shard_map/ppermute | solution.py:34
  105.6 1.4 %collective-permute-done.30.e0 = bf16[512,256]{1,0:T(8,128)(2,1)S(1)} collective-permute-done((bf16[512,256]{1,0:T(8,128)(2,1)S(1)}, bf16[512,256]{1,0:T(8,128)(2,1)S(1)}, u32[]{:S(2)}, u32[]{:S(2)}) %collective-permute-start.30) | collective-permute-done | bytes 262176 | tf_op jit(solution)/shard_map/ppermute | solution.py:34
  107.0 1.9 %collective-permute-done.28.e3 = bf16[512,256]{1,0:T(8,128)(2,1)S(1)} collective-permute-done((bf16[512,256]{1,0:T(8,128)(2,1)S(1)}, bf16[512,256]{1,0:T(8,128)(2,1)S(1)}, u32[]{:S(2)}, u32[]{:S(2)}) %collective-permute-start.28) | collective-permute-done | bytes 262176 | tf_op jit(solution)/shard_map/ppermute | solution.py:34
  109.0 1.4 %collective-permute-done.35.e1 = bf16[512,256]{1,0:T(8,128)(2,1)S(1)} collective-permute-done((bf16[512,256]{1,0:T(8,128)(2,1)S(1)}, bf16[512,256]{1,0:T(8,128)(2,1)S(1)}, u32[]{:S(2)}, u32[]{:S(2)}) %collective-permute-start.35) | collective-permute-done | bytes 262176 | tf_op jit(solution)/shard_map/ppermute | solution.py:34
  110.4 1.6 %collective-permute-start.39 = (bf16[512,256]{1,0:T(8,128)(2,1)S(1)}, bf16[512,256]{1,0:T(8,128)(2,1)S(1)}, u32[]{:S(2)}, u32[]{:S(2)}) collective-permute-start(bf16[512,256]{1,0:T(8,128)(2,1)S(1)} %collective-permute-done.35.e1), channel_id=1, source_target_pairs={{0,8},{1,9},{2,10},{3,11},{4,12},{5,13},{6,14},{7,15},{8,0},{9,1},... | collective-permute-start | bytes 786440 | tf_op jit(solution)/shard_map/ppermute | solution.py:34
  112.0 1.8 %collective-permute-done.31.e1 = bf16[512,256]{1,0:T(8,128)(2,1)S(1)} collective-permute-done((bf16[512,256]{1,0:T(8,128)(2,1)S(1)}, bf16[512,256]{1,0:T(8,128)(2,1)S(1)}, u32[]{:S(2)}, u32[]{:S(2)}) %collective-permute-start.31) | collective-permute-done | bytes 262176 | tf_op jit(solution)/shard_map/ppermute | solution.py:34
  114.3 1.5 %collective-permute-start.36 = (bf16[512,256]{1,0:T(8,128)(2,1)S(1)}, bf16[512,256]{1,0:T(8,128)(2,1)S(1)}, u32[]{:S(2)}, u32[]{:S(2)}) collective-permute-start(bf16[512,256]{1,0:T(8,128)(2,1)S(1)} %collective-permute-done.34.e0), channel_id=1, source_target_pairs={{0,4},{1,3},{2,6},{3,1},{4,0},{5,7},{6,2},{7,5},{8,12},{9,11},{10,... | collective-permute-start | bytes 786440 | tf_op jit(solution)/shard_map/ppermute | solution.py:34
  115.8 3.6 %collective-permute-done.38.e0 = bf16[512,256]{1,0:T(8,128)(2,1)S(1)} collective-permute-done((bf16[512,256]{1,0:T(8,128)(2,1)S(1)}, bf16[512,256]{1,0:T(8,128)(2,1)S(1)}, u32[]{:S(2)}, u32[]{:S(2)}) %collective-permute-start.38) | collective-permute-done | bytes 262176 | tf_op jit(solution)/shard_map/ppermute | solution.py:34
  119.9 2.8 %collective-permute-done.39.e1 = bf16[512,256]{1,0:T(8,128)(2,1)S(1)} collective-permute-done((bf16[512,256]{1,0:T(8,128)(2,1)S(1)}, bf16[512,256]{1,0:T(8,128)(2,1)S(1)}, u32[]{:S(2)}, u32[]{:S(2)}) %collective-permute-start.39) | collective-permute-done | bytes 262176 | tf_op jit(solution)/shard_map/ppermute | solution.py:34
  123.2 1.5 %collective-permute-start.41 = (bf16[512,256]{1,0:T(8,128)(2,1)S(1)}, bf16[512,256]{1,0:T(8,128)(2,1)S(1)}, u32[]{:S(2)}, u32[]{:S(2)}) collective-permute-start(bf16[512,256]{1,0:T(8,128)(2,1)S(1)} %collective-permute-done.39.e1), channel_id=1, source_target_pairs={{0,4},{1,3},{2,6},{3,1},{4,0},{5,7},{6,2},{7,5},{8,12},{9,11},{10,... | collective-permute-start | bytes 786440 | tf_op jit(solution)/shard_map/ppermute | solution.py:34
  124.8 1.3 backward.4
  126.2 1.3 backward.5
  128.1 1.3 backward.6
  129.5 2.4 %collective-permute-done.41.e3 = bf16[512,256]{1,0:T(8,128)(2,1)S(1)} collective-permute-done((bf16[512,256]{1,0:T(8,128)(2,1)S(1)}, bf16[512,256]{1,0:T(8,128)(2,1)S(1)}, u32[]{:S(2)}, u32[]{:S(2)}) %collective-permute-start.41) | collective-permute-done | bytes 262176 | tf_op jit(solution)/shard_map/ppermute | solution.py:34
  131.9 1.3 backward.7
  135.2 4.2 %encoder_gradient.1 = f32[4096,128]{1,0:T(8,128)} custom-call(s32[16]{0:T(128)S(1)} %pad_add_fusion.3.order, bf16[16,256,512]{2,1,0:T(8,128)(2,1)S(1)} %turn.1.rest_1_.mine, bf16[16,256,512]{2,1,0:T(8,128)(2,1)S(1)} %collective-permute-done.29.earlier.theirs, bf16[512,128]{1,0:T(8,128)(2,1)S(1)} %get-tuple-element.60.dpre, ...), custom_call_target="tpu_custom_call" | custom-call | flops 1073741824 | bytes 10485760 | tf_op jit(solution)/shard_map/encoder_gradient/pallas_call | solution.py:126
  139.4 2.1 %decoder_gradient.1 = (f32[128,4096]{1,0:T(8,128)}, f32[1,1]{1,0:T(1,128)}) custom-call(s32[16]{0:T(128)S(1)} %pad_add_fusion.3.order, f32[128,1024]{1,0:T(8,128)S(1)} %get-tuple-element.42.refs_0_, f32[128,1024]{1,0:T(8,128)S(1)} %get-tuple-element.45.refs_1_, f32[128,1024]{1,0:T(8,128)S(1)} %get-tuple-element.48.refs_2_, ...), custom_call_target="tpu_custom_call" | custom-call | flops 524288 | bytes 5242880 | tf_op jit(solution)/shard_map/decoder_gradient/pallas_call | solution.py:126
  (96 shorter events, 29.8 us)
Async XLA Ops:
  2.3 16.1 %collective-permute-start = (bf16[512,256]{1,0:T(8,128)(2,1)S(1)}, bf16[512,256]{1,0:T(8,128)(2,1)S(1)}, u32[]{:S(2)}, u32[]{:S(2)}) collective-permute-start(bf16[512,256]{1,0:T(8,128)(2,1)S(1)} %fusion.refs_0_), channel_id=1, source_target_pairs={{0,16},{1,17},{2,18},{3,19},{4,20},{5,21},{6,22},{7,23},{8,24},{9,... | collective-permute-start | bytes 786440 | tf_op jit(solution)/shard_map/ppermute | solution.py:34
  6.4 14.2 %collective-permute-start.6 = (bf16[512,256]{1,0:T(8,128)(2,1)S(1)}, bf16[512,256]{1,0:T(8,128)(2,1)S(1)}, u32[]{:S(2)}, u32[]{:S(2)}) collective-permute-start(bf16[512,256]{1,0:T(8,128)(2,1)S(1)} %fusion.refs_0_), channel_id=1, source_target_pairs={{0,2},{1,5},{2,0},{3,7},{4,6},{5,1},{6,4},{7,3},{8,10},{9,13},{10,... | collective-permute-start | bytes 786440 | tf_op jit(solution)/shard_map/ppermute | solution.py:34
  7.9 14.2 %collective-permute-start.7 = (bf16[512,256]{1,0:T(8,128)(2,1)S(1)}, bf16[512,256]{1,0:T(8,128)(2,1)S(1)}, u32[]{:S(2)}, u32[]{:S(2)}) collective-permute-start(bf16[512,256]{1,0:T(8,128)(2,1)S(1)} %fusion.refs_0_), channel_id=1, source_target_pairs={{0,4},{1,3},{2,6},{3,1},{4,0},{5,7},{6,2},{7,5},{8,12},{9,11},{10,... | collective-permute-start | bytes 786440 | tf_op jit(solution)/shard_map/ppermute | solution.py:34
  9.4 14.2 %collective-permute-start.9 = (bf16[512,256]{1,0:T(8,128)(2,1)S(1)}, bf16[512,256]{1,0:T(8,128)(2,1)S(1)}, u32[]{:S(2)}, u32[]{:S(2)}) collective-permute-start(bf16[512,256]{1,0:T(8,128)(2,1)S(1)} %fusion.refs_0_), channel_id=1, source_target_pairs={{0,8},{1,9},{2,10},{3,11},{4,12},{5,13},{6,14},{7,15},{8,0},{9,1},... | collective-permute-start | bytes 786440 | tf_op jit(solution)/shard_map/ppermute | solution.py:34
  18.4 8.6 %collective-permute-start.2 = (bf16[512,256]{1,0:T(8,128)(2,1)S(1)}, bf16[512,256]{1,0:T(8,128)(2,1)S(1)}, u32[]{:S(2)}, u32[]{:S(2)}) collective-permute-start(bf16[512,256]{1,0:T(8,128)(2,1)S(1)} %collective-permute-done.refs_8_), channel_id=1, source_target_pairs={{0,2},{1,5},{2,0},{3,7},{4,6},{5,1},{6,4},{7,3},{8,10},{9,13},{10,... | collective-permute-start | bytes 786440 | tf_op jit(solution)/shard_map/ppermute | solution.py:34
  20.0 9.2 %collective-permute-start.1 = (bf16[512,256]{1,0:T(8,128)(2,1)S(1)}, bf16[512,256]{1,0:T(8,128)(2,1)S(1)}, u32[]{:S(2)}, u32[]{:S(2)}) collective-permute-start(bf16[512,256]{1,0:T(8,128)(2,1)S(1)} %collective-permute-done.refs_8_), channel_id=1, source_target_pairs={{0,8},{1,9},{2,10},{3,11},{4,12},{5,13},{6,14},{7,15},{8,0},{9,1},... | collective-permute-start | bytes 786440 | tf_op jit(solution)/shard_map/ppermute | solution.py:34
  20.6 10.2 %collective-permute-start.8 = (bf16[512,256]{1,0:T(8,128)(2,1)S(1)}, bf16[512,256]{1,0:T(8,128)(2,1)S(1)}, u32[]{:S(2)}, u32[]{:S(2)}) collective-permute-start(bf16[512,256]{1,0:T(8,128)(2,1)S(1)} %collective-permute-done.6.refs_1_), channel_id=1, source_target_pairs={{0,4},{1,3},{2,6},{3,1},{4,0},{5,7},{6,2},{7,5},{8,12},{9,11},{10,... | collective-permute-start | bytes 786440 | tf_op jit(solution)/shard_map/ppermute | solution.py:34
  22.1 12.8 %collective-permute-start.10 = (bf16[512,256]{1,0:T(8,128)(2,1)S(1)}, bf16[512,256]{1,0:T(8,128)(2,1)S(1)}, u32[]{:S(2)}, u32[]{:S(2)}) collective-permute-start(bf16[512,256]{1,0:T(8,128)(2,1)S(1)} %collective-permute-done.6.refs_1_), channel_id=1, source_target_pairs={{0,8},{1,9},{2,10},{3,11},{4,12},{5,13},{6,14},{7,15},{8,0},{9,1},... | collective-permute-start | bytes 786440 | tf_op jit(solution)/shard_map/ppermute | solution.py:34
  23.6 14.8 %collective-permute-start.11 = (bf16[512,256]{1,0:T(8,128)(2,1)S(1)}, bf16[512,256]{1,0:T(8,128)(2,1)S(1)}, u32[]{:S(2)}, u32[]{:S(2)}) collective-permute-start(bf16[512,256]{1,0:T(8,128)(2,1)S(1)} %collective-permute-done.9.refs_4_), channel_id=1, source_target_pairs={{0,4},{1,3},{2,6},{3,1},{4,0},{5,7},{6,2},{7,5},{8,12},{9,11},{10,... | collective-permute-start | bytes 786440 | tf_op jit(solution)/shard_map/ppermute | solution.py:34
  27.0 12.3 %collective-permute-start.3 = (bf16[512,256]{1,0:T(8,128)(2,1)S(1)}, bf16[512,256]{1,0:T(8,128)(2,1)S(1)}, u32[]{:S(2)}, u32[]{:S(2)}) collective-permute-start(bf16[512,256]{1,0:T(8,128)(2,1)S(1)} %collective-permute-done.2.refs_9_), channel_id=1, source_target_pairs={{0,8},{1,9},{2,10},{3,11},{4,12},{5,13},{6,14},{7,15},{8,0},{9,1},... | collective-permute-start | bytes 786440 | tf_op jit(solution)/shard_map/ppermute | solution.py:34
  29.2 11.4 %collective-permute-start.13 = (bf16[512,256]{1,0:T(8,128)(2,1)S(1)}, bf16[512,256]{1,0:T(8,128)(2,1)S(1)}, u32[]{:S(2)}, u32[]{:S(2)}) collective-permute-start(bf16[512,256]{1,0:T(8,128)(2,1)S(1)} %collective-permute-done.refs_8_), channel_id=1, source_target_pairs={{0,4},{1,3},{2,6},{3,1},{4,0},{5,7},{6,2},{7,5},{8,12},{9,11},{10,... | collective-permute-start | bytes 786440 | tf_op jit(solution)/shard_map/ppermute | solution.py:34
  30.7 10.5 %collective-permute-start.14 = (bf16[512,256]{1,0:T(8,128)(2,1)S(1)}, bf16[512,256]{1,0:T(8,128)(2,1)S(1)}, u32[]{:S(2)}, u32[]{:S(2)}) collective-permute-start(bf16[512,256]{1,0:T(8,128)(2,1)S(1)} %collective-permute-done.2.refs_9_), channel_id=1, source_target_pairs={{0,4},{1,3},{2,6},{3,1},{4,0},{5,7},{6,2},{7,5},{8,12},{9,11},{10,... | collective-permute-start | bytes 786440 | tf_op jit(solution)/shard_map/ppermute | solution.py:34
  34.8 6.4 %collective-permute-start.12 = (bf16[512,256]{1,0:T(8,128)(2,1)S(1)}, bf16[512,256]{1,0:T(8,128)(2,1)S(1)}, u32[]{:S(2)}, u32[]{:S(2)}) collective-permute-start(bf16[512,256]{1,0:T(8,128)(2,1)S(1)} %collective-permute-done.10.refs_5_), channel_id=1, source_target_pairs={{0,4},{1,3},{2,6},{3,1},{4,0},{5,7},{6,2},{7,5},{8,12},{9,11},{10,... | collective-permute-start | bytes 786440 | tf_op jit(solution)/shard_map/ppermute | solution.py:34
  38.4 8.1 %collective-permute-start.4 = (bf16[512,256]{1,0:T(8,128)(2,1)S(1)}, bf16[512,256]{1,0:T(8,128)(2,1)S(1)}, u32[]{:S(2)}, u32[]{:S(2)}) collective-permute-start(bf16[512,256]{1,0:T(8,128)(2,1)S(1)} %collective-permute-done.1.refs_0_.refs_12_), channel_id=1, source_target_pairs={{0,4},{1,3},{2,6},{3,1},{4,0},{5,7},{6,2},{7,5},{8,12},{9,11},{10,... | collective-permute-start | bytes 786440 | tf_op jit(solution)/shard_map/ppermute | solution.py:34
  39.3 8.3 %collective-permute-start.5 = (bf16[512,256]{1,0:T(8,128)(2,1)S(1)}, bf16[512,256]{1,0:T(8,128)(2,1)S(1)}, u32[]{:S(2)}, u32[]{:S(2)}) collective-permute-start(bf16[512,256]{1,0:T(8,128)(2,1)S(1)} %collective-permute-done.3.refs_1_.refs_13_), channel_id=1, source_target_pairs={{0,4},{1,3},{2,6},{3,1},{4,0},{5,7},{6,2},{7,5},{8,12},{9,11},{10,... | collective-permute-start | bytes 786440 | tf_op jit(solution)/shard_map/ppermute | solution.py:34
  51.1 9.2 %collective-permute-start.15 = (bf16[2,512,256]{2,1,0:T(8,128)(2,1)S(1)}, bf16[2,512,256]{2,1,0:T(8,128)(2,1)S(1)}, u32[]{:S(2)}, u32[]{:S(2)}) collective-permute-start(bf16[2,512,256]{2,1,0:T(8,128)(2,1)S(1)} %get-tuple-element.35), channel_id=1, source_target_pairs={{0,4},{1,3},{2,6},{3,1},{4,0},{5,7},{6,2},{7,5},{8,12},{9,11},{10,... | collective-permute-start | bytes 1572872 | tf_op jit(solution)/shard_map/ppermute | solution.py:34
  55.7 67.6 %collective-permute-start.29 = (bf16[16,256,512]{2,1,0:T(8,128)(2,1)S(1)}, bf16[16,256,512]{2,1,0:T(8,128)(2,1)S(1)}, u32[]{:S(2)}, u32[]{:S(2)}) collective-permute-start(bf16[16,256,512]{2,1,0:T(8,128)(2,1)S(1)} %turn.1.rest_1_.mine), channel_id=1, source_target_pairs={{0,1},{1,0},{2,3},{3,2},{4,5},{5,4},{6,7},{7,6},{8,9},{9,8},{10,11... | collective-permute-start | bytes 12582920 | tf_op jit(solution)/shard_map/ppermute | solution.py:50
  56.8 9.2 %collective-permute-start.19 = (bf16[2,512,256]{2,1,0:T(8,128)(2,1)S(1)}, bf16[2,512,256]{2,1,0:T(8,128)(2,1)S(1)}, u32[]{:S(2)}, u32[]{:S(2)}) collective-permute-start(bf16[2,512,256]{2,1,0:T(8,128)(2,1)S(1)} %get-tuple-element.39), channel_id=1, source_target_pairs={{0,4},{1,3},{2,6},{3,1},{4,0},{5,7},{6,2},{7,5},{8,12},{9,11},{10,... | collective-permute-start | bytes 1572872 | tf_op jit(solution)/shard_map/ppermute | solution.py:34
  61.4 13.4 %collective-permute-start.23 = (bf16[2,512,256]{2,1,0:T(8,128)(2,1)S(1)}, bf16[2,512,256]{2,1,0:T(8,128)(2,1)S(1)}, u32[]{:S(2)}, u32[]{:S(2)}) collective-permute-start(bf16[2,512,256]{2,1,0:T(8,128)(2,1)S(1)} %get-tuple-element.41), channel_id=1, source_target_pairs={{0,4},{1,3},{2,6},{3,1},{4,0},{5,7},{6,2},{7,5},{8,12},{9,11},{10,... | collective-permute-start | bytes 1572872 | tf_op jit(solution)/shard_map/ppermute | solution.py:34
  62.4 8.7 %collective-permute-start.16 = (bf16[512,256]{1,0:T(8,128)(2,1)S(1)}, bf16[512,256]{1,0:T(8,128)(2,1)S(1)}, u32[]{:S(2)}, u32[]{:S(2)}) collective-permute-start(bf16[512,256]{1,0:T(8,128)(2,1)S(1)} %get-tuple-element.67), channel_id=1, source_target_pairs={{0,8},{1,9},{2,10},{3,11},{4,12},{5,13},{6,14},{7,15},{8,0},{9,1},... | collective-permute-start | bytes 786440 | tf_op jit(solution)/shard_map/ppermute | solution.py:34
  63.1 13.0 %collective-permute-start.20 = (bf16[512,256]{1,0:T(8,128)(2,1)S(1)}, bf16[512,256]{1,0:T(8,128)(2,1)S(1)}, u32[]{:S(2)}, u32[]{:S(2)}) collective-permute-start(bf16[512,256]{1,0:T(8,128)(2,1)S(1)} %get-tuple-element.66), channel_id=1, source_target_pairs={{0,8},{1,9},{2,10},{3,11},{4,12},{5,13},{6,14},{7,15},{8,0},{9,1},... | collective-permute-start | bytes 786440 | tf_op jit(solution)/shard_map/ppermute | solution.py:34
  71.2 8.4 %collective-permute-start.21 = (bf16[512,256]{1,0:T(8,128)(2,1)S(1)}, bf16[512,256]{1,0:T(8,128)(2,1)S(1)}, u32[]{:S(2)}, u32[]{:S(2)}) collective-permute-start(bf16[512,256]{1,0:T(8,128)(2,1)S(1)} %fusion.4), channel_id=1, source_target_pairs={{0,2},{1,5},{2,0},{3,7},{4,6},{5,1},{6,4},{7,3},{8,10},{9,13},{10,... | collective-permute-start | bytes 786440 | tf_op jit(solution)/shard_map/ppermute | solution.py:34
  72.8 11.4 %collective-permute-start.17 = (bf16[2,512,256]{2,1,0:T(8,128)(2,1)S(1)}, bf16[2,512,256]{2,1,0:T(8,128)(2,1)S(1)}, u32[]{:S(2)}, u32[]{:S(2)}) collective-permute-start(bf16[2,512,256]{2,1,0:T(8,128)(2,1)S(1)} %get-tuple-element.37), channel_id=1, source_target_pairs={{0,4},{1,3},{2,6},{3,1},{4,0},{5,7},{6,2},{7,5},{8,12},{9,11},{10,... | collective-permute-start | bytes 1572872 | tf_op jit(solution)/shard_map/ppermute | solution.py:34
  74.9 7.5 %collective-permute-start.24 = (bf16[512,256]{1,0:T(8,128)(2,1)S(1)}, bf16[512,256]{1,0:T(8,128)(2,1)S(1)}, u32[]{:S(2)}, u32[]{:S(2)}) collective-permute-start(bf16[512,256]{1,0:T(8,128)(2,1)S(1)} %fusion.13), channel_id=1, source_target_pairs={{0,2},{1,5},{2,0},{3,7},{4,6},{5,1},{6,4},{7,3},{8,10},{9,13},{10,... | collective-permute-start | bytes 786440 | tf_op jit(solution)/shard_map/ppermute | solution.py:34
  79.7 10.3 %collective-permute-start.22 = (bf16[512,256]{1,0:T(8,128)(2,1)S(1)}, bf16[512,256]{1,0:T(8,128)(2,1)S(1)}, u32[]{:S(2)}, u32[]{:S(2)}) collective-permute-start(bf16[512,256]{1,0:T(8,128)(2,1)S(1)} %fusion.7), channel_id=1, source_target_pairs={{0,16},{1,17},{2,18},{3,19},{4,20},{5,21},{6,22},{7,23},{8,24},{9,... | collective-permute-start | bytes 786440 | tf_op jit(solution)/shard_map/ppermute | solution.py:34
  82.5 8.8 %collective-permute-start.25 = (bf16[512,256]{1,0:T(8,128)(2,1)S(1)}, bf16[512,256]{1,0:T(8,128)(2,1)S(1)}, u32[]{:S(2)}, u32[]{:S(2)}) collective-permute-start(bf16[512,256]{1,0:T(8,128)(2,1)S(1)} %fusion.2), channel_id=1, source_target_pairs={{0,8},{1,9},{2,10},{3,11},{4,12},{5,13},{6,14},{7,15},{8,0},{9,1},... | collective-permute-start | bytes 786440 | tf_op jit(solution)/shard_map/ppermute | solution.py:34
  84.3 7.0 %collective-permute-start.18 = (bf16[512,256]{1,0:T(8,128)(2,1)S(1)}, bf16[512,256]{1,0:T(8,128)(2,1)S(1)}, u32[]{:S(2)}, u32[]{:S(2)}) collective-permute-start(bf16[512,256]{1,0:T(8,128)(2,1)S(1)} %fusion.12), channel_id=1, source_target_pairs={{0,2},{1,5},{2,0},{3,7},{4,6},{5,1},{6,4},{7,3},{8,10},{9,13},{10,... | collective-permute-start | bytes 786440 | tf_op jit(solution)/shard_map/ppermute | solution.py:34
  92.3 8.1 %collective-permute-start.26 = (bf16[512,256]{1,0:T(8,128)(2,1)S(1)}, bf16[512,256]{1,0:T(8,128)(2,1)S(1)}, u32[]{:S(2)}, u32[]{:S(2)}) collective-permute-start(bf16[512,256]{1,0:T(8,128)(2,1)S(1)} %get-tuple-element.62.e0), channel_id=1, source_target_pairs={{0,2},{1,5},{2,0},{3,7},{4,6},{5,1},{6,4},{7,3},{8,10},{9,13},{10,... | collective-permute-start | bytes 786440 | tf_op jit(solution)/shard_map/ppermute | solution.py:34
  92.9 11.1 %collective-permute-start.34 = (bf16[512,256]{1,0:T(8,128)(2,1)S(1)}, bf16[512,256]{1,0:T(8,128)(2,1)S(1)}, u32[]{:S(2)}, u32[]{:S(2)}) collective-permute-start(bf16[512,256]{1,0:T(8,128)(2,1)S(1)} %get-tuple-element.62.e0), channel_id=1, source_target_pairs={{0,16},{1,17},{2,18},{3,19},{4,20},{5,21},{6,22},{7,23},{8,24},{9,... | collective-permute-start | bytes 786440 | tf_op jit(solution)/shard_map/ppermute | solution.py:34
  95.5 9.0 %collective-permute-start.27 = (bf16[512,256]{1,0:T(8,128)(2,1)S(1)}, bf16[512,256]{1,0:T(8,128)(2,1)S(1)}, u32[]{:S(2)}, u32[]{:S(2)}) collective-permute-start(bf16[512,256]{1,0:T(8,128)(2,1)S(1)} %get-tuple-element.62.e0), channel_id=1, source_target_pairs={{0,4},{1,3},{2,6},{3,1},{4,0},{5,7},{6,2},{7,5},{8,12},{9,11},{10,... | collective-permute-start | bytes 786440 | tf_op jit(solution)/shard_map/ppermute | solution.py:34
  96.7 10.4 %collective-permute-start.30 = (bf16[512,256]{1,0:T(8,128)(2,1)S(1)}, bf16[512,256]{1,0:T(8,128)(2,1)S(1)}, u32[]{:S(2)}, u32[]{:S(2)}) collective-permute-start(bf16[512,256]{1,0:T(8,128)(2,1)S(1)} %get-tuple-element.62.e0), channel_id=1, source_target_pairs={{0,8},{1,9},{2,10},{3,11},{4,12},{5,13},{6,14},{7,15},{8,0},{9,1},... | collective-permute-start | bytes 786440 | tf_op jit(solution)/shard_map/ppermute | solution.py:34
  100.4 8.6 %collective-permute-start.28 = (bf16[512,256]{1,0:T(8,128)(2,1)S(1)}, bf16[512,256]{1,0:T(8,128)(2,1)S(1)}, u32[]{:S(2)}, u32[]{:S(2)}) collective-permute-start(bf16[512,256]{1,0:T(8,128)(2,1)S(1)} %collective-permute-done.26.e1), channel_id=1, source_target_pairs={{0,4},{1,3},{2,6},{3,1},{4,0},{5,7},{6,2},{7,5},{8,12},{9,11},{10,... | collective-permute-start | bytes 786440 | tf_op jit(solution)/shard_map/ppermute | solution.py:34
  104.0 6.4 %collective-permute-start.35 = (bf16[512,256]{1,0:T(8,128)(2,1)S(1)}, bf16[512,256]{1,0:T(8,128)(2,1)S(1)}, u32[]{:S(2)}, u32[]{:S(2)}) collective-permute-start(bf16[512,256]{1,0:T(8,128)(2,1)S(1)} %collective-permute-done.34.e0), channel_id=1, source_target_pairs={{0,2},{1,5},{2,0},{3,7},{4,6},{5,1},{6,4},{7,3},{8,10},{9,13},{10,... | collective-permute-start | bytes 786440 | tf_op jit(solution)/shard_map/ppermute | solution.py:34
  104.5 9.2 %collective-permute-start.31 = (bf16[512,256]{1,0:T(8,128)(2,1)S(1)}, bf16[512,256]{1,0:T(8,128)(2,1)S(1)}, u32[]{:S(2)}, u32[]{:S(2)}) collective-permute-start(bf16[512,256]{1,0:T(8,128)(2,1)S(1)} %collective-permute-done.26.e1), channel_id=1, source_target_pairs={{0,8},{1,9},{2,10},{3,11},{4,12},{5,13},{6,14},{7,15},{8,0},{9,1},... | collective-permute-start | bytes 786440 | tf_op jit(solution)/shard_map/ppermute | solution.py:34
  107.0 7.3 %collective-permute-start.32 = (bf16[512,256]{1,0:T(8,128)(2,1)S(1)}, bf16[512,256]{1,0:T(8,128)(2,1)S(1)}, u32[]{:S(2)}, u32[]{:S(2)}) collective-permute-start(bf16[512,256]{1,0:T(8,128)(2,1)S(1)} %collective-permute-done.30.e0), channel_id=1, source_target_pairs={{0,4},{1,3},{2,6},{3,1},{4,0},{5,7},{6,2},{7,5},{8,12},{9,11},{10,... | collective-permute-start | bytes 786440 | tf_op jit(solution)/shard_map/ppermute | solution.py:34
  108.9 10.4 %collective-permute-start.38 = (bf16[512,256]{1,0:T(8,128)(2,1)S(1)}, bf16[512,256]{1,0:T(8,128)(2,1)S(1)}, u32[]{:S(2)}, u32[]{:S(2)}) collective-permute-start(bf16[512,256]{1,0:T(8,128)(2,1)S(1)} %collective-permute-done.34.e0), channel_id=1, source_target_pairs={{0,8},{1,9},{2,10},{3,11},{4,12},{5,13},{6,14},{7,15},{8,0},{9,1},... | collective-permute-start | bytes 786440 | tf_op jit(solution)/shard_map/ppermute | solution.py:34
  110.4 12.3 %collective-permute-start.39 = (bf16[512,256]{1,0:T(8,128)(2,1)S(1)}, bf16[512,256]{1,0:T(8,128)(2,1)S(1)}, u32[]{:S(2)}, u32[]{:S(2)}) collective-permute-start(bf16[512,256]{1,0:T(8,128)(2,1)S(1)} %collective-permute-done.35.e1), channel_id=1, source_target_pairs={{0,8},{1,9},{2,10},{3,11},{4,12},{5,13},{6,14},{7,15},{8,0},{9,1},... | collective-permute-start | bytes 786440 | tf_op jit(solution)/shard_map/ppermute | solution.py:34
  113.8 12.4 %collective-permute-start.33 = (bf16[512,256]{1,0:T(8,128)(2,1)S(1)}, bf16[512,256]{1,0:T(8,128)(2,1)S(1)}, u32[]{:S(2)}, u32[]{:S(2)}) collective-permute-start(bf16[512,256]{1,0:T(8,128)(2,1)S(1)} %collective-permute-done.31.e1), channel_id=1, source_target_pairs={{0,4},{1,3},{2,6},{3,1},{4,0},{5,7},{6,2},{7,5},{8,12},{9,11},{10,... | collective-permute-start | bytes 786440 | tf_op jit(solution)/shard_map/ppermute | solution.py:34
  114.3 13.2 %collective-permute-start.36 = (bf16[512,256]{1,0:T(8,128)(2,1)S(1)}, bf16[512,256]{1,0:T(8,128)(2,1)S(1)}, u32[]{:S(2)}, u32[]{:S(2)}) collective-permute-start(bf16[512,256]{1,0:T(8,128)(2,1)S(1)} %collective-permute-done.34.e0), channel_id=1, source_target_pairs={{0,4},{1,3},{2,6},{3,1},{4,0},{5,7},{6,2},{7,5},{8,12},{9,11},{10,... | collective-permute-start | bytes 786440 | tf_op jit(solution)/shard_map/ppermute | solution.py:34
  119.4 8.7 %collective-permute-start.37 = (bf16[512,256]{1,0:T(8,128)(2,1)S(1)}, bf16[512,256]{1,0:T(8,128)(2,1)S(1)}, u32[]{:S(2)}, u32[]{:S(2)}) collective-permute-start(bf16[512,256]{1,0:T(8,128)(2,1)S(1)} %collective-permute-done.35.e1), channel_id=1, source_target_pairs={{0,4},{1,3},{2,6},{3,1},{4,0},{5,7},{6,2},{7,5},{8,12},{9,11},{10,... | collective-permute-start | bytes 786440 | tf_op jit(solution)/shard_map/ppermute | solution.py:34
  122.7 6.8 %collective-permute-start.40 = (bf16[512,256]{1,0:T(8,128)(2,1)S(1)}, bf16[512,256]{1,0:T(8,128)(2,1)S(1)}, u32[]{:S(2)}, u32[]{:S(2)}) collective-permute-start(bf16[512,256]{1,0:T(8,128)(2,1)S(1)} %collective-permute-done.38.e0), channel_id=1, source_target_pairs={{0,4},{1,3},{2,6},{3,1},{4,0},{5,7},{6,2},{7,5},{8,12},{9,11},{10,... | collective-permute-start | bytes 786440 | tf_op jit(solution)/shard_map/ppermute | solution.py:34
  123.2 8.7 %collective-permute-start.41 = (bf16[512,256]{1,0:T(8,128)(2,1)S(1)}, bf16[512,256]{1,0:T(8,128)(2,1)S(1)}, u32[]{:S(2)}, u32[]{:S(2)}) collective-permute-start(bf16[512,256]{1,0:T(8,128)(2,1)S(1)} %collective-permute-done.39.e1), channel_id=1, source_target_pairs={{0,4},{1,3},{2,6},{3,1},{4,0},{5,7},{6,2},{7,5},{8,12},{9,11},{10,... | collective-permute-start | bytes 786440 | tf_op jit(solution)/shard_map/ppermute | solution.py:34
  126.1 13.3 %collective-permute-start.42 = (bf16[128,1024]{1,0:T(8,128)(2,1)S(1)}, bf16[128,1024]{1,0:T(8,128)(2,1)S(1)}, u32[]{:S(2)}, u32[]{:S(2)}) collective-permute-start(bf16[128,1024]{1,0:T(8,128)(2,1)S(1)} %get-tuple-element.53), channel_id=1, source_target_pairs={{0,1},{1,0},{2,3},{3,2},{4,5},{5,4},{6,7},{7,6},{8,9},{9,8},{10,11... | collective-permute-start | bytes 786440 | tf_op jit(solution)/shard_map/ppermute | solution.py:50
  127.5 11.9 %collective-permute-start.43 = (bf16[128,1024]{1,0:T(8,128)(2,1)S(1)}, bf16[128,1024]{1,0:T(8,128)(2,1)S(1)}, u32[]{:S(2)}, u32[]{:S(2)}) collective-permute-start(bf16[128,1024]{1,0:T(8,128)(2,1)S(1)} %get-tuple-element.54), channel_id=1, source_target_pairs={{0,1},{1,0},{2,3},{3,2},{4,5},{5,4},{6,7},{7,6},{8,9},{9,8},{10,11... | collective-permute-start | bytes 786440 | tf_op jit(solution)/shard_map/ppermute | solution.py:50
  129.4 10.0 %collective-permute-start.44 = (bf16[128,1024]{1,0:T(8,128)(2,1)S(1)}, bf16[128,1024]{1,0:T(8,128)(2,1)S(1)}, u32[]{:S(2)}, u32[]{:S(2)}) collective-permute-start(bf16[128,1024]{1,0:T(8,128)(2,1)S(1)} %get-tuple-element.55), channel_id=1, source_target_pairs={{0,1},{1,0},{2,3},{3,2},{4,5},{5,4},{6,7},{7,6},{8,9},{9,8},{10,11... | collective-permute-start | bytes 786440 | tf_op jit(solution)/shard_map/ppermute | solution.py:50
  133.3 6.1 %collective-permute-start.45 = (bf16[128,1024]{1,0:T(8,128)(2,1)S(1)}, bf16[128,1024]{1,0:T(8,128)(2,1)S(1)}, u32[]{:S(2)}, u32[]{:S(2)}) collective-permute-start(bf16[128,1024]{1,0:T(8,128)(2,1)S(1)} %get-tuple-element.56), channel_id=1, source_target_pairs={{0,1},{1,0},{2,3},{3,2},{4,5},{5,4},{6,7},{7,6},{8,9},{9,8},{10,11... | collective-permute-start | bytes 786440 | tf_op jit(solution)/shard_map/ppermute | solution.py:50
  133.3 1.7 %collective-permute-start.47 = (bf16[512,128]{1,0:T(8,128)(2,1)S(1)}, bf16[512,128]{1,0:T(8,128)(2,1)S(1)}, u32[]{:S(2)}, u32[]{:S(2)}) collective-permute-start(bf16[512,128]{1,0:T(8,128)(2,1)S(1)} %get-tuple-element.61), channel_id=1, source_target_pairs={{0,1},{1,0},{2,3},{3,2},{4,5},{5,4},{6,7},{7,6},{8,9},{9,8},{10,11... | collective-permute-start | bytes 393224 | tf_op jit(solution)/shard_map/ppermute | solution.py:50
  135.1 4.3 %collective-permute-start.46 = (f32[8,128]{1,0:T(8,128)S(1)}, f32[8,128]{1,0:T(8,128)S(1)}, u32[]{:S(2)}, u32[]{:S(2)}) collective-permute-start(f32[8,128]{1,0:T(8,128)S(1)} %get-tuple-element.57.refs_8_), channel_id=1, source_target_pairs={{0,1},{1,0},{2,3},{3,2},{4,5},{5,4},{6,7},{7,6},{8,9},{9,8},{10,11... | collective-permute-start | bytes 12296 | tf_op jit(solution)/shard_map/ppermute | solution.py:440
  (6 other events, 38.2 us)

commit v5 on v4

--- a/solution.py
+++ b/solution.py
@@ -155,17 +155,19 @@
     pairs.append((start, begun))
     for b in range(count):
         at = pl.ds(pl.multiple_of(order[b] * width, width), width)
-        pairs += [(xs[b], held.at[b]), (weight.at[at], rows_of.at[b])]
+        here = pl.ds(b * width, width)
+        pairs += [(xs[b], held.at[:, here]), (weight.at[at], rows_of.at[here])]
     loads = [pltpu.make_async_copy(a, b, sems.at[n]) for n, (a, b) in enumerate(pairs)]
     for load in loads:
         load.start()
     for load in loads[:-2 * count]:
         load.wait()
     total = begun[...]
-    for b in range(count):
-        loads[2 * (b - count)].wait()
-        loads[2 * (b - count) + 1].wait()
-        total = total + jnp.dot(held[b], rows_of[b], preferred_element_type=F32)
+    for b in range(0, count, 4):
+        for load in loads[2 * (b - count):][:8]:
+            load.wait()
+        here = pl.ds(b * width, 4 * width)
+        total = total + jnp.dot(held[:, here], rows_of[here, :], preferred_element_type=F32)
     if last:
         act[...], slope[...] = activate(total, gates[...])
     else:
@@ -184,7 +186,7 @@
         return activate(total, active) if last else [total]
     out = [jax.ShapeDtypeStruct((rows, lats), F32)]
     operands = blocks + [weight, start]
-    scratch = [pltpu.VMEM((count, rows, width), BF16), pltpu.VMEM((count, width, lats), BF16)]
+    scratch = [pltpu.VMEM((rows, count * width), BF16), pltpu.VMEM((count * width, lats), BF16)]
     scratch.append(pltpu.VMEM(start.shape, F32))
     if last:
         out = [jax.ShapeDtypeStruct((rows, lats), BF16)] + out

time: 142 us -> 141 us (level)
  transfers between devices with their start and end apart: 48 -> 48, of which waited for: 25 -> 25; matrix products, arithmetic and copies ran while one was open for 2% -> 2% of each run, Pallas kernels for 16% -> 15%
where the time goes in v5:
time: 141 us
  waiting for transfers between devices  56.8 us (40%)
  starting transfers between devices  51.2 us (36%)
  Pallas kernels  26.6 us (19%)
  other arithmetic  3.86 us (3%)
  local copies, waits for them, and re-layouts  1.75 us (1%)
    ppermute x41, waiting for transfers between devices, swap(): return lax.ppermute(x, ('lat', 'dp'), pairs)  55.6 us
    ppermute x41, starting transfers between devices, swap(): return lax.ppermute(x, ('lat', 'dp'), pairs)  49.7 us
    pallas_call x14, Pallas kernels, call(): pl.pallas_call(body, grid_spec=pltpu.PrefetchScalarGridSpec(num_scalar_pr...  26.6 us
  transfers between devices with their start and end apart: 48, of which 25 were waited for; matrix products, arithmetic and copies ran while one was open for 2% of the time, Pallas kernels for 15%

profile of v5, /device:TPU:0, one launch (start us, length us, event | category | flops | bytes accessed | tf_op | source)
XLA Modules:
  0.0 141.1 jit_solution(167298594561822603)
XLA Ops:
  2.3 4.1 %collective-permute-start = (bf16[512,256]{1,0:T(8,128)(2,1)S(1)}, bf16[512,256]{1,0:T(8,128)(2,1)S(1)}, u32[]{:S(2)}, u32[]{:S(2)}) collective-permute-start(bf16[512,256]{1,0:T(8,128)(2,1)S(1)} %fusion.refs_0_), channel_id=1, source_target_pairs={{0,16},{1,17},{2,18},{3,19},{4,20},{5,21},{6,22},{7,23},{8,24},{9,... | collective-permute-start | bytes 786440 | tf_op jit(solution)/shard_map/ppermute | solution.py:34
  6.4 1.5 %collective-permute-start.6 = (bf16[512,256]{1,0:T(8,128)(2,1)S(1)}, bf16[512,256]{1,0:T(8,128)(2,1)S(1)}, u32[]{:S(2)}, u32[]{:S(2)}) collective-permute-start(bf16[512,256]{1,0:T(8,128)(2,1)S(1)} %fusion.refs_0_), channel_id=1, source_target_pairs={{0,2},{1,5},{2,0},{3,7},{4,6},{5,1},{6,4},{7,3},{8,10},{9,13},{10,... | collective-permute-start | bytes 786440 | tf_op jit(solution)/shard_map/ppermute | solution.py:34
  7.9 1.5 %collective-permute-start.7 = (bf16[512,256]{1,0:T(8,128)(2,1)S(1)}, bf16[512,256]{1,0:T(8,128)(2,1)S(1)}, u32[]{:S(2)}, u32[]{:S(2)}) collective-permute-start(bf16[512,256]{1,0:T(8,128)(2,1)S(1)} %fusion.refs_0_), channel_id=1, source_target_pairs={{0,4},{1,3},{2,6},{3,1},{4,0},{5,7},{6,2},{7,5},{8,12},{9,11},{10,... | collective-permute-start | bytes 786440 | tf_op jit(solution)/shard_map/ppermute | solution.py:34
  9.4 1.6 %collective-permute-start.9 = (bf16[512,256]{1,0:T(8,128)(2,1)S(1)}, bf16[512,256]{1,0:T(8,128)(2,1)S(1)}, u32[]{:S(2)}, u32[]{:S(2)}) collective-permute-start(bf16[512,256]{1,0:T(8,128)(2,1)S(1)} %fusion.refs_0_), channel_id=1, source_target_pairs={{0,8},{1,9},{2,10},{3,11},{4,12},{5,13},{6,14},{7,15},{8,0},{9,1},... | collective-permute-start | bytes 786440 | tf_op jit(solution)/shard_map/ppermute | solution.py:34
  11.0 7.4 %collective-permute-done.refs_8_ = bf16[512,256]{1,0:T(8,128)(2,1)S(1)} collective-permute-done((bf16[512,256]{1,0:T(8,128)(2,1)S(1)}, bf16[512,256]{1,0:T(8,128)(2,1)S(1)}, u32[]{:S(2)}, u32[]{:S(2)}) %collective-permute-start) | collective-permute-done | bytes 262176 | tf_op jit(solution)/shard_map/ppermute | solution.py:34
  18.4 1.5 %collective-permute-start.2 = (bf16[512,256]{1,0:T(8,128)(2,1)S(1)}, bf16[512,256]{1,0:T(8,128)(2,1)S(1)}, u32[]{:S(2)}, u32[]{:S(2)}) collective-permute-start(bf16[512,256]{1,0:T(8,128)(2,1)S(1)} %collective-permute-done.refs_8_), channel_id=1, source_target_pairs={{0,2},{1,5},{2,0},{3,7},{4,6},{5,1},{6,4},{7,3},{8,10},{9,13},{10,... | collective-permute-start | bytes 786440 | tf_op jit(solution)/shard_map/ppermute | solution.py:34
  20.6 1.5 %collective-permute-start.8 = (bf16[512,256]{1,0:T(8,128)(2,1)S(1)}, bf16[512,256]{1,0:T(8,128)(2,1)S(1)}, u32[]{:S(2)}, u32[]{:S(2)}) collective-permute-start(bf16[512,256]{1,0:T(8,128)(2,1)S(1)} %collective-permute-done.6.refs_1_), channel_id=1, source_target_pairs={{0,4},{1,3},{2,6},{3,1},{4,0},{5,7},{6,2},{7,5},{8,12},{9,11},{10,... | collective-permute-start | bytes 786440 | tf_op jit(solution)/shard_map/ppermute | solution.py:34
  22.1 1.5 %collective-permute-start.10 = (bf16[512,256]{1,0:T(8,128)(2,1)S(1)}, bf16[512,256]{1,0:T(8,128)(2,1)S(1)}, u32[]{:S(2)}, u32[]{:S(2)}) collective-permute-start(bf16[512,256]{1,0:T(8,128)(2,1)S(1)} %collective-permute-done.6.refs_1_), channel_id=1, source_target_pairs={{0,8},{1,9},{2,10},{3,11},{4,12},{5,13},{6,14},{7,15},{8,0},{9,1},... | collective-permute-start | bytes 786440 | tf_op jit(solution)/shard_map/ppermute | solution.py:34
  24.1 2.9 %collective-permute-done.2.refs_9_ = bf16[512,256]{1,0:T(8,128)(2,1)S(1)} collective-permute-done((bf16[512,256]{1,0:T(8,128)(2,1)S(1)}, bf16[512,256]{1,0:T(8,128)(2,1)S(1)}, u32[]{:S(2)}, u32[]{:S(2)}) %collective-permute-start.2) | collective-permute-done | bytes 262176 | tf_op jit(solution)/shard_map/ppermute | solution.py:34
  27.9 1.3 collective-permute-done.1.refs_0_.refs_12_
  29.2 1.5 %collective-permute-start.13 = (bf16[512,256]{1,0:T(8,128)(2,1)S(1)}, bf16[512,256]{1,0:T(8,128)(2,1)S(1)}, u32[]{:S(2)}, u32[]{:S(2)}) collective-permute-start(bf16[512,256]{1,0:T(8,128)(2,1)S(1)} %collective-permute-done.refs_8_), channel_id=1, source_target_pairs={{0,4},{1,3},{2,6},{3,1},{4,0},{5,7},{6,2},{7,5},{8,12},{9,11},{10,... | collective-permute-start | bytes 786440 | tf_op jit(solution)/shard_map/ppermute | solution.py:34
  31.2 3.6 %collective-permute-done.10.refs_5_ = bf16[512,256]{1,0:T(8,128)(2,1)S(1)} collective-permute-done((bf16[512,256]{1,0:T(8,128)(2,1)S(1)}, bf16[512,256]{1,0:T(8,128)(2,1)S(1)}, u32[]{:S(2)}, u32[]{:S(2)}) %collective-permute-start.10) | collective-permute-done | bytes 262176 | tf_op jit(solution)/shard_map/ppermute | solution.py:34
  36.1 1.6 %copy-done.1 = bf16[256,4096]{1,0:T(8,128)(2,1)S(1)} copy-done((bf16[256,4096]{1,0:T(8,128)(2,1)S(1)}, bf16[256,4096]{1,0:T(8,128)(2,1)}, u32[]{:S(2)}) %copy-start.1) | copy-done | bytes 2097176
  41.2 4.8 %encode.2.refs_5_ = f32[512,256]{1,0:T(8,128)S(1)} custom-call(s32[12]{0:T(128)S(1)} %pad_add_fusion.2.order, bf16[512,256]{1,0:T(8,128)(2,1)S(1)} %fusion.refs_0_, bf16[512,256]{1,0:T(8,128)(2,1)S(1)} %collective-permute-done.6.refs_1_, bf16[512,256]{1,0:T(8,128)(2,1)S(1)} %collective-permute-done.7.refs_2_, ...), custom_call_target="tpu_custom_call" | custom-call | flops 805306368 | bytes 5767168 | tf_op jit(solution)/shard_map/encode/pallas_call | solution.py:126
  46.1 1.6 %collective-permute-done.5.refs_3_.refs_15_ = bf16[512,256]{1,0:T(8,128)(2,1)S(1)} collective-permute-done((bf16[512,256]{1,0:T(8,128)(2,1)S(1)}, bf16[512,256]{1,0:T(8,128)(2,1)S(1)}, u32[]{:S(2)}, u32[]{:S(2)}) %collective-permute-start.5) | collective-permute-done | bytes 262176 | tf_op jit(solution)/shard_map/ppermute | solution.py:34
  47.7 2.0 %encode.3 = (bf16[512,256]{1,0:T(8,128)(2,1)S(1)}, f32[512,256]{1,0:T(8,128)S(1)}) custom-call(s32[4]{0:T(128)S(1)} %get-tuple-element.70.order, bf16[512,256]{1,0:T(8,128)(2,1)S(1)} %collective-permute-done.1.refs_0_.refs_12_, bf16[512,256]{1,0:T(8,128)(2,1)S(1)} %collective-permute-done.3.refs_1_.refs_13_, ...), custom_call_target="tpu_custom_call" | custom-call | flops 268435456 | bytes 2621440 | tf_op jit(solution)/shard_map/encode/pallas_call | solution.py:126
  51.6 3.6 %turn.1.rest_1_.mine = bf16[16,256,512]{2,1,0:T(8,128)(2,1)S(1)} custom-call(s32[16]{0:T(128)S(1)} %pad_add_fusion.3.order, bf16[512,256]{1,0:T(8,128)(2,1)S(1)} %fusion.refs_0_, bf16[512,256]{1,0:T(8,128)(2,1)S(1)} %collective-permute-done.6.refs_1_, bf16[512,256]{1,0:T(8,128)(2,1)S(1)} %collective-permute-done.7.refs_2_, ...), custom_call_target="tpu_custom_call" | custom-call | bytes 8388608 | tf_op jit(solution)/shard_map/turn/pallas_call | solution.py:126
  56.3 1.3 collective-permute-start.19
  57.6 2.3 %collective-permute-done.15.rest_0_ = bf16[2,512,256]{2,1,0:T(8,128)(2,1)S(1)} collective-permute-done((bf16[2,512,256]{2,1,0:T(8,128)(2,1)S(1)}, bf16[2,512,256]{2,1,0:T(8,128)(2,1)S(1)}, u32[]{:S(2)}, u32[]{:S(2)}) %collective-permute-start.15) | collective-permute-done | bytes 524320 | tf_op jit(solution)/shard_map/ppermute | solution.py:34
  62.6 1.5 %collective-permute-start.20 = (bf16[512,256]{1,0:T(8,128)(2,1)S(1)}, bf16[512,256]{1,0:T(8,128)(2,1)S(1)}, u32[]{:S(2)}, u32[]{:S(2)}) collective-permute-start(bf16[512,256]{1,0:T(8,128)(2,1)S(1)} %get-tuple-element.66), channel_id=1, source_target_pairs={{0,8},{1,9},{2,10},{3,11},{4,12},{5,13},{6,14},{7,15},{8,0},{9,1},... | collective-permute-start | bytes 786440 | tf_op jit(solution)/shard_map/ppermute | solution.py:34
  64.1 1.5 %collective-permute-done.19 = bf16[2,512,256]{2,1,0:T(8,128)(2,1)S(1)} collective-permute-done((bf16[2,512,256]{2,1,0:T(8,128)(2,1)S(1)}, bf16[2,512,256]{2,1,0:T(8,128)(2,1)S(1)}, u32[]{:S(2)}, u32[]{:S(2)}) %collective-permute-start.19) | collective-permute-done | bytes 524320 | tf_op jit(solution)/shard_map/ppermute | solution.py:34
  65.7 5.0 %collective-permute-done.16.rest_0_ = bf16[512,256]{1,0:T(8,128)(2,1)S(1)} collective-permute-done((bf16[512,256]{1,0:T(8,128)(2,1)S(1)}, bf16[512,256]{1,0:T(8,128)(2,1)S(1)}, u32[]{:S(2)}, u32[]{:S(2)}) %collective-permute-start.16) | collective-permute-done | bytes 262176 | tf_op jit(solution)/shard_map/ppermute | solution.py:34
  72.3 1.7 %collective-permute-start.17 = (bf16[2,512,256]{2,1,0:T(8,128)(2,1)S(1)}, bf16[2,512,256]{2,1,0:T(8,128)(2,1)S(1)}, u32[]{:S(2)}, u32[]{:S(2)}) collective-permute-start(bf16[2,512,256]{2,1,0:T(8,128)(2,1)S(1)} %get-tuple-element.37), channel_id=1, source_target_pairs={{0,4},{1,3},{2,6},{3,1},{4,0},{5,7},{6,2},{7,5},{8,12},{9,11},{10,... | collective-permute-start | bytes 1572872 | tf_op jit(solution)/shard_map/ppermute | solution.py:34
  75.6 3.6 %collective-permute-done.21 = bf16[512,256]{1,0:T(8,128)(2,1)S(1)} collective-permute-done((bf16[512,256]{1,0:T(8,128)(2,1)S(1)}, bf16[512,256]{1,0:T(8,128)(2,1)S(1)}, u32[]{:S(2)}, u32[]{:S(2)}) %collective-permute-start.21) | collective-permute-done | bytes 262176 | tf_op jit(solution)/shard_map/ppermute | solution.py:34
  79.3 2.4 %collective-permute-start.22 = (bf16[512,256]{1,0:T(8,128)(2,1)S(1)}, bf16[512,256]{1,0:T(8,128)(2,1)S(1)}, u32[]{:S(2)}, u32[]{:S(2)}) collective-permute-start(bf16[512,256]{1,0:T(8,128)(2,1)S(1)} %fusion.7), channel_id=1, source_target_pairs={{0,16},{1,17},{2,18},{3,19},{4,20},{5,21},{6,22},{7,23},{8,24},{9,... | collective-permute-start | bytes 786440 | tf_op jit(solution)/shard_map/ppermute | solution.py:34
  82.0 1.5 %collective-permute-start.25 = (bf16[512,256]{1,0:T(8,128)(2,1)S(1)}, bf16[512,256]{1,0:T(8,128)(2,1)S(1)}, u32[]{:S(2)}, u32[]{:S(2)}) collective-permute-start(bf16[512,256]{1,0:T(8,128)(2,1)S(1)} %fusion.2), channel_id=1, source_target_pairs={{0,8},{1,9},{2,10},{3,11},{4,12},{5,13},{6,14},{7,15},{8,0},{9,1},... | collective-permute-start | bytes 786440 | tf_op jit(solution)/shard_map/ppermute | solution.py:34
  84.8 4.7 %collective-permute-done.22 = bf16[512,256]{1,0:T(8,128)(2,1)S(1)} collective-permute-done((bf16[512,256]{1,0:T(8,128)(2,1)S(1)}, bf16[512,256]{1,0:T(8,128)(2,1)S(1)}, u32[]{:S(2)}, u32[]{:S(2)}) %collective-permute-start.22) | collective-permute-done | bytes 262176 | tf_op jit(solution)/shard_map/ppermute | solution.py:34
  89.5 1.3 collective-permute-done.25
  92.5 2.5 %collective-permute-start.34 = (bf16[512,256]{1,0:T(8,128)(2,1)S(1)}, bf16[512,256]{1,0:T(8,128)(2,1)S(1)}, u32[]{:S(2)}, u32[]{:S(2)}) collective-permute-start(bf16[512,256]{1,0:T(8,128)(2,1)S(1)} %get-tuple-element.62.e0), channel_id=1, source_target_pairs={{0,16},{1,17},{2,18},{3,19},{4,20},{5,21},{6,22},{7,23},{8,24},{9,... | collective-permute-start | bytes 786440 | tf_op jit(solution)/shard_map/ppermute | solution.py:34
  96.2 2.5 %collective-permute-start.30 = (bf16[512,256]{1,0:T(8,128)(2,1)S(1)}, bf16[512,256]{1,0:T(8,128)(2,1)S(1)}, u32[]{:S(2)}, u32[]{:S(2)}) collective-permute-start(bf16[512,256]{1,0:T(8,128)(2,1)S(1)} %get-tuple-element.62.e0), channel_id=1, source_target_pairs={{0,8},{1,9},{2,10},{3,11},{4,12},{5,13},{6,14},{7,15},{8,0},{9,1},... | collective-permute-start | bytes 786440 | tf_op jit(solution)/shard_map/ppermute | solution.py:34
  99.9 1.2 collective-permute-start.28
  101.1 2.5 %collective-permute-done.34.e0 = bf16[512,256]{1,0:T(8,128)(2,1)S(1)} collective-permute-done((bf16[512,256]{1,0:T(8,128)(2,1)S(1)}, bf16[512,256]{1,0:T(8,128)(2,1)S(1)}, u32[]{:S(2)}, u32[]{:S(2)}) %collective-permute-start.34) | collective-permute-done | bytes 262176 | tf_op jit(solution)/shard_map/ppermute | solution.py:34
  105.1 1.4 %collective-permute-done.30.e0 = bf16[512,256]{1,0:T(8,128)(2,1)S(1)} collective-permute-done((bf16[512,256]{1,0:T(8,128)(2,1)S(1)}, bf16[512,256]{1,0:T(8,128)(2,1)S(1)}, u32[]{:S(2)}, u32[]{:S(2)}) %collective-permute-start.30) | collective-permute-done | bytes 262176 | tf_op jit(solution)/shard_map/ppermute | solution.py:34
  106.6 1.7 %collective-permute-done.28.e3 = bf16[512,256]{1,0:T(8,128)(2,1)S(1)} collective-permute-done((bf16[512,256]{1,0:T(8,128)(2,1)S(1)}, bf16[512,256]{1,0:T(8,128)(2,1)S(1)}, u32[]{:S(2)}, u32[]{:S(2)}) %collective-permute-start.28) | collective-permute-done | bytes 262176 | tf_op jit(solution)/shard_map/ppermute | solution.py:34
  108.2 1.8 %collective-permute-done.35.e1 = bf16[512,256]{1,0:T(8,128)(2,1)S(1)} collective-permute-done((bf16[512,256]{1,0:T(8,128)(2,1)S(1)}, bf16[512,256]{1,0:T(8,128)(2,1)S(1)}, u32[]{:S(2)}, u32[]{:S(2)}) %collective-permute-start.35) | collective-permute-done | bytes 262176 | tf_op jit(solution)/shard_map/ppermute | solution.py:34
  110.0 1.7 %collective-permute-start.39 = (bf16[512,256]{1,0:T(8,128)(2,1)S(1)}, bf16[512,256]{1,0:T(8,128)(2,1)S(1)}, u32[]{:S(2)}, u32[]{:S(2)}) collective-permute-start(bf16[512,256]{1,0:T(8,128)(2,1)S(1)} %collective-permute-done.35.e1), channel_id=1, source_target_pairs={{0,8},{1,9},{2,10},{3,11},{4,12},{5,13},{6,14},{7,15},{8,0},{9,1},... | collective-permute-start | bytes 786440 | tf_op jit(solution)/shard_map/ppermute | solution.py:34
  111.7 1.6 %collective-permute-done.31.e1 = bf16[512,256]{1,0:T(8,128)(2,1)S(1)} collective-permute-done((bf16[512,256]{1,0:T(8,128)(2,1)S(1)}, bf16[512,256]{1,0:T(8,128)(2,1)S(1)}, u32[]{:S(2)}, u32[]{:S(2)}) %collective-permute-start.31) | collective-permute-done | bytes 262176 | tf_op jit(solution)/shard_map/ppermute | solution.py:34
  113.8 1.5 %collective-permute-start.36 = (bf16[512,256]{1,0:T(8,128)(2,1)S(1)}, bf16[512,256]{1,0:T(8,128)(2,1)S(1)}, u32[]{:S(2)}, u32[]{:S(2)}) collective-permute-start(bf16[512,256]{1,0:T(8,128)(2,1)S(1)} %collective-permute-done.34.e0), channel_id=1, source_target_pairs={{0,4},{1,3},{2,6},{3,1},{4,0},{5,7},{6,2},{7,5},{8,12},{9,11},{10,... | collective-permute-start | bytes 786440 | tf_op jit(solution)/shard_map/ppermute | solution.py:34
  115.3 3.6 %collective-permute-done.38.e0 = bf16[512,256]{1,0:T(8,128)(2,1)S(1)} collective-permute-done((bf16[512,256]{1,0:T(8,128)(2,1)S(1)}, bf16[512,256]{1,0:T(8,128)(2,1)S(1)}, u32[]{:S(2)}, u32[]{:S(2)}) %collective-permute-start.38) | collective-permute-done | bytes 262176 | tf_op jit(solution)/shard_map/ppermute | solution.py:34
  119.5 2.9 %collective-permute-done.39.e1 = bf16[512,256]{1,0:T(8,128)(2,1)S(1)} collective-permute-done((bf16[512,256]{1,0:T(8,128)(2,1)S(1)}, bf16[512,256]{1,0:T(8,128)(2,1)S(1)}, u32[]{:S(2)}, u32[]{:S(2)}) %collective-permute-start.39) | collective-permute-done | bytes 262176 | tf_op jit(solution)/shard_map/ppermute | solution.py:34
  122.9 1.4 %collective-permute-start.41 = (bf16[512,256]{1,0:T(8,128)(2,1)S(1)}, bf16[512,256]{1,0:T(8,128)(2,1)S(1)}, u32[]{:S(2)}, u32[]{:S(2)}) collective-permute-start(bf16[512,256]{1,0:T(8,128)(2,1)S(1)} %collective-permute-done.39.e1), channel_id=1, source_target_pairs={{0,4},{1,3},{2,6},{3,1},{4,0},{5,7},{6,2},{7,5},{8,12},{9,11},{10,... | collective-permute-start | bytes 786440 | tf_op jit(solution)/shard_map/ppermute | solution.py:34
  124.4 1.3 backward.4
  125.8 1.3 backward.5
  127.7 1.3 backward.6
  129.1 2.4 %collective-permute-done.41.e3 = bf16[512,256]{1,0:T(8,128)(2,1)S(1)} collective-permute-done((bf16[512,256]{1,0:T(8,128)(2,1)S(1)}, bf16[512,256]{1,0:T(8,128)(2,1)S(1)}, u32[]{:S(2)}, u32[]{:S(2)}) %collective-permute-start.41) | collective-permute-done | bytes 262176 | tf_op jit(solution)/shard_map/ppermute | solution.py:34
  131.5 1.3 backward.7
  134.8 4.2 %encoder_gradient.1 = f32[4096,128]{1,0:T(8,128)} custom-call(s32[16]{0:T(128)S(1)} %pad_add_fusion.3.order, bf16[16,256,512]{2,1,0:T(8,128)(2,1)S(1)} %turn.1.rest_1_.mine, bf16[16,256,512]{2,1,0:T(8,128)(2,1)S(1)} %collective-permute-done.29.earlier.theirs, bf16[512,128]{1,0:T(8,128)(2,1)S(1)} %get-tuple-element.60.dpre, ...), custom_call_target="tpu_custom_call" | custom-call | flops 1073741824 | bytes 10485760 | tf_op jit(solution)/shard_map/encoder_gradient/pallas_call | solution.py:126
  139.0 2.1 %decoder_gradient.1 = (f32[128,4096]{1,0:T(8,128)}, f32[1,1]{1,0:T(1,128)}) custom-call(s32[16]{0:T(128)S(1)} %pad_add_fusion.3.order, f32[128,1024]{1,0:T(8,128)S(1)} %get-tuple-element.42.refs_0_, f32[128,1024]{1,0:T(8,128)S(1)} %get-tuple-element.45.refs_1_, f32[128,1024]{1,0:T(8,128)S(1)} %get-tuple-element.48.refs_2_, ...), custom_call_target="tpu_custom_call" | custom-call | flops 524288 | bytes 5242880 | tf_op jit(solution)/shard_map/decoder_gradient/pallas_call | solution.py:126
  (96 shorter events, 29.8 us)
Async XLA Ops:
  2.3 16.1 %collective-permute-start = (bf16[512,256]{1,0:T(8,128)(2,1)S(1)}, bf16[512,256]{1,0:T(8,128)(2,1)S(1)}, u32[]{:S(2)}, u32[]{:S(2)}) collective-permute-start(bf16[512,256]{1,0:T(8,128)(2,1)S(1)} %fusion.refs_0_), channel_id=1, source_target_pairs={{0,16},{1,17},{2,18},{3,19},{4,20},{5,21},{6,22},{7,23},{8,24},{9,... | collective-permute-start | bytes 786440 | tf_op jit(solution)/shard_map/ppermute | solution.py:34
  6.4 14.2 %collective-permute-start.6 = (bf16[512,256]{1,0:T(8,128)(2,1)S(1)}, bf16[512,256]{1,0:T(8,128)(2,1)S(1)}, u32[]{:S(2)}, u32[]{:S(2)}) collective-permute-start(bf16[512,256]{1,0:T(8,128)(2,1)S(1)} %fusion.refs_0_), channel_id=1, source_target_pairs={{0,2},{1,5},{2,0},{3,7},{4,6},{5,1},{6,4},{7,3},{8,10},{9,13},{10,... | collective-permute-start | bytes 786440 | tf_op jit(solution)/shard_map/ppermute | solution.py:34
  7.9 14.2 %collective-permute-start.7 = (bf16[512,256]{1,0:T(8,128)(2,1)S(1)}, bf16[512,256]{1,0:T(8,128)(2,1)S(1)}, u32[]{:S(2)}, u32[]{:S(2)}) collective-permute-start(bf16[512,256]{1,0:T(8,128)(2,1)S(1)} %fusion.refs_0_), channel_id=1, source_target_pairs={{0,4},{1,3},{2,6},{3,1},{4,0},{5,7},{6,2},{7,5},{8,12},{9,11},{10,... | collective-permute-start | bytes 786440 | tf_op jit(solution)/shard_map/ppermute | solution.py:34
  9.4 14.2 %collective-permute-start.9 = (bf16[512,256]{1,0:T(8,128)(2,1)S(1)}, bf16[512,256]{1,0:T(8,128)(2,1)S(1)}, u32[]{:S(2)}, u32[]{:S(2)}) collective-permute-start(bf16[512,256]{1,0:T(8,128)(2,1)S(1)} %fusion.refs_0_), channel_id=1, source_target_pairs={{0,8},{1,9},{2,10},{3,11},{4,12},{5,13},{6,14},{7,15},{8,0},{9,1},... | collective-permute-start | bytes 786440 | tf_op jit(solution)/shard_map/ppermute | solution.py:34
  18.4 8.6 %collective-permute-start.2 = (bf16[512,256]{1,0:T(8,128)(2,1)S(1)}, bf16[512,256]{1,0:T(8,128)(2,1)S(1)}, u32[]{:S(2)}, u32[]{:S(2)}) collective-permute-start(bf16[512,256]{1,0:T(8,128)(2,1)S(1)} %collective-permute-done.refs_8_), channel_id=1, source_target_pairs={{0,2},{1,5},{2,0},{3,7},{4,6},{5,1},{6,4},{7,3},{8,10},{9,13},{10,... | collective-permute-start | bytes 786440 | tf_op jit(solution)/shard_map/ppermute | solution.py:34
  20.0 9.2 %collective-permute-start.1 = (bf16[512,256]{1,0:T(8,128)(2,1)S(1)}, bf16[512,256]{1,0:T(8,128)(2,1)S(1)}, u32[]{:S(2)}, u32[]{:S(2)}) collective-permute-start(bf16[512,256]{1,0:T(8,128)(2,1)S(1)} %collective-permute-done.refs_8_), channel_id=1, source_target_pairs={{0,8},{1,9},{2,10},{3,11},{4,12},{5,13},{6,14},{7,15},{8,0},{9,1},... | collective-permute-start | bytes 786440 | tf_op jit(solution)/shard_map/ppermute | solution.py:34
  20.6 10.2 %collective-permute-start.8 = (bf16[512,256]{1,0:T(8,128)(2,1)S(1)}, bf16[512,256]{1,0:T(8,128)(2,1)S(1)}, u32[]{:S(2)}, u32[]{:S(2)}) collective-permute-start(bf16[512,256]{1,0:T(8,128)(2,1)S(1)} %collective-permute-done.6.refs_1_), channel_id=1, source_target_pairs={{0,4},{1,3},{2,6},{3,1},{4,0},{5,7},{6,2},{7,5},{8,12},{9,11},{10,... | collective-permute-start | bytes 786440 | tf_op jit(solution)/shard_map/ppermute | solution.py:34
  22.1 12.8 %collective-permute-start.10 = (bf16[512,256]{1,0:T(8,128)(2,1)S(1)}, bf16[512,256]{1,0:T(8,128)(2,1)S(1)}, u32[]{:S(2)}, u32[]{:S(2)}) collective-permute-start(bf16[512,256]{1,0:T(8,128)(2,1)S(1)} %collective-permute-done.6.refs_1_), channel_id=1, source_target_pairs={{0,8},{1,9},{2,10},{3,11},{4,12},{5,13},{6,14},{7,15},{8,0},{9,1},... | collective-permute-start | bytes 786440 | tf_op jit(solution)/shard_map/ppermute | solution.py:34
  23.6 14.8 %collective-permute-start.11 = (bf16[512,256]{1,0:T(8,128)(2,1)S(1)}, bf16[512,256]{1,0:T(8,128)(2,1)S(1)}, u32[]{:S(2)}, u32[]{:S(2)}) collective-permute-start(bf16[512,256]{1,0:T(8,128)(2,1)S(1)} %collective-permute-done.9.refs_4_), channel_id=1, source_target_pairs={{0,4},{1,3},{2,6},{3,1},{4,0},{5,7},{6,2},{7,5},{8,12},{9,11},{10,... | collective-permute-start | bytes 786440 | tf_op jit(solution)/shard_map/ppermute | solution.py:34
  27.0 12.3 %collective-permute-start.3 = (bf16[512,256]{1,0:T(8,128)(2,1)S(1)}, bf16[512,256]{1,0:T(8,128)(2,1)S(1)}, u32[]{:S(2)}, u32[]{:S(2)}) collective-permute-start(bf16[512,256]{1,0:T(8,128)(2,1)S(1)} %collective-permute-done.2.refs_9_), channel_id=1, source_target_pairs={{0,8},{1,9},{2,10},{3,11},{4,12},{5,13},{6,14},{7,15},{8,0},{9,1},... | collective-permute-start | bytes 786440 | tf_op jit(solution)/shard_map/ppermute | solution.py:34
  29.2 11.4 %collective-permute-start.13 = (bf16[512,256]{1,0:T(8,128)(2,1)S(1)}, bf16[512,256]{1,0:T(8,128)(2,1)S(1)}, u32[]{:S(2)}, u32[]{:S(2)}) collective-permute-start(bf16[512,256]{1,0:T(8,128)(2,1)S(1)} %collective-permute-done.refs_8_), channel_id=1, source_target_pairs={{0,4},{1,3},{2,6},{3,1},{4,0},{5,7},{6,2},{7,5},{8,12},{9,11},{10,... | collective-permute-start | bytes 786440 | tf_op jit(solution)/shard_map/ppermute | solution.py:34
  30.7 10.5 %collective-permute-start.14 = (bf16[512,256]{1,0:T(8,128)(2,1)S(1)}, bf16[512,256]{1,0:T(8,128)(2,1)S(1)}, u32[]{:S(2)}, u32[]{:S(2)}) collective-permute-start(bf16[512,256]{1,0:T(8,128)(2,1)S(1)} %collective-permute-done.2.refs_9_), channel_id=1, source_target_pairs={{0,4},{1,3},{2,6},{3,1},{4,0},{5,7},{6,2},{7,5},{8,12},{9,11},{10,... | collective-permute-start | bytes 786440 | tf_op jit(solution)/shard_map/ppermute | solution.py:34
  34.8 6.4 %collective-permute-start.12 = (bf16[512,256]{1,0:T(8,128)(2,1)S(1)}, bf16[512,256]{1,0:T(8,128)(2,1)S(1)}, u32[]{:S(2)}, u32[]{:S(2)}) collective-permute-start(bf16[512,256]{1,0:T(8,128)(2,1)S(1)} %collective-permute-done.10.refs_5_), channel_id=1, source_target_pairs={{0,4},{1,3},{2,6},{3,1},{4,0},{5,7},{6,2},{7,5},{8,12},{9,11},{10,... | collective-permute-start | bytes 786440 | tf_op jit(solution)/shard_map/ppermute | solution.py:34
  38.4 7.6 %collective-permute-start.4 = (bf16[512,256]{1,0:T(8,128)(2,1)S(1)}, bf16[512,256]{1,0:T(8,128)(2,1)S(1)}, u32[]{:S(2)}, u32[]{:S(2)}) collective-permute-start(bf16[512,256]{1,0:T(8,128)(2,1)S(1)} %collective-permute-done.1.refs_0_.refs_12_), channel_id=1, source_target_pairs={{0,4},{1,3},{2,6},{3,1},{4,0},{5,7},{6,2},{7,5},{8,12},{9,11},{10,... | collective-permute-start | bytes 786440 | tf_op jit(solution)/shard_map/ppermute | solution.py:34
  39.3 8.3 %collective-permute-start.5 = (bf16[512,256]{1,0:T(8,128)(2,1)S(1)}, bf16[512,256]{1,0:T(8,128)(2,1)S(1)}, u32[]{:S(2)}, u32[]{:S(2)}) collective-permute-start(bf16[512,256]{1,0:T(8,128)(2,1)S(1)} %collective-permute-done.3.refs_1_.refs_13_), channel_id=1, source_target_pairs={{0,4},{1,3},{2,6},{3,1},{4,0},{5,7},{6,2},{7,5},{8,12},{9,11},{10,... | collective-permute-start | bytes 786440 | tf_op jit(solution)/shard_map/ppermute | solution.py:34
  50.6 9.2 %collective-permute-start.15 = (bf16[2,512,256]{2,1,0:T(8,128)(2,1)S(1)}, bf16[2,512,256]{2,1,0:T(8,128)(2,1)S(1)}, u32[]{:S(2)}, u32[]{:S(2)}) collective-permute-start(bf16[2,512,256]{2,1,0:T(8,128)(2,1)S(1)} %get-tuple-element.35), channel_id=1, source_target_pairs={{0,4},{1,3},{2,6},{3,1},{4,0},{5,7},{6,2},{7,5},{8,12},{9,11},{10,... | collective-permute-start | bytes 1572872 | tf_op jit(solution)/shard_map/ppermute | solution.py:34
  55.2 67.7 %collective-permute-start.29 = (bf16[16,256,512]{2,1,0:T(8,128)(2,1)S(1)}, bf16[16,256,512]{2,1,0:T(8,128)(2,1)S(1)}, u32[]{:S(2)}, u32[]{:S(2)}) collective-permute-start(bf16[16,256,512]{2,1,0:T(8,128)(2,1)S(1)} %turn.1.rest_1_.mine), channel_id=1, source_target_pairs={{0,1},{1,0},{2,3},{3,2},{4,5},{5,4},{6,7},{7,6},{8,9},{9,8},{10,11... | collective-permute-start | bytes 12582920 | tf_op jit(solution)/shard_map/ppermute | solution.py:50
  56.3 9.2 %collective-permute-start.19 = (bf16[2,512,256]{2,1,0:T(8,128)(2,1)S(1)}, bf16[2,512,256]{2,1,0:T(8,128)(2,1)S(1)}, u32[]{:S(2)}, u32[]{:S(2)}) collective-permute-start(bf16[2,512,256]{2,1,0:T(8,128)(2,1)S(1)} %get-tuple-element.39), channel_id=1, source_target_pairs={{0,4},{1,3},{2,6},{3,1},{4,0},{5,7},{6,2},{7,5},{8,12},{9,11},{10,... | collective-permute-start | bytes 1572872 | tf_op jit(solution)/shard_map/ppermute | solution.py:34
  60.9 13.4 %collective-permute-start.23 = (bf16[2,512,256]{2,1,0:T(8,128)(2,1)S(1)}, bf16[2,512,256]{2,1,0:T(8,128)(2,1)S(1)}, u32[]{:S(2)}, u32[]{:S(2)}) collective-permute-start(bf16[2,512,256]{2,1,0:T(8,128)(2,1)S(1)} %get-tuple-element.41), channel_id=1, source_target_pairs={{0,4},{1,3},{2,6},{3,1},{4,0},{5,7},{6,2},{7,5},{8,12},{9,11},{10,... | collective-permute-start | bytes 1572872 | tf_op jit(solution)/shard_map/ppermute | solution.py:34
  62.0 8.7 %collective-permute-start.16 = (bf16[512,256]{1,0:T(8,128)(2,1)S(1)}, bf16[512,256]{1,0:T(8,128)(2,1)S(1)}, u32[]{:S(2)}, u32[]{:S(2)}) collective-permute-start(bf16[512,256]{1,0:T(8,128)(2,1)S(1)} %get-tuple-element.67), channel_id=1, source_target_pairs={{0,8},{1,9},{2,10},{3,11},{4,12},{5,13},{6,14},{7,15},{8,0},{9,1},... | collective-permute-start | bytes 786440 | tf_op jit(solution)/shard_map/ppermute | solution.py:34
  62.6 13.0 %collective-permute-start.20 = (bf16[512,256]{1,0:T(8,128)(2,1)S(1)}, bf16[512,256]{1,0:T(8,128)(2,1)S(1)}, u32[]{:S(2)}, u32[]{:S(2)}) collective-permute-start(bf16[512,256]{1,0:T(8,128)(2,1)S(1)} %get-tuple-element.66), channel_id=1, source_target_pairs={{0,8},{1,9},{2,10},{3,11},{4,12},{5,13},{6,14},{7,15},{8,0},{9,1},... | collective-permute-start | bytes 786440 | tf_op jit(solution)/shard_map/ppermute | solution.py:34
  70.8 8.4 %collective-permute-start.21 = (bf16[512,256]{1,0:T(8,128)(2,1)S(1)}, bf16[512,256]{1,0:T(8,128)(2,1)S(1)}, u32[]{:S(2)}, u32[]{:S(2)}) collective-permute-start(bf16[512,256]{1,0:T(8,128)(2,1)S(1)} %fusion.4), channel_id=1, source_target_pairs={{0,2},{1,5},{2,0},{3,7},{4,6},{5,1},{6,4},{7,3},{8,10},{9,13},{10,... | collective-permute-start | bytes 786440 | tf_op jit(solution)/shard_map/ppermute | solution.py:34
  72.3 11.4 %collective-permute-start.17 = (bf16[2,512,256]{2,1,0:T(8,128)(2,1)S(1)}, bf16[2,512,256]{2,1,0:T(8,128)(2,1)S(1)}, u32[]{:S(2)}, u32[]{:S(2)}) collective-permute-start(bf16[2,512,256]{2,1,0:T(8,128)(2,1)S(1)} %get-tuple-element.37), channel_id=1, source_target_pairs={{0,4},{1,3},{2,6},{3,1},{4,0},{5,7},{6,2},{7,5},{8,12},{9,11},{10,... | collective-permute-start | bytes 1572872 | tf_op jit(solution)/shard_map/ppermute | solution.py:34
  74.4 7.5 %collective-permute-start.24 = (bf16[512,256]{1,0:T(8,128)(2,1)S(1)}, bf16[512,256]{1,0:T(8,128)(2,1)S(1)}, u32[]{:S(2)}, u32[]{:S(2)}) collective-permute-start(bf16[512,256]{1,0:T(8,128)(2,1)S(1)} %fusion.13), channel_id=1, source_target_pairs={{0,2},{1,5},{2,0},{3,7},{4,6},{5,1},{6,4},{7,3},{8,10},{9,13},{10,... | collective-permute-start | bytes 786440 | tf_op jit(solution)/shard_map/ppermute | solution.py:34
  79.3 10.3 %collective-permute-start.22 = (bf16[512,256]{1,0:T(8,128)(2,1)S(1)}, bf16[512,256]{1,0:T(8,128)(2,1)S(1)}, u32[]{:S(2)}, u32[]{:S(2)}) collective-permute-start(bf16[512,256]{1,0:T(8,128)(2,1)S(1)} %fusion.7), channel_id=1, source_target_pairs={{0,16},{1,17},{2,18},{3,19},{4,20},{5,21},{6,22},{7,23},{8,24},{9,... | collective-permute-start | bytes 786440 | tf_op jit(solution)/shard_map/ppermute | solution.py:34
  82.0 8.8 %collective-permute-start.25 = (bf16[512,256]{1,0:T(8,128)(2,1)S(1)}, bf16[512,256]{1,0:T(8,128)(2,1)S(1)}, u32[]{:S(2)}, u32[]{:S(2)}) collective-permute-start(bf16[512,256]{1,0:T(8,128)(2,1)S(1)} %fusion.2), channel_id=1, source_target_pairs={{0,8},{1,9},{2,10},{3,11},{4,12},{5,13},{6,14},{7,15},{8,0},{9,1},... | collective-permute-start | bytes 786440 | tf_op jit(solution)/shard_map/ppermute | solution.py:34
  83.8 7.0 %collective-permute-start.18 = (bf16[512,256]{1,0:T(8,128)(2,1)S(1)}, bf16[512,256]{1,0:T(8,128)(2,1)S(1)}, u32[]{:S(2)}, u32[]{:S(2)}) collective-permute-start(bf16[512,256]{1,0:T(8,128)(2,1)S(1)} %fusion.12), channel_id=1, source_target_pairs={{0,2},{1,5},{2,0},{3,7},{4,6},{5,1},{6,4},{7,3},{8,10},{9,13},{10,... | collective-permute-start | bytes 786440 | tf_op jit(solution)/shard_map/ppermute | solution.py:34
  91.9 8.0 %collective-permute-start.26 = (bf16[512,256]{1,0:T(8,128)(2,1)S(1)}, bf16[512,256]{1,0:T(8,128)(2,1)S(1)}, u32[]{:S(2)}, u32[]{:S(2)}) collective-permute-start(bf16[512,256]{1,0:T(8,128)(2,1)S(1)} %get-tuple-element.62.e0), channel_id=1, source_target_pairs={{0,2},{1,5},{2,0},{3,7},{4,6},{5,1},{6,4},{7,3},{8,10},{9,13},{10,... | collective-permute-start | bytes 786440 | tf_op jit(solution)/shard_map/ppermute | solution.py:34
  92.5 11.2 %collective-permute-start.34 = (bf16[512,256]{1,0:T(8,128)(2,1)S(1)}, bf16[512,256]{1,0:T(8,128)(2,1)S(1)}, u32[]{:S(2)}, u32[]{:S(2)}) collective-permute-start(bf16[512,256]{1,0:T(8,128)(2,1)S(1)} %get-tuple-element.62.e0), channel_id=1, source_target_pairs={{0,16},{1,17},{2,18},{3,19},{4,20},{5,21},{6,22},{7,23},{8,24},{9,... | collective-permute-start | bytes 786440 | tf_op jit(solution)/shard_map/ppermute | solution.py:34
  95.0 9.1 %collective-permute-start.27 = (bf16[512,256]{1,0:T(8,128)(2,1)S(1)}, bf16[512,256]{1,0:T(8,128)(2,1)S(1)}, u32[]{:S(2)}, u32[]{:S(2)}) collective-permute-start(bf16[512,256]{1,0:T(8,128)(2,1)S(1)} %get-tuple-element.62.e0), channel_id=1, source_target_pairs={{0,4},{1,3},{2,6},{3,1},{4,0},{5,7},{6,2},{7,5},{8,12},{9,11},{10,... | collective-permute-start | bytes 786440 | tf_op jit(solution)/shard_map/ppermute | solution.py:34
  96.2 10.4 %collective-permute-start.30 = (bf16[512,256]{1,0:T(8,128)(2,1)S(1)}, bf16[512,256]{1,0:T(8,128)(2,1)S(1)}, u32[]{:S(2)}, u32[]{:S(2)}) collective-permute-start(bf16[512,256]{1,0:T(8,128)(2,1)S(1)} %get-tuple-element.62.e0), channel_id=1, source_target_pairs={{0,8},{1,9},{2,10},{3,11},{4,12},{5,13},{6,14},{7,15},{8,0},{9,1},... | collective-permute-start | bytes 786440 | tf_op jit(solution)/shard_map/ppermute | solution.py:34
  99.9 8.3 %collective-permute-start.28 = (bf16[512,256]{1,0:T(8,128)(2,1)S(1)}, bf16[512,256]{1,0:T(8,128)(2,1)S(1)}, u32[]{:S(2)}, u32[]{:S(2)}) collective-permute-start(bf16[512,256]{1,0:T(8,128)(2,1)S(1)} %collective-permute-done.26.e1), channel_id=1, source_target_pairs={{0,4},{1,3},{2,6},{3,1},{4,0},{5,7},{6,2},{7,5},{8,12},{9,11},{10,... | collective-permute-start | bytes 786440 | tf_op jit(solution)/shard_map/ppermute | solution.py:34
  103.6 6.4 %collective-permute-start.35 = (bf16[512,256]{1,0:T(8,128)(2,1)S(1)}, bf16[512,256]{1,0:T(8,128)(2,1)S(1)}, u32[]{:S(2)}, u32[]{:S(2)}) collective-permute-start(bf16[512,256]{1,0:T(8,128)(2,1)S(1)} %collective-permute-done.34.e0), channel_id=1, source_target_pairs={{0,2},{1,5},{2,0},{3,7},{4,6},{5,1},{6,4},{7,3},{8,10},{9,13},{10,... | collective-permute-start | bytes 786440 | tf_op jit(solution)/shard_map/ppermute | solution.py:34
  104.1 9.2 %collective-permute-start.31 = (bf16[512,256]{1,0:T(8,128)(2,1)S(1)}, bf16[512,256]{1,0:T(8,128)(2,1)S(1)}, u32[]{:S(2)}, u32[]{:S(2)}) collective-permute-start(bf16[512,256]{1,0:T(8,128)(2,1)S(1)} %collective-permute-done.26.e1), channel_id=1, source_target_pairs={{0,8},{1,9},{2,10},{3,11},{4,12},{5,13},{6,14},{7,15},{8,0},{9,1},... | collective-permute-start | bytes 786440 | tf_op jit(solution)/shard_map/ppermute | solution.py:34
  106.5 7.3 %collective-permute-start.32 = (bf16[512,256]{1,0:T(8,128)(2,1)S(1)}, bf16[512,256]{1,0:T(8,128)(2,1)S(1)}, u32[]{:S(2)}, u32[]{:S(2)}) collective-permute-start(bf16[512,256]{1,0:T(8,128)(2,1)S(1)} %collective-permute-done.30.e0), channel_id=1, source_target_pairs={{0,4},{1,3},{2,6},{3,1},{4,0},{5,7},{6,2},{7,5},{8,12},{9,11},{10,... | collective-permute-start | bytes 786440 | tf_op jit(solution)/shard_map/ppermute | solution.py:34
  108.2 10.7 %collective-permute-start.38 = (bf16[512,256]{1,0:T(8,128)(2,1)S(1)}, bf16[512,256]{1,0:T(8,128)(2,1)S(1)}, u32[]{:S(2)}, u32[]{:S(2)}) collective-permute-start(bf16[512,256]{1,0:T(8,128)(2,1)S(1)} %collective-permute-done.34.e0), channel_id=1, source_target_pairs={{0,8},{1,9},{2,10},{3,11},{4,12},{5,13},{6,14},{7,15},{8,0},{9,1},... | collective-permute-start | bytes 786440 | tf_op jit(solution)/shard_map/ppermute | solution.py:34
  110.0 12.3 %collective-permute-start.39 = (bf16[512,256]{1,0:T(8,128)(2,1)S(1)}, bf16[512,256]{1,0:T(8,128)(2,1)S(1)}, u32[]{:S(2)}, u32[]{:S(2)}) collective-permute-start(bf16[512,256]{1,0:T(8,128)(2,1)S(1)} %collective-permute-done.35.e1), channel_id=1, source_target_pairs={{0,8},{1,9},{2,10},{3,11},{4,12},{5,13},{6,14},{7,15},{8,0},{9,1},... | collective-permute-start | bytes 786440 | tf_op jit(solution)/shard_map/ppermute | solution.py:34
  113.3 12.4 %collective-permute-start.33 = (bf16[512,256]{1,0:T(8,128)(2,1)S(1)}, bf16[512,256]{1,0:T(8,128)(2,1)S(1)}, u32[]{:S(2)}, u32[]{:S(2)}) collective-permute-start(bf16[512,256]{1,0:T(8,128)(2,1)S(1)} %collective-permute-done.31.e1), channel_id=1, source_target_pairs={{0,4},{1,3},{2,6},{3,1},{4,0},{5,7},{6,2},{7,5},{8,12},{9,11},{10,... | collective-permute-start | bytes 786440 | tf_op jit(solution)/shard_map/ppermute | solution.py:34
  113.8 13.3 %collective-permute-start.36 = (bf16[512,256]{1,0:T(8,128)(2,1)S(1)}, bf16[512,256]{1,0:T(8,128)(2,1)S(1)}, u32[]{:S(2)}, u32[]{:S(2)}) collective-permute-start(bf16[512,256]{1,0:T(8,128)(2,1)S(1)} %collective-permute-done.34.e0), channel_id=1, source_target_pairs={{0,4},{1,3},{2,6},{3,1},{4,0},{5,7},{6,2},{7,5},{8,12},{9,11},{10,... | collective-permute-start | bytes 786440 | tf_op jit(solution)/shard_map/ppermute | solution.py:34
  118.9 8.7 %collective-permute-start.37 = (bf16[512,256]{1,0:T(8,128)(2,1)S(1)}, bf16[512,256]{1,0:T(8,128)(2,1)S(1)}, u32[]{:S(2)}, u32[]{:S(2)}) collective-permute-start(bf16[512,256]{1,0:T(8,128)(2,1)S(1)} %collective-permute-done.35.e1), channel_id=1, source_target_pairs={{0,4},{1,3},{2,6},{3,1},{4,0},{5,7},{6,2},{7,5},{8,12},{9,11},{10,... | collective-permute-start | bytes 786440 | tf_op jit(solution)/shard_map/ppermute | solution.py:34
  122.3 6.8 %collective-permute-start.40 = (bf16[512,256]{1,0:T(8,128)(2,1)S(1)}, bf16[512,256]{1,0:T(8,128)(2,1)S(1)}, u32[]{:S(2)}, u32[]{:S(2)}) collective-permute-start(bf16[512,256]{1,0:T(8,128)(2,1)S(1)} %collective-permute-done.38.e0), channel_id=1, source_target_pairs={{0,4},{1,3},{2,6},{3,1},{4,0},{5,7},{6,2},{7,5},{8,12},{9,11},{10,... | collective-permute-start | bytes 786440 | tf_op jit(solution)/shard_map/ppermute | solution.py:34
  122.9 8.6 %collective-permute-start.41 = (bf16[512,256]{1,0:T(8,128)(2,1)S(1)}, bf16[512,256]{1,0:T(8,128)(2,1)S(1)}, u32[]{:S(2)}, u32[]{:S(2)}) collective-permute-start(bf16[512,256]{1,0:T(8,128)(2,1)S(1)} %collective-permute-done.39.e1), channel_id=1, source_target_pairs={{0,4},{1,3},{2,6},{3,1},{4,0},{5,7},{6,2},{7,5},{8,12},{9,11},{10,... | collective-permute-start | bytes 786440 | tf_op jit(solution)/shard_map/ppermute | solution.py:34
  125.7 13.3 %collective-permute-start.42 = (bf16[128,1024]{1,0:T(8,128)(2,1)S(1)}, bf16[128,1024]{1,0:T(8,128)(2,1)S(1)}, u32[]{:S(2)}, u32[]{:S(2)}) collective-permute-start(bf16[128,1024]{1,0:T(8,128)(2,1)S(1)} %get-tuple-element.53), channel_id=1, source_target_pairs={{0,1},{1,0},{2,3},{3,2},{4,5},{5,4},{6,7},{7,6},{8,9},{9,8},{10,11... | collective-permute-start | bytes 786440 | tf_op jit(solution)/shard_map/ppermute | solution.py:50
  127.1 11.9 %collective-permute-start.43 = (bf16[128,1024]{1,0:T(8,128)(2,1)S(1)}, bf16[128,1024]{1,0:T(8,128)(2,1)S(1)}, u32[]{:S(2)}, u32[]{:S(2)}) collective-permute-start(bf16[128,1024]{1,0:T(8,128)(2,1)S(1)} %get-tuple-element.54), channel_id=1, source_target_pairs={{0,1},{1,0},{2,3},{3,2},{4,5},{5,4},{6,7},{7,6},{8,9},{9,8},{10,11... | collective-permute-start | bytes 786440 | tf_op jit(solution)/shard_map/ppermute | solution.py:50
  129.0 10.0 %collective-permute-start.44 = (bf16[128,1024]{1,0:T(8,128)(2,1)S(1)}, bf16[128,1024]{1,0:T(8,128)(2,1)S(1)}, u32[]{:S(2)}, u32[]{:S(2)}) collective-permute-start(bf16[128,1024]{1,0:T(8,128)(2,1)S(1)} %get-tuple-element.55), channel_id=1, source_target_pairs={{0,1},{1,0},{2,3},{3,2},{4,5},{5,4},{6,7},{7,6},{8,9},{9,8},{10,11... | collective-permute-start | bytes 786440 | tf_op jit(solution)/shard_map/ppermute | solution.py:50
  132.9 6.1 %collective-permute-start.45 = (bf16[128,1024]{1,0:T(8,128)(2,1)S(1)}, bf16[128,1024]{1,0:T(8,128)(2,1)S(1)}, u32[]{:S(2)}, u32[]{:S(2)}) collective-permute-start(bf16[128,1024]{1,0:T(8,128)(2,1)S(1)} %get-tuple-element.56), channel_id=1, source_target_pairs={{0,1},{1,0},{2,3},{3,2},{4,5},{5,4},{6,7},{7,6},{8,9},{9,8},{10,11... | collective-permute-start | bytes 786440 | tf_op jit(solution)/shard_map/ppermute | solution.py:50
  132.9 1.7 %collective-permute-start.47 = (bf16[512,128]{1,0:T(8,128)(2,1)S(1)}, bf16[512,128]{1,0:T(8,128)(2,1)S(1)}, u32[]{:S(2)}, u32[]{:S(2)}) collective-permute-start(bf16[512,128]{1,0:T(8,128)(2,1)S(1)} %get-tuple-element.61), channel_id=1, source_target_pairs={{0,1},{1,0},{2,3},{3,2},{4,5},{5,4},{6,7},{7,6},{8,9},{9,8},{10,11... | collective-permute-start | bytes 393224 | tf_op jit(solution)/shard_map/ppermute | solution.py:50
  134.6 4.3 %collective-permute-start.46 = (f32[8,128]{1,0:T(8,128)S(1)}, f32[8,128]{1,0:T(8,128)S(1)}, u32[]{:S(2)}, u32[]{:S(2)}) collective-permute-start(f32[8,128]{1,0:T(8,128)S(1)} %get-tuple-element.57.refs_8_), channel_id=1, source_target_pairs={{0,1},{1,0},{2,3},{3,2},{4,5},{5,4},{6,7},{7,6},{8,9},{9,8},{10,11... | collective-permute-start | bytes 12296 | tf_op jit(solution)/shard_map/ppermute | solution.py:442
  (6 other events, 38.2 us)
